TPU v7x, 32 devices: a whole 2x2x4 slice. The times are simulated.
32 devices in a mesh: req: 4 (over y, x), vocab: 8 (over z, core).
Axes of the slice: x: 2, y: 2, z: 4, core: 2. Of those that a mesh axis runs over, the one named last changes fastest.
Arguments:
- hidden: bfloat16 [8192, 4096], P('req', 'vocab'), may hold values from -320 to 320
- gain: float32 [4096], replicated, may hold values from 0.5 to 1.5
- head: bfloat16 [4096, 32768], P(None, ('req', 'vocab'))
- targets: int32 [8192], P('req'), may hold values from 0 to 32767
- lengths: int32 [4, 4], P('req'), may hold values from 1 to 1280, 2048 in all within a row
Outputs:
- token_logprob: float32 [8192], P(('req', 'vocab'))
- token_entropy: float32 [8192], P(('req', 'vocab'))
- seq_logprob: float32 [12], P('req')
- seq_entropy: float32 [12], P('req')
Inputs may be any that keep to these rules, and one draw needn't show every extreme that they name: lengths[q, 3] counts the empty slots at the end of index q's rows.
All inputs are finite; a program needn't handle non-finite values.
Results may differ from a plain program's by a relative error of at most 0.0012.
Values may be sent and summed in bfloat16 or wider, within the bound.
No kernel may reach another device: no remote copies, remote signals or barrier semaphores. Data moves between devices by JAX's collectives and lax.ppermute only.
A program may use at most 128 MiB of HBM per device.

v0:
```python
import jax
import jax.numpy as jnp
from jax import lax
from jax.sharding import PartitionSpec as P

D = 4096
SEQ_DEV = 3


EPS = 1e-05


def finish_rows(peak, total, moment, picked):
    log_total = peak + jnp.log(total)
    return (picked - log_total, log_total - moment / total)


def shards(hidden, gain, head, targets, lengths):
    rows = hidden.shape[0]
    vocab_index = lax.axis_index("vocab")
    vocab_count = lax.axis_size("vocab")
    shard_cols = head.shape[1]
    width_cols = shard_cols * lax.axis_size("req")
    col_pos = jnp.arange(width_cols, dtype=jnp.int32)
    col_ids = (
        col_pos // shard_cols * (vocab_count * shard_cols)
        + vocab_index * shard_cols
        + col_pos % shard_cols
    )
    block = min(512, rows)
    count = rows // block
    seq_lens = lengths[0, :SEQ_DEV]
    ends = jnp.cumsum(seq_lens)
    starts = ends - seq_lens
    live = ends[-1]
    full_rows = lax.all_gather(hidden, "vocab", axis=1, tiled=True)
    values = full_rows.astype(jnp.float32)
    mean_sq = jnp.sum(values * values, axis=1) / D
    normed = (values * lax.rsqrt(mean_sq + EPS)[:, None] * gain[None, :]).astype(jnp.bfloat16)
    columns = lax.all_gather(head, "req", axis=1, tiled=True)

    def block_logits(start):
        rows_blk = lax.dynamic_slice_in_dim(normed, start, block, 0)
        return jnp.dot(rows_blk, columns, preferred_element_type=jnp.float32)

    def compute_block(start):
        logits = block_logits(start)
        wanted = lax.dynamic_slice_in_dim(targets, start, block, 0)
        peak = jnp.max(logits, axis=1)
        weights = jnp.exp(logits - peak[:, None])
        total = jnp.sum(weights, axis=1)
        moment = jnp.sum(weights * logits, axis=1)
        picked = jnp.sum(jnp.where(col_ids[None, :] == wanted[:, None], logits, 0.0), axis=1)
        return (peak, total, moment, picked)

    def one_block(block_index):
        start = block_index * block
        return compute_block(start)

    peak, total, moment, picked = lax.map(one_block, jnp.arange(count, dtype=jnp.int32))
    peak = peak.reshape(rows)
    total = total.reshape(rows)
    moment = moment.reshape(rows)
    picked = picked.reshape(rows)
    share = rows // vocab_count
    divisor = seq_lens.astype(jnp.float32)
    peak, total, moment, picked = (
        lax.all_to_all(peak, "vocab", split_axis=0, concat_axis=0, tiled=True),
        lax.all_to_all(total, "vocab", split_axis=0, concat_axis=0, tiled=True),
        lax.all_to_all(moment, "vocab", split_axis=0, concat_axis=0, tiled=True),
        lax.all_to_all(picked, "vocab", split_axis=0, concat_axis=0, tiled=True),
    )
    peak = peak.reshape(vocab_count, share)
    total = total.reshape(vocab_count, share)
    moment = moment.reshape(vocab_count, share)
    picked = picked.reshape(vocab_count, share)
    best = jnp.max(peak, axis=0)
    factor = jnp.exp(peak - best[None, :])
    own_lp, own_ent = finish_rows(
        best,
        jnp.sum(total * factor, axis=0),
        jnp.sum(moment * factor, axis=0),
        jnp.sum(picked, axis=0),
    )
    local = vocab_index * share + jnp.arange(share, dtype=jnp.int32)
    valid = local < live
    own_lp = jnp.where(valid, own_lp, 0.0)
    own_ent = jnp.where(valid, own_ent, 0.0)
    member = ((local[None, :] >= starts[:, None]) & (local[None, :] < ends[:, None])).astype(
        jnp.float32
    )
    part_lp = jnp.sum(member * own_lp[None, :], axis=1)
    part_ent = jnp.sum(member * own_ent[None, :], axis=1)
    sum_lp, sum_ent = lax.psum((part_lp, part_ent), "vocab")
    seq_lp = sum_lp / divisor
    seq_ent = sum_ent / divisor
    return (own_lp, own_ent, seq_lp, seq_ent)


def solution(mesh):
    in_specs = (P("req", "vocab"), P(), P(None, ("req", "vocab")), P("req"), P("req", None))
    out_specs = (P(("req", "vocab")), P(("req", "vocab")), P("req"), P("req"))
    return jax.shard_map(shards, mesh=mesh, in_specs=in_specs, out_specs=out_specs, check_vma=False)
```

profile of v0, /device:TPU:0, one launch (start us, length us, event | category | flops | bytes accessed | tf_op | source)
XLA Modules:
  0.0 633.0 jit_solution(2667164119245899134)
XLA Ops:
  8.7 154.8 %all-gather.3.cloned.1.call-done = bf16[2048,4096]{1,0:T(8,128)(2,1)} async-done(((bf16[2048,512]{1,0:T(8,128)(2,1)}), bf16[2048,4096]{1,0:T(8,128)(2,1)}) %all-gather.3.cloned.1.call-update) | async-done | bytes 16777232 | tf_op jit(solution)/shard_map/all_gather | solution.py:36
  163.5 7.8 %fusion.16 = f32[2048]{0:T(1024)S(1)} fusion(bf16[2048,4096]{1,0:T(8,128)(2,1)} %all-gather.3.cloned.1.call-done), kind=kLoop, calls=%fused_computation.24 | loop fusion | flops 25163776 | bytes 16785408 | tf_op jit(solution)/shard_map/reduce_sum | solution.py:38
  171.2 7.4 %copy-done = bf16[2048,4096]{1,0:T(8,128)(2,1)S(1)} copy-done((bf16[2048,4096]{1,0:T(8,128)(2,1)S(1)}, bf16[2048,4096]{1,0:T(8,128)(2,1)}, u32[]{:S(2)}) %copy-start) | copy-done | bytes 16777240
  178.7 9.5 %fusion.18 = bf16[2048,4096]{1,0:T(8,128)(2,1)} fusion(bf16[2048,4096]{1,0:T(8,128)(2,1)S(1)} %copy-done, f32[4096]{0:T(1024)S(1)} %copy-done.1, f32[2048]{0:T(1024)S(1)} %add_rsqrt_fusion), kind=kLoop, calls=%fused_computation.26 | loop fusion | flops 33554432 | bytes 33579008 | tf_op jit(solution)/shard_map/convert_element_type | solution.py:39
  188.1 272.6 %all-gather.5.cloned.1.call-done = bf16[4096,4096]{1,0:T(8,128)(2,1)} async-done(((bf16[4096,1024]{1,0:T(8,128)(2,1)}), bf16[4096,4096]{1,0:T(8,128)(2,1)}) %all-gather.5.cloned.1.call-update) | async-done | bytes 33554448 | tf_op jit(solution)/shard_map/all_gather | solution.py:40
  460.8 112.7 %while.17 = (s32[]{:T(128)}, f32[4,512]{1,0:T(4,128)S(1)}, f32[4,512]{1,0:T(4,128)S(1)}, f32[4,512]{1,0:T(4,128)S(1)}, f32[4,512]{1,0:T(4,128)S(1)}, /*index=5*/...) while((s32[]{:T(128)}, f32[4,512]{1,0:T(4,128)S(1)}, ...), condition=%wide.region_7.8_spmd.clone, body=%wide.region_2.7_spmd.clone.sunk | while | flops 17196705792 | bytes 54591704 | solution.py:60
  462.0 22.9 %fusion.30 = (f32[512]{0:T(512)S(1)}, f32[512,4096]{1,0:T(8,128)S(1)}) fusion(bf16[4096,4096]{1,0:T(8,128)(2,1)} %get-tuple-element.227, bf16[2048,4096]{1,0:T(8,128)(2,1)} %get-tuple-element.226, s32[]{:T(128)S(6)} %select_n.67), kind=kOutput, calls=%fused_computation.47.clone.1 | convolution fusion | flops 17181966336 | bytes 46139396 | tf_op jit(solution)/shard_map/while/body/eval_jaxpr/dot_general | solution.py:44
  484.9 0.8 dynamic_slice.22
  485.7 3.0 multiply_reduce_fusion.2
  490.2 22.9 %fusion.30 = (f32[512]{0:T(512)S(1)}, f32[512,4096]{1,0:T(8,128)S(1)}) fusion(bf16[4096,4096]{1,0:T(8,128)(2,1)} %get-tuple-element.227, bf16[2048,4096]{1,0:T(8,128)(2,1)} %get-tuple-element.226, s32[]{:T(128)S(6)} %select_n.67), kind=kOutput, calls=%fused_computation.47.clone.1 | convolution fusion | flops 17181966336 | bytes 46139396 | tf_op jit(solution)/shard_map/while/body/eval_jaxpr/dot_general | solution.py:44
  513.9 3.0 multiply_reduce_fusion.2
  518.3 22.9 %fusion.30 = (f32[512]{0:T(512)S(1)}, f32[512,4096]{1,0:T(8,128)S(1)}) fusion(bf16[4096,4096]{1,0:T(8,128)(2,1)} %get-tuple-element.227, bf16[2048,4096]{1,0:T(8,128)(2,1)} %get-tuple-element.226, s32[]{:T(128)S(6)} %select_n.67), kind=kOutput, calls=%fused_computation.47.clone.1 | convolution fusion | flops 17181966336 | bytes 46139396 | tf_op jit(solution)/shard_map/while/body/eval_jaxpr/dot_general | solution.py:44
  542.0 3.0 multiply_reduce_fusion.2
  546.5 22.9 %fusion.30 = (f32[512]{0:T(512)S(1)}, f32[512,4096]{1,0:T(8,128)S(1)}) fusion(bf16[4096,4096]{1,0:T(8,128)(2,1)} %get-tuple-element.227, bf16[2048,4096]{1,0:T(8,128)(2,1)} %get-tuple-element.226, s32[]{:T(128)S(6)} %select_n.67), kind=kOutput, calls=%fused_computation.47.clone.1 | convolution fusion | flops 17181966336 | bytes 46139396 | tf_op jit(solution)/shard_map/while/body/eval_jaxpr/dot_general | solution.py:44
  570.2 3.0 multiply_reduce_fusion.2
  574.0 4.6 all-to-all-start.1
  579.3 5.0 all-to-all-done.1
  584.2 3.3 all-to-all-start.2
  588.4 4.7 all-to-all-done.2
  593.1 3.3 all-to-all-start
  597.1 4.9 all-to-all-done
  602.0 3.3 all-to-all-start.3
  606.0 4.9 all-to-all-done.3
  611.8 13.8 %all-reduce = (f32[3]{0:T(128)S(1)}, f32[3]{0:T(128)S(1)}) all-reduce(f32[3]{0:T(128)S(1)} %get-tuple-element.92, f32[3]{0:T(128)S(1)} %get-tuple-element.91), channel_id=1, replica_groups=mesh['req'=4,'vocab'=8] {'vocab'}, use_global_device_ids=true, to_apply=%region_13.14 | all-reduce | flops 6 | bytes 48 | tf_op jit(solution)/shard_map/psum | solution.py:94
  (61 shorter events, 11.6 us)
Async XLA Ops:
  7.2 164.1 %copy-start.1 = (f32[4096]{0:T(1024)S(1)}, f32[4096]{0:T(1024)}, u32[]{:S(2)}) copy-start(f32[4096]{0:T(1024)} %param.8) | copy-start | bytes 49156
  7.2 156.3 %all-gather.3.cloned.1.call-start = ((), (), s32[]{:S(2)}) async-start(), calls=%async_computation.4 | async-start | bytes 18874368 | tf_op jit(solution)/shard_map/all_gather | solution.py:36
  7.9 452.9 %all-gather.5.cloned.1.call-start = ((), (), s32[]{:S(2)}) async-start(), calls=%async_computation.5 | async-start | bytes 41943040 | tf_op jit(solution)/shard_map/all_gather | solution.py:40
  163.5 15.2 %copy-start = (bf16[2048,4096]{1,0:T(8,128)(2,1)S(1)}, bf16[2048,4096]{1,0:T(8,128)(2,1)}, u32[]{:S(2)}) copy-start(bf16[2048,4096]{1,0:T(8,128)(2,1)} %all-gather.3.cloned.1.call-done) | copy-start | bytes 50331652
  460.8 126.8 %copy-start.4 = (s32[1,4]{1,0:T(1,128)S(1)}, s32[1,4]{1,0:T(1,128)}, u32[]{:S(2)}) copy-start(s32[1,4]{1,0:T(1,128)} %param.11) | copy-start | bytes 52
  574.0 10.2 %all-to-all-start.1 = ((f32[8,256,1]{1,2,0:T(1,128)}), f32[8,256,1]{1,2,0:T(1,128)S(1)}, u32[]{:S(2)}, u32[]{:S(2)}) async-start(f32[8,256,1]{1,2,0:T(1,128)} %all_to_all.26), calls=%async_computation.1 | async-start | bytes 16384 | tf_op jit(solution)/shard_map/all_to_all | solution.py:68
  584.2 8.9 %all-to-all-start.2 = ((f32[8,256,1]{1,2,0:T(1,128)}), f32[8,256,1]{1,2,0:T(1,128)S(1)}, u32[]{:S(2)}, u32[]{:S(2)}) async-start(f32[8,256,1]{1,2,0:T(1,128)} %all_to_all.28), calls=%async_computation.2 | async-start | bytes 16384 | tf_op jit(solution)/shard_map/all_to_all | solution.py:69
  593.1 8.9 %all-to-all-start = ((f32[8,256,1]{1,2,0:T(1,128)}), f32[8,256,1]{1,2,0:T(1,128)S(1)}, u32[]{:S(2)}, u32[]{:S(2)}) async-start(f32[8,256,1]{1,2,0:T(1,128)} %all_to_all.24), calls=%async_computation | async-start | bytes 16384 | tf_op jit(solution)/shard_map/all_to_all | solution.py:71
  602.0 8.9 %all-to-all-start.3 = ((f32[8,256,1]{1,2,0:T(1,128)}), f32[8,256,1]{1,2,0:T(1,128)S(1)}, u32[]{:S(2)}, u32[]{:S(2)}) async-start(f32[8,256,1]{1,2,0:T(1,128)} %all_to_all.30), calls=%async_computation.3 | async-start | bytes 16384 | tf_op jit(solution)/shard_map/all_to_all | solution.py:70
  611.5 14.6 %copy-start.2 = (f32[256]{0:T(256)}, f32[256]{0:T(256)S(1)}, u32[]{:S(2)}) copy-start(f32[256]{0:T(256)S(1)} %get-tuple-element.117) | copy-start | bytes 3076
  611.6 14.6 %copy-start.3 = (f32[256]{0:T(256)}, f32[256]{0:T(256)S(1)}, u32[]{:S(2)}) copy-start(f32[256]{0:T(256)S(1)} %get-tuple-element.118) | copy-start | bytes 3076
Sparse Core Ops, SparseCore 0:
  9.6 153.7 all-gather.2
  165.3 295.3 all-gather.4
where the time goes:
time: 633 us
  waiting for transfers between devices  448 us (71%)
  matrix products  91.7 us (14%)
  other arithmetic  30.9 us (5%)
  local copies, waits for them, and re-layouts  16.7 us (3%)
  starting transfers between devices  14.7 us (2%)
  between operations  14.2 us (2%)
  blocking collectives  13.8 us (2%)
    all_gather x1, waiting for transfers between devices, shards(): columns = lax.all_gather(head, 'req', axis=1, tiled=True)  273 us
    all_gather x1, waiting for transfers between devices, shards(): full_rows = lax.all_gather(hidden, 'vocab', axis=1, tiled=True)  155 us
    dot_general x4, matrix products, block_logits(): return jnp.dot(rows_blk, columns, preferred_element_type=jnp.float32)  91.7 us
    psum x1, blocking collectives, shards(): sum_lp, sum_ent = lax.psum((part_lp, part_ent), 'vocab')  13.8 us
  transfers between devices with their start and end apart: 6, of which 6 were waited for; matrix products, arithmetic and copies ran while one was open for 3% of the time, Pallas kernels for 0%

commit v1 on v0

v1 whole, which is shorter than its diff:
```python
import functools
import jax
import jax.numpy as jnp
from jax import lax
from jax.experimental import pallas as pl
from jax.experimental.pallas import tpu as pltpu
from jax.sharding import PartitionSpec as P


def round_up(n, m):
    return (n + m - 1) // m * m


def stats_kernel(tiles, groups, n_pieces, n_heads, *refs):
    kofs, colbase, rs_ref, tgt_ref = refs[:4]
    pieces = refs[4 : 4 + n_pieces]
    heads = refs[4 + n_pieces : 4 + n_pieces + n_heads]
    out_ref, x_scr, h_scr, m_scr, s_scr, w_scr, p_scr, x_sem, h_sem = refs[4 + n_pieces + n_heads :]
    r, i = pl.program_id(0), pl.program_id(1)
    n_tiles, n_steps = len(tiles), sum(g[2] for g in groups)
    width = h_scr.shape[3]
    step = r * n_steps + i
    xs = lax.rem(r, x_scr.shape[0])
    hs = lax.rem(step, 2) if n_steps > 1 else 0

    def row_copies(k, slot):
        return [
            pltpu.make_async_copy(
                pieces[a].at[pl.ds(src, rows)],
                x_scr.at[slot, pl.ds(dst, rows), pl.ds(pl.multiple_of(kofs[j], 128), pieces[a].shape[1])],
                x_sem.at[slot],
            )
            for a, j, src, rows, dst in tiles[k]
        ]

    def head_copies(g, block, slot):
        return [
            pltpu.make_async_copy(
                heads[groups[g][which]].at[:, pl.ds(pl.multiple_of(block * width, width), width)],
                h_scr.at[slot, which],
                h_sem.at[slot],
            )
            for which in range(2)
        ]

    def start_head(at, slot):
        first = 0
        for g, (_, _, blocks) in enumerate(groups):
            @pl.when((at >= first) & (at < first + blocks))
            def _(g=g, first=first):
                for copy in head_copies(g, at - first, slot):
                    copy.start()
            first += blocks

    def start_rows(at, slot):
        for k in range(n_tiles):
            @pl.when(at == k)
            def _(k=k):
                for copy in row_copies(k, slot):
                    copy.start()

    @pl.when(step == 0)
    def _():
        start_rows(0, 0)
        start_head(0, 0)

    @pl.when(i == 0)
    def _():
        if n_tiles > 1:
            @pl.when(r + 1 < n_tiles)
            def _():
                start_rows(r + 1, lax.rem(r + 1, 2))
        m_scr[...] = jnp.full(m_scr.shape, -jnp.inf, jnp.float32)
        s_scr[...] = jnp.zeros(s_scr.shape, jnp.float32)
        w_scr[...] = jnp.zeros(w_scr.shape, jnp.float32)
        p_scr[...] = jnp.zeros(p_scr.shape, jnp.float32)
        for k in range(n_tiles):
            @pl.when(r == k)
            def _(k=k):
                for copy in row_copies(k, xs):
                    copy.wait()

    if n_steps > 1:
        @pl.when(step + 1 < n_tiles * n_steps)
        def _():
            start_head(lax.rem(i + 1, n_steps), lax.rem(step + 1, 2))
    @pl.when((i == 0) & (r == 0) if n_steps == 1 else i >= 0)
    def _():
        for copy in head_copies(0, 0, hs):
            copy.wait()

    rows = x_scr.shape[1]
    sub = 64
    lane = lax.broadcasted_iota(jnp.int32, (sub, 128), 1)
    for which in range(2):
        raw = jnp.dot(x_scr[xs], h_scr[hs, which], preferred_element_type=jnp.float32)
        base = colbase[i * 2 + which]
        for at in range(0, rows, sub):
            here = pl.ds(at, sub)
            scale = rs_ref[here, :]
            wanted = tgt_ref[here, :] - base - lane
            parts = [raw[at : at + sub, c : c + 128] * scale for c in range(0, width, 128)]
            old = m_scr[here, :]
            new = functools.reduce(jnp.maximum, parts, old)
            fade = jnp.exp(old - new)
            total, moment, picked = s_scr[here, :] * fade, w_scr[here, :] * fade, p_scr[here, :]
            for c, part in enumerate(parts):
                weight = jnp.exp(part - new)
                total += weight
                moment += weight * part
                picked = jnp.where(wanted == c * 128, part, picked)
            m_scr[here, :], s_scr[here, :], w_scr[here, :], p_scr[here, :] = new, total, moment, picked

    @pl.when(i == n_steps - 1)
    def _():
        peak_t = m_scr[...].T
        peak = jnp.max(peak_t, axis=0, keepdims=True)
        fade = jnp.exp(peak_t - peak)
        out_ref[0:1, :] = peak
        out_ref[1:2, :] = jnp.sum(s_scr[...].T * fade, axis=0, keepdims=True)
        out_ref[2:3, :] = jnp.sum(w_scr[...].T * fade, axis=0, keepdims=True)
        out_ref[3:4, :] = jnp.sum(p_scr[...].T, axis=0, keepdims=True)


def stats(tiles, tile_rows, groups, kofs, colbase, scale, wanted, pieces, heads):
    rows = round_up(tile_rows, 128)
    n_tiles, n_steps = len(tiles), sum(g[2] for g in groups)
    depth = heads[0].shape[0]
    width = min([256] + [h.shape[1] for h in heads])

    def column(v):
        return jnp.pad(v.reshape(n_tiles, tile_rows), ((0, 0), (0, rows - tile_rows))).reshape(-1, 1)

    row_block = pl.BlockSpec((rows, 1), lambda r, i: (r, 0))
    out = pl.pallas_call(
        functools.partial(stats_kernel, tiles, groups, len(pieces), len(heads)),
        grid=(n_tiles, n_steps),
        in_specs=[pl.BlockSpec(memory_space=pltpu.SMEM)] * 2
        + [row_block] * 2
        + [pl.BlockSpec(memory_space=pl.ANY)] * (len(pieces) + len(heads)),
        out_specs=pl.BlockSpec((4, rows), lambda r, i: (0, r)),
        out_shape=jax.ShapeDtypeStruct((4, n_tiles * rows), jnp.float32),
        scratch_shapes=[
            pltpu.VMEM((min(n_tiles, 2), rows, depth), jnp.bfloat16),
            pltpu.VMEM((min(n_steps, 2), 2, depth, width), jnp.bfloat16),
        ]
        + [pltpu.VMEM((rows, 128), jnp.float32)] * 4
        + [pltpu.SemaphoreType.DMA((min(n_tiles, 2),)), pltpu.SemaphoreType.DMA((min(n_steps, 2),))],
        compiler_params=pltpu.CompilerParams(
            dimension_semantics=("arbitrary", "arbitrary"), vmem_limit_bytes=48 * 1024 * 1024
        ),
        cost_estimate=pl.CostEstimate(
            flops=2 * n_tiles * rows * n_steps * 2 * width * depth,
            bytes_accessed=2 * depth * (n_tiles * rows + 2 * width * n_steps),
            transcendentals=n_tiles * rows * n_steps * 2 * width,
        ),
    )(kofs, colbase, column(scale), column(wanted), *pieces, *heads)
    return out.reshape(4, n_tiles, rows)[:, :, :tile_rows].reshape(4, n_tiles * tile_rows)


EPS = 1e-05
SHRINK = 2.0**-9


def merge(stats):
    peak, total, moment, picked = (stats[:, k] for k in range(4))
    best = jnp.max(peak, axis=0)
    fade = jnp.exp(peak - best[None])
    return jnp.stack(
        [best, jnp.sum(total * fade, axis=0), jnp.sum(moment * fade, axis=0), jnp.sum(picked, axis=0)]
    )


def shards(hidden, gain, head, targets, lengths):
    n_req, n_vocab = lax.axis_size("req"), lax.axis_size("vocab")
    q, v = lax.axis_index("req"), lax.axis_index("vocab")
    spots = n_vocab // 2
    s, c = v // 2, v % 2
    rows, feats = hidden.shape
    depth, cols = head.shape
    blk, half = rows // n_vocab, rows // 2
    cut = half - blk
    every = ("req", "vocab")

    def move(x, where):
        pairs = [
            (a * n_vocab + b, where(a, b)) for a in range(n_req) for b in range(n_vocab)
        ]
        return lax.ppermute(x, every, pairs)

    def to_core(x):
        return move(x, lambda a, b: a * n_vocab + (b ^ 1))

    def to_x(x):
        return move(x, lambda a, b: (a ^ 1) * n_vocab + b)

    def to_y(x):
        return move(x, lambda a, b: (a ^ 2) * n_vocab + b)

    def to_z(x):
        return move(x, lambda a, b: a * n_vocab + (b + 2) % n_vocab)

    def ring(x):
        out = [x]
        for _ in range(spots - 1):
            out.append(to_z(out[-1]))
        return out

    n_far = max(1, min(4, cols // 128))
    far_cols = cols // n_far
    far = [to_x(head[:, k * far_cols : (k + 1) * far_cols]) for k in range(n_far)]

    values = hidden.astype(jnp.float32)
    own_gain = lax.dynamic_slice_in_dim(gain, v * feats, feats) * SHRINK
    scaled = (values * own_gain[None, :]).astype(jnp.bfloat16).reshape(spots, 2, blk, feats)
    mine = lax.dynamic_index_in_dim(scaled, c, 1, keepdims=False).reshape(half, feats)
    other = lax.dynamic_index_in_dim(scaled, 1 - c, 1, keepdims=False).reshape(half, feats)
    got = to_core(other)
    piece = jnp.where(
        c == 0, jnp.concatenate([mine, got], axis=1), jnp.concatenate([got, mine], axis=1)
    )
    a0, b0 = piece[:cut], piece[cut:]
    yb0 = to_y(b0)
    a_pieces = ring(a0)
    ya_pieces = [to_y(p) for p in a_pieces]
    b_pieces = ring(b0)
    yb_pieces = ring(yb0)

    near = to_core(head)
    far_near = [to_core(h) for h in far]

    square = lax.psum(jnp.sum(values * values, axis=1), "vocab")
    scale = lax.rsqrt(square / depth + EPS) * (1.0 / SHRINK)
    scale = lax.dynamic_index_in_dim(scale.reshape(spots, 2, blk), c, 1, keepdims=False).reshape(half)
    wanted = lax.dynamic_index_in_dim(targets.reshape(spots, 2, blk), c, 1, keepdims=False).reshape(half)
    y_side = to_y(jnp.stack([scale, wanted.astype(jnp.float32)]))
    y_scale, y_wanted = y_side[0], y_side[1].astype(jnp.int32)

    kofs = (s + spots - jnp.arange(spots, dtype=jnp.int32)) % spots * (2 * feats)
    own_base = (q * n_vocab + v) * cols
    pair_base = (q * n_vocab + (v ^ 1)) * cols
    far_base = ((q ^ 1) * n_vocab + v) * cols
    far_pair_base = ((q ^ 1) * n_vocab + (v ^ 1)) * cols
    groups = [(head, near, own_base, pair_base)] + [
        (far[k], far_near[k], far_base + k * far_cols, far_pair_base + k * far_cols)
        for k in range(n_far)
    ]

    def call(row_sets, chosen):
        tiles, arrays, scales, wants = [], [], [], []
        for sets in row_sets:
            at, tile = 0, []
            for pieces, set_scale, set_wanted in sets:
                n = set_scale.shape[0]
                for j, p in enumerate(pieces):
                    tile.append((len(arrays), j, 0, n, at))
                    arrays.append(p)
                at += n
                scales.append(set_scale)
                wants.append(set_wanted)
            tiles.append(tile)
        width = min(256, far_cols)
        plan, heads, bases = [], [], []
        for g in chosen:
            one, two, base, pair = groups[g]
            blocks = one.shape[1] // width
            plan.append((len(heads), len(heads) + 1, blocks))
            heads += [one, two]
            for k in range(blocks):
                bases += [base + k * width, pair + k * width]
        return stats(
            tiles,
            at,
            plan,
            kofs,
            jnp.stack(bases).astype(jnp.int32),
            jnp.concatenate(scales),
            jnp.concatenate(wants),
            arrays,
            heads,
        )

    set_a = (a_pieces, scale[:cut], wanted[:cut])
    set_b = (b_pieces, scale[cut:], wanted[cut:])
    set_ya = (ya_pieces, y_scale[:cut], y_wanted[:cut])
    set_yb = (yb_pieces, y_scale[cut:], y_wanted[cut:])
    last = n_far
    early = list(range(0, max(1, last - 1)))
    late = list(range(max(1, last - 1), last))
    parts_a = [call([[set_a]], early)]
    if late:
        parts_a.append(call([[set_a]], late))
    parts_ya = [call([[set_ya]], early + late)]
    both = call([[set_b, set_yb]], early + late)
    ends = call([[set_a, set_b], [set_ya, set_yb]], [last])
    own = jnp.concatenate([merge(jnp.stack(parts_a)), both[:, :blk]], axis=1)
    peer = jnp.concatenate([parts_ya[0], both[:, blk:]], axis=1)
    own = merge(jnp.stack([own, ends[:, :half]]))
    peer = merge(jnp.stack([peer, ends[:, half:]]))

    first = q // 2 == 0
    whole = jnp.stack([jnp.where(first, own, peer), jnp.where(first, peer, own)])
    whole = whole.reshape(2, 4, spots, blk).transpose(0, 2, 1, 3).reshape(2 * spots, 4 * blk)
    kin = [
        [(2 * a + b) * n_vocab + 2 * k + core for a in range(2) for k in range(spots)]
        for b in range(2)
        for core in range(2)
    ]
    whole = lax.all_to_all(
        whole, every, split_axis=0, concat_axis=0, axis_index_groups=kin, tiled=True
    )
    peak, total, moment, picked = merge(whole.reshape(2 * spots, 4, blk))
    log_total = peak + jnp.log(total)
    lp, ent = picked - log_total, log_total - moment / total

    seq_lens = lengths[0, :-1]
    stops = jnp.cumsum(seq_lens)
    starts = stops - seq_lens
    local = v * blk + jnp.arange(blk, dtype=jnp.int32)
    valid = local < stops[-1]
    lp = jnp.where(valid, lp, 0.0)
    ent = jnp.where(valid, ent, 0.0)
    member = (local[None, :] >= starts[:, None]) & (local[None, :] < stops[:, None])
    sums = jnp.sum(jnp.where(member[None], jnp.stack([lp, ent])[:, None, :], 0.0), axis=2)
    sums = jnp.sum(
        lax.all_to_all(
            jnp.broadcast_to(sums.reshape(1, -1), (n_vocab, sums.size)),
            "vocab",
            split_axis=0,
            concat_axis=0,
            tiled=True,
        ),
        axis=0,
    ).reshape(sums.shape)
    means = sums / seq_lens.astype(jnp.float32)[None]
    return (lp, ent, means[0], means[1])


def solution(mesh):
    in_specs = (P("req", "vocab"), P(), P(None, ("req", "vocab")), P("req"), P("req", None))
    out_specs = (P(("req", "vocab")), P(("req", "vocab")), P("req"), P("req"))
    return jax.shard_map(shards, mesh=mesh, in_specs=in_specs, out_specs=out_specs, check_vma=False)
```

time: 633 us -> 439 us (0.69)
  waiting for transfers between devices: 448 us -> 216 us
  Pallas kernels: 0 us -> 109 us
  matrix products: 91.7 us -> 0 us
  local copies, waits for them, and re-layouts: 16.7 us -> 39.9 us
  blocking collectives: 13.8 us -> 31 us
  other arithmetic: 30.9 us -> 14.6 us
  between operations: 14.2 us -> 1.34 us
  starting transfers between devices: 14.7 us -> 26.3 us
    all_gather x2 -> x0, waiting for transfers between devices: 427 us -> none  [the longest x1 273 us: shards(): columns = lax.all_gather(head, 'req', axis=1, tiled=True)]
    ppermute x0 -> x25, waiting for transfers between devices: none -> 210 us  [move(): return lax.ppermute(x, every, pairs)]
    pallas_call x0 -> x5, Pallas kernels: none -> 109 us  [stats(): pl.pallas_call(functools.partial(stats_kernel, tiles, groups, len(pieces)...]
    dot_general x4 -> x0, matrix products: 91.7 us -> none  [block_logits(): return jnp.dot(rows_blk, columns, preferred_element_type=jnp.float32)]
    ppermute x0 -> x25, starting transfers between devices: none -> 22.7 us  [move(): return lax.ppermute(x, every, pairs)]
    reduce_sum x8 -> x6, other arithmetic: 20 us -> 0.24 us  [the longest x3 0.1 us: merge(): jnp.sum(total * fade, axis=0)]
    reshape x1 -> x14, local copies, waits for them, and re-layouts: 0.01 us -> 14.5 us  [the longest x10 14.4 us: column(): jnp.pad(v.reshape(n_tiles, tile_rows), ((0, 0), (0, rows - tile_rows)))]
    all_to_all x4 -> x1, waiting for transfers between devices: 19.5 us -> 6.05 us  [shards(): lax.all_to_all(whole, every, split_axis=0, concat_axis=0, axis_index_grou...]
  transfers between devices with their start and end apart: 6 -> 26, of which waited for: 6 -> 14; matrix products, arithmetic and copies ran while one was open for 3% -> 8% of each run, Pallas kernels for 0% -> 6%
where the time goes in v1:
time: 439 us; the launch traced here: 438 us
  waiting for transfers between devices  216 us (49%)
  Pallas kernels  109 us (25%)
  local copies, waits for them, and re-layouts  39.9 us (9%)
  blocking collectives  31 us (7%)
  starting transfers between devices  26.3 us (6%)
  other arithmetic  14.6 us (3%)
    ppermute x25, waiting for transfers between devices, move(): return lax.ppermute(x, every, pairs)  210 us
    pallas_call x5, Pallas kernels, stats(): pl.pallas_call(functools.partial(stats_kernel, tiles, groups, len(pieces)...  109 us
    psum x1, blocking collectives, shards(): square = lax.psum(jnp.sum(values * values, axis=1), 'vocab')  23.1 us
    ppermute x25, starting transfers between devices, move(): return lax.ppermute(x, every, pairs)  22.7 us
    reshape x10, local copies, waits for them, and re-layouts, column(): jnp.pad(v.reshape(n_tiles, tile_rows), ((0, 0), (0, rows - tile_rows)))  14.4 us
    unnamed x78, local copies, waits for them, and re-layouts  9.02 us
  transfers between devices with their start and end apart: 26, of which 14 were waited for; matrix products, arithmetic and copies ran while one was open for 8% of the time, Pallas kernels for 6%

profile of v1, /device:TPU:0, one launch (start us, length us, event | category | flops | bytes accessed | tf_op | source)
XLA Modules:
  0.0 437.9 jit_solution(11644792139516320008)
XLA Ops:
  1.4 2.3 fusion.1
  5.7 6.3 %fusion.46 = (bf16[4096,256]{1,0:T(8,128)(2,1)}, bf16[4096,256]{1,0:T(8,128)(2,1)}, bf16[4096,256]{1,0:T(8,128)(2,1)}, bf16[4096,256]{1,0:T(8,128)(2,1)}) fusion(bf16[4096,1024]{1,0:T(8,128)(2,1)} %refs_8_.3), kind=kLoop, calls=%fused_computation.131 | loop fusion | bytes 16777216 | tf_op jit(solution)/shard_map/slice | solution.py:211
  12.1 2.6 collective-permute-start.23
  18.3 23.1 %psum.7 = f32[2048]{0:T(1024)S(1)} all-reduce(f32[2048]{0:T(1024)S(1)} %get-tuple-element.35), channel_id=1, replica_groups=mesh['req'=4,'vocab'=8] {'vocab'}, use_global_device_ids=true, to_apply=%region_2.3 | all-reduce | flops 2048 | bytes 16384 | tf_op jit(solution)/shard_map/psum | solution.py:232
  43.8 9.8 %collective-permute-done.15.refs_8_.refs_16_ = bf16[256,1024]{1,0:T(8,128)(2,1)S(1)} collective-permute-done((bf16[256,1024]{1,0:T(8,128)(2,1)S(1)}, bf16[256,1024]{1,0:T(8,128)(2,1)S(1)}, u32[]{:S(2)}, u32[]{:S(2)}) %collective-permute-start.15) | collective-permute-done | bytes 524320 | tf_op jit(solution)/shard_map/ppermute | solution.py:189
  58.1 12.2 %collective-permute-done.16.refs_9_.refs_17_ = bf16[256,1024]{1,0:T(8,128)(2,1)S(1)} collective-permute-done((bf16[256,1024]{1,0:T(8,128)(2,1)S(1)}, bf16[256,1024]{1,0:T(8,128)(2,1)S(1)}, u32[]{:S(2)}, u32[]{:S(2)}) %collective-permute-start.16) | collective-permute-done | bytes 524320 | tf_op jit(solution)/shard_map/ppermute | solution.py:189
  72.3 29.4 %collective-permute-done.1.refs_5_ = bf16[768,1024]{1,0:T(8,128)(2,1)} collective-permute-done((bf16[768,1024]{1,0:T(8,128)(2,1)S(1)}, bf16[768,1024]{1,0:T(8,128)(2,1)}, u32[]{:S(2)}, u32[]{:S(2)}) %collective-permute-start.1) | collective-permute-done | bytes 1572896 | tf_op jit(solution)/shard_map/ppermute | solution.py:189
  101.7 4.5 %collective-permute-done.5.refs_10_.refs_14_ = bf16[4096,256]{1,0:T(8,128)(2,1)S(1)} collective-permute-done((bf16[4096,256]{1,0:T(8,128)(2,1)}, bf16[4096,256]{1,0:T(8,128)(2,1)S(1)}, u32[]{:S(2)}, u32[]{:S(2)}) %collective-permute-start.5) | collective-permute-done | bytes 2097184 | tf_op jit(solution)/shard_map/ppermute | solution.py:189
  108.3 43.1 %collective-permute-done.7.refs_12_.refs_16_ = bf16[4096,256]{1,0:T(8,128)(2,1)} collective-permute-done((bf16[4096,256]{1,0:T(8,128)(2,1)}, bf16[4096,256]{1,0:T(8,128)(2,1)}, u32[]{:S(2)}, u32[]{:S(2)}) %collective-permute-start.7) | collective-permute-done | bytes 2097184 | tf_op jit(solution)/shard_map/ppermute | solution.py:189
  154.2 41.8 %collective-permute-done.9.refs_8_.refs_18_.refs_14_ = bf16[4096,256]{1,0:T(8,128)(2,1)} collective-permute-done((bf16[4096,256]{1,0:T(8,128)(2,1)S(1)}, bf16[4096,256]{1,0:T(8,128)(2,1)}, u32[]{:S(2)}, u32[]{:S(2)}) %collective-permute-start.9) | collective-permute-done | bytes 2097184 | tf_op jit(solution)/shard_map/ppermute | solution.py:189
  201.0 11.6 %collective-permute-done.14.refs_7_.refs_11_ = bf16[256,1024]{1,0:T(8,128)(2,1)S(1)} collective-permute-done((bf16[256,1024]{1,0:T(8,128)(2,1)S(1)}, bf16[256,1024]{1,0:T(8,128)(2,1)S(1)}, u32[]{:S(2)}, u32[]{:S(2)}) %collective-permute-start.14) | collective-permute-done | bytes 524320 | tf_op jit(solution)/shard_map/ppermute | solution.py:189
  216.4 7.5 %collective-permute-done.18.refs_11_.refs_19_ = bf16[256,1024]{1,0:T(8,128)(2,1)S(1)} collective-permute-done((bf16[256,1024]{1,0:T(8,128)(2,1)S(1)}, bf16[256,1024]{1,0:T(8,128)(2,1)S(1)}, u32[]{:S(2)}, u32[]{:S(2)}) %collective-permute-start.18) | collective-permute-done | bytes 524320 | tf_op jit(solution)/shard_map/ppermute | solution.py:189
  228.9 19.2 %collective-permute-done.20.refs_13_.refs_5_ = bf16[768,1024]{1,0:T(8,128)(2,1)} collective-permute-done((bf16[768,1024]{1,0:T(8,128)(2,1)}, bf16[768,1024]{1,0:T(8,128)(2,1)}, u32[]{:S(2)}, u32[]{:S(2)}) %collective-permute-start.20) | collective-permute-done | bytes 1572896 | tf_op jit(solution)/shard_map/ppermute | solution.py:189
  249.7 6.9 %collective-permute-done.3.refs_7_ = bf16[768,1024]{1,0:T(8,128)(2,1)} collective-permute-done((bf16[768,1024]{1,0:T(8,128)(2,1)}, bf16[768,1024]{1,0:T(8,128)(2,1)}, u32[]{:S(2)}, u32[]{:S(2)}) %collective-permute-start.3) | collective-permute-done | bytes 1572896 | tf_op jit(solution)/shard_map/ppermute | solution.py:189
  270.1 2.1 copy.114.refs_3_
  284.0 8.8 %shard_map.85 = f32[4,768]{1,0:T(4,128)S(1)} custom-call(s32[4]{0:T(128)S(1)} %copy-done.24, s32[2]{0:T(128)S(1)} %pad_add_fusion.2.refs_1_, f32[768,1]{1,0:T(8,128)S(1)} %copy.105.refs_2_, s32[768,1]{1,0:T(8,128)S(1)} %copy-done.2, bf16[768,1024]{1,0:T(8,128)(2,1)S(1)} %slice.190.refs_4_, bf16[768,1024]{1,0:T(8,128)(2,1)} %collective-permute-done.1.refs_5_, ...), custom_call_target="tpu_custom_call" | custom-call | flops 3221225472 | bytes 10485760 | tf_op jit(solution)/shard_map/pallas_call | solution.py:135
  292.8 22.7 %collective-permute-done.22.refs_15_.refs_7_ = bf16[768,1024]{1,0:T(8,128)(2,1)} collective-permute-done((bf16[768,1024]{1,0:T(8,128)(2,1)}, bf16[768,1024]{1,0:T(8,128)(2,1)}, u32[]{:S(2)}, u32[]{:S(2)}) %collective-permute-start.22) | collective-permute-done | bytes 1572896 | tf_op jit(solution)/shard_map/ppermute | solution.py:189
  315.5 16.3 %shard_map.87 = f32[4,2048]{1,0:T(4,128)S(1)} custom-call(s32[4]{0:T(128)S(1)} %copy-done.24, s32[2]{0:T(128)S(1)} %pad_add_fusion.3.refs_1_, f32[2048,1]{1,0:T(8,128)S(1)} %copy.113.refs_2_, s32[2048,1]{1,0:T(8,128)} %copy.114.refs_3_, bf16[768,1024]{1,0:T(8,128)(2,1)} %copy-done, bf16[768,1024]{1,0:T(8,128)(2,1)} %collective-permute-done.1.refs_5_, ...), custom_call_target="tpu_custom_call" | custom-call | flops 8589934592 | bytes 20971520 | tf_op jit(solution)/shard_map/pallas_call | solution.py:135
  331.9 22.3 %shard_map.86 = f32[4,512]{1,0:T(4,128)S(1)} custom-call(s32[4]{0:T(128)S(1)} %copy-done.24, s32[14]{0:T(128)S(1)} %stack.191.refs_1_, f32[512,1]{1,0:T(8,128)S(1)} %copy-done.6, s32[512,1]{1,0:T(8,128)S(1)} %copy-done.7, bf16[256,1024]{1,0:T(8,128)(2,1)S(1)} %slice.200.refs_4_.refs_8_, bf16[256,1024]{1,0:T(8,128)(2,1)S(1)} %copy-done.11, ...), custom_call_target="tpu_custom_call" | custom-call | flops 15032385536 | bytes 33554432 | tf_op jit(solution)/shard_map/pallas_call | solution.py:135
  354.3 28.7 %shard_map.84 = f32[4,768]{1,0:T(4,128)S(1)} custom-call(s32[4]{0:T(128)S(1)} %copy-done.24, s32[12]{0:T(128)S(1)} %stack.181.refs_1_, f32[768,1]{1,0:T(8,128)S(1)} %copy.105.refs_2_, s32[768,1]{1,0:T(8,128)S(1)} %copy-done.3, bf16[768,1024]{1,0:T(8,128)(2,1)S(1)} %copy-done.1, bf16[768,1024]{1,0:T(8,128)(2,1)} %collective-permute-done.1.refs_5_, ...), custom_call_target="tpu_custom_call" | custom-call | flops 19327352832 | bytes 31457280 | tf_op jit(solution)/shard_map/pallas_call | solution.py:135
  383.3 32.4 %shard_map.88 = f32[4,768]{1,0:T(4,128)S(1)} custom-call(s32[4]{0:T(128)S(1)} %copy-done.24, s32[14]{0:T(128)S(1)} %stack.191.refs_1_, f32[768,1]{1,0:T(8,128)S(1)} %copy-done.4, s32[768,1]{1,0:T(8,128)S(1)} %copy-done.5, bf16[768,1024]{1,0:T(8,128)(2,1)S(1)} %copy-done.9, bf16[768,1024]{1,0:T(8,128)(2,1)} %collective-permute-done.20.refs_13_.refs_5_, ...), custom_call_target="tpu_custom_call" | custom-call | flops 22548578304 | bytes 35651584 | tf_op jit(solution)/shard_map/pallas_call | solution.py:135
  416.6 3.6 all-to-all-start
  421.0 6.0 %all-to-all-done = f32[8,1,1024]{2,1,0:T(1,128)S(1)} async-done(((f32[8,1,1024]{2,1,0:T(1,128)}), f32[8,1,1024]{2,1,0:T(1,128)S(1)}, u32[]{:S(2)}, u32[]{:S(2)}) %all-to-all-start) | async-done | bytes 32800 | tf_op jit(solution)/shard_map/all_to_all | solution.py:309
  429.4 7.9 %all_to_all.16 = f32[8,1,6]{2,1,0:T(1,128)S(1)} all-to-all(f32[8,1,6]{2,1,0:T(1,128)S(1)} %broadcast_in_dim.60), channel_id=1, replica_groups=mesh['req'=4,'vocab'=8] {'vocab'}, dimensions={0} | all-to-all | bytes 384 | tf_op jit(solution)/shard_map/all_to_all | solution.py:326
  (192 shorter events, 65.4 us)
Async XLA Ops:
  12.1 59.0 %collective-permute-start.23 = (bf16[4096,256]{1,0:T(8,128)(2,1)}, bf16[4096,256]{1,0:T(8,128)(2,1)}, u32[]{:S(2)}, u32[]{:S(2)}) collective-permute-start(bf16[4096,256]{1,0:T(8,128)(2,1)} %get-tuple-element.31), channel_id=1, source_target_pairs={{0,8},{1,9},{2,10},{3,11},{4,12},{5,13},{6,14},{7,15},{8,0},{9,1},... | collective-permute-start | bytes 6291464 | tf_op jit(solution)/shard_map/ppermute | solution.py:189
  16.7 26.4 %collective-permute-start.12 = (bf16[256,1024]{1,0:T(8,128)(2,1)S(1)}, bf16[256,1024]{1,0:T(8,128)(2,1)S(1)}, u32[]{:S(2)}, u32[]{:S(2)}) collective-permute-start(bf16[256,1024]{1,0:T(8,128)(2,1)S(1)} %slice.200.refs_4_.refs_8_), channel_id=1, source_target_pairs={{0,2},{1,3},{2,4},{3,5},{4,6},{5,7},{6,0},{7,1},{8,10},{9,11},{10,... | collective-permute-start | bytes 1572872 | tf_op jit(solution)/shard_map/ppermute | solution.py:189
  18.3 313.6 %collective-permute-start.4 = (bf16[4096,1024]{1,0:T(8,128)(2,1)}, bf16[4096,1024]{1,0:T(8,128)(2,1)}, u32[]{:S(2)}, u32[]{:S(2)}) collective-permute-start(bf16[4096,1024]{1,0:T(8,128)(2,1)} %refs_8_.3), channel_id=1, source_target_pairs={{0,1},{1,0},{2,3},{3,2},{4,5},{5,4},{6,7},{7,6},{8,9},{9,8},{10,11... | collective-permute-start | bytes 25165832 | tf_op jit(solution)/shard_map/ppermute | solution.py:189
  41.4 12.1 %collective-permute-start.15 = (bf16[256,1024]{1,0:T(8,128)(2,1)S(1)}, bf16[256,1024]{1,0:T(8,128)(2,1)S(1)}, u32[]{:S(2)}, u32[]{:S(2)}) collective-permute-start(bf16[256,1024]{1,0:T(8,128)(2,1)S(1)} %slice.200.refs_4_.refs_8_), channel_id=1, source_target_pairs={{0,16},{1,17},{2,18},{3,19},{4,20},{5,21},{6,22},{7,23},{8,24},{9,... | collective-permute-start | bytes 1572872 | tf_op jit(solution)/shard_map/ppermute | solution.py:189
  43.1 14.9 %collective-permute-start.13 = (bf16[256,1024]{1,0:T(8,128)(2,1)S(1)}, bf16[256,1024]{1,0:T(8,128)(2,1)S(1)}, u32[]{:S(2)}, u32[]{:S(2)}) collective-permute-start(bf16[256,1024]{1,0:T(8,128)(2,1)S(1)} %collective-permute-done.12.refs_5_.refs_9_), channel_id=1, source_target_pairs={{0,2},{1,3},{2,4},{3,5},{4,6},{5,7},{6,0},{7,1},{8,10},{9,11},{10,... | collective-permute-start | bytes 1572872 | tf_op jit(solution)/shard_map/ppermute | solution.py:189
  43.2 10.5 %collective-permute-start.11 = (f32[2,1024]{1,0:T(2,128)S(1)}, f32[2,1024]{1,0:T(2,128)S(1)}, u32[]{:S(2)}, u32[]{:S(2)}) collective-permute-start(f32[2,1024]{1,0:T(2,128)S(1)} %pad_maximum_fusion.4), channel_id=1, source_target_pairs={{0,16},{1,17},{2,18},{3,19},{4,20},{5,21},{6,22},{7,23},{8,24},{9,... | collective-permute-start | bytes 24584 | tf_op jit(solution)/shard_map/ppermute | solution.py:189
  53.6 16.7 %collective-permute-start.16 = (bf16[256,1024]{1,0:T(8,128)(2,1)S(1)}, bf16[256,1024]{1,0:T(8,128)(2,1)S(1)}, u32[]{:S(2)}, u32[]{:S(2)}) collective-permute-start(bf16[256,1024]{1,0:T(8,128)(2,1)S(1)} %collective-permute-done.15.refs_8_.refs_16_), channel_id=1, source_target_pairs={{0,2},{1,3},{2,4},{3,5},{4,6},{5,7},{6,0},{7,1},{8,10},{9,11},{10,... | collective-permute-start | bytes 1572872 | tf_op jit(solution)/shard_map/ppermute | solution.py:189
  54.4 51.9 %collective-permute-start.5 = (bf16[4096,256]{1,0:T(8,128)(2,1)}, bf16[4096,256]{1,0:T(8,128)(2,1)S(1)}, u32[]{:S(2)}, u32[]{:S(2)}) collective-permute-start(bf16[4096,256]{1,0:T(8,128)(2,1)} %get-tuple-element.30), channel_id=1, source_target_pairs={{0,8},{1,9},{2,10},{3,11},{4,12},{5,13},{6,14},{7,15},{8,0},{9,1},... | collective-permute-start | bytes 6291464 | tf_op jit(solution)/shard_map/ppermute | solution.py:189
  58.0 43.7 %collective-permute-start.1 = (bf16[768,1024]{1,0:T(8,128)(2,1)S(1)}, bf16[768,1024]{1,0:T(8,128)(2,1)}, u32[]{:S(2)}, u32[]{:S(2)}) collective-permute-start(bf16[768,1024]{1,0:T(8,128)(2,1)S(1)} %slice.190.refs_4_), channel_id=1, source_target_pairs={{0,2},{1,3},{2,4},{3,5},{4,6},{5,7},{6,0},{7,1},{8,10},{9,11},{10,... | collective-permute-start | bytes 4718600 | tf_op jit(solution)/shard_map/ppermute | solution.py:189
  70.2 81.1 %collective-permute-start.7 = (bf16[4096,256]{1,0:T(8,128)(2,1)}, bf16[4096,256]{1,0:T(8,128)(2,1)}, u32[]{:S(2)}, u32[]{:S(2)}) collective-permute-start(bf16[4096,256]{1,0:T(8,128)(2,1)} %get-tuple-element.29), channel_id=1, source_target_pairs={{0,8},{1,9},{2,10},{3,11},{4,12},{5,13},{6,14},{7,15},{8,0},{9,1},... | collective-permute-start | bytes 6291464 | tf_op jit(solution)/shard_map/ppermute | solution.py:189
  71.0 125.0 %collective-permute-start.9 = (bf16[4096,256]{1,0:T(8,128)(2,1)S(1)}, bf16[4096,256]{1,0:T(8,128)(2,1)}, u32[]{:S(2)}, u32[]{:S(2)}) collective-permute-start(bf16[4096,256]{1,0:T(8,128)(2,1)S(1)} %copy-done.27), channel_id=1, source_target_pairs={{0,8},{1,9},{2,10},{3,11},{4,12},{5,13},{6,14},{7,15},{8,0},{9,1},... | collective-permute-start | bytes 6291464 | tf_op jit(solution)/shard_map/ppermute | solution.py:189
  101.7 113.5 %collective-permute-start.2 = (bf16[768,1024]{1,0:T(8,128)(2,1)}, bf16[768,1024]{1,0:T(8,128)(2,1)}, u32[]{:S(2)}, u32[]{:S(2)}) collective-permute-start(bf16[768,1024]{1,0:T(8,128)(2,1)} %collective-permute-done.1.refs_5_), channel_id=1, source_target_pairs={{0,2},{1,3},{2,4},{3,5},{4,6},{5,7},{6,0},{7,1},{8,10},{9,11},{10,... | collective-permute-start | bytes 4718600 | tf_op jit(solution)/shard_map/ppermute | solution.py:189
  106.3 108.9 %collective-permute-start.19 = (bf16[768,1024]{1,0:T(8,128)(2,1)S(1)}, bf16[768,1024]{1,0:T(8,128)(2,1)S(1)}, u32[]{:S(2)}, u32[]{:S(2)}) collective-permute-start(bf16[768,1024]{1,0:T(8,128)(2,1)S(1)} %slice.190.refs_4_), channel_id=1, source_target_pairs={{0,16},{1,17},{2,18},{3,19},{4,20},{5,21},{6,22},{7,23},{8,24},{9,... | collective-permute-start | bytes 4718600 | tf_op jit(solution)/shard_map/ppermute | solution.py:189
  151.3 47.3 %collective-permute-start.17 = (bf16[256,1024]{1,0:T(8,128)(2,1)S(1)}, bf16[256,1024]{1,0:T(8,128)(2,1)S(1)}, u32[]{:S(2)}, u32[]{:S(2)}) collective-permute-start(bf16[256,1024]{1,0:T(8,128)(2,1)S(1)} %collective-permute-done.16.refs_9_.refs_17_), channel_id=1, source_target_pairs={{0,2},{1,3},{2,4},{3,5},{4,6},{5,7},{6,0},{7,1},{8,10},{9,11},{10,... | collective-permute-start | bytes 1572872 | tf_op jit(solution)/shard_map/ppermute | solution.py:189
  196.0 16.6 %collective-permute-start.14 = (bf16[256,1024]{1,0:T(8,128)(2,1)S(1)}, bf16[256,1024]{1,0:T(8,128)(2,1)S(1)}, u32[]{:S(2)}, u32[]{:S(2)}) collective-permute-start(bf16[256,1024]{1,0:T(8,128)(2,1)S(1)} %collective-permute-done.13.refs_6_.refs_10_), channel_id=1, source_target_pairs={{0,2},{1,3},{2,4},{3,5},{4,6},{5,7},{6,0},{7,1},{8,10},{9,11},{10,... | collective-permute-start | bytes 1572872 | tf_op jit(solution)/shard_map/ppermute | solution.py:189
  198.7 25.2 %collective-permute-start.18 = (bf16[256,1024]{1,0:T(8,128)(2,1)S(1)}, bf16[256,1024]{1,0:T(8,128)(2,1)S(1)}, u32[]{:S(2)}, u32[]{:S(2)}) collective-permute-start(bf16[256,1024]{1,0:T(8,128)(2,1)S(1)} %collective-permute-done.17.refs_10_.refs_18_), channel_id=1, source_target_pairs={{0,2},{1,3},{2,4},{3,5},{4,6},{5,7},{6,0},{7,1},{8,10},{9,11},{10,... | collective-permute-start | bytes 1572872 | tf_op jit(solution)/shard_map/ppermute | solution.py:189
  213.4 34.6 %collective-permute-start.20 = (bf16[768,1024]{1,0:T(8,128)(2,1)}, bf16[768,1024]{1,0:T(8,128)(2,1)}, u32[]{:S(2)}, u32[]{:S(2)}) collective-permute-start(bf16[768,1024]{1,0:T(8,128)(2,1)} %collective-permute-done.1.refs_5_), channel_id=1, source_target_pairs={{0,16},{1,17},{2,18},{3,19},{4,20},{5,21},{6,22},{7,23},{8,24},{9,... | collective-permute-start | bytes 4718600 | tf_op jit(solution)/shard_map/ppermute | solution.py:189
  215.2 41.5 %collective-permute-start.3 = (bf16[768,1024]{1,0:T(8,128)(2,1)}, bf16[768,1024]{1,0:T(8,128)(2,1)}, u32[]{:S(2)}, u32[]{:S(2)}) collective-permute-start(bf16[768,1024]{1,0:T(8,128)(2,1)} %collective-permute-done.2.refs_6_), channel_id=1, source_target_pairs={{0,2},{1,3},{2,4},{3,5},{4,6},{5,7},{6,0},{7,1},{8,10},{9,11},{10,... | collective-permute-start | bytes 4718600 | tf_op jit(solution)/shard_map/ppermute | solution.py:189
  216.4 50.6 %collective-permute-start.24 = (bf16[4096,256]{1,0:T(8,128)(2,1)}, bf16[4096,256]{1,0:T(8,128)(2,1)}, u32[]{:S(2)}, u32[]{:S(2)}) collective-permute-start(bf16[4096,256]{1,0:T(8,128)(2,1)} %collective-permute-done.23.refs_20_), channel_id=1, source_target_pairs={{0,1},{1,0},{2,3},{3,2},{4,5},{5,4},{6,7},{7,6},{8,9},{9,8},{10,11... | collective-permute-start | bytes 6291464 | tf_op jit(solution)/shard_map/ppermute | solution.py:189
  224.7 42.4 %collective-permute-start.10 = (bf16[4096,256]{1,0:T(8,128)(2,1)}, bf16[4096,256]{1,0:T(8,128)(2,1)}, u32[]{:S(2)}, u32[]{:S(2)}) collective-permute-start(bf16[4096,256]{1,0:T(8,128)(2,1)} %collective-permute-done.9.refs_8_.refs_18_.refs_14_), channel_id=1, source_target_pairs={{0,1},{1,0},{2,3},{3,2},{4,5},{5,4},{6,7},{7,6},{8,9},{9,8},{10,11... | collective-permute-start | bytes 6291464 | tf_op jit(solution)/shard_map/ppermute | solution.py:189
  248.1 44.7 %collective-permute-start.21 = (bf16[768,1024]{1,0:T(8,128)(2,1)}, bf16[768,1024]{1,0:T(8,128)(2,1)}, u32[]{:S(2)}, u32[]{:S(2)}) collective-permute-start(bf16[768,1024]{1,0:T(8,128)(2,1)} %collective-permute-done.2.refs_6_), channel_id=1, source_target_pairs={{0,16},{1,17},{2,18},{3,19},{4,20},{5,21},{6,22},{7,23},{8,24},{9,... | collective-permute-start | bytes 4718600 | tf_op jit(solution)/shard_map/ppermute | solution.py:189
  256.6 58.8 %collective-permute-start.22 = (bf16[768,1024]{1,0:T(8,128)(2,1)}, bf16[768,1024]{1,0:T(8,128)(2,1)}, u32[]{:S(2)}, u32[]{:S(2)}) collective-permute-start(bf16[768,1024]{1,0:T(8,128)(2,1)} %collective-permute-done.3.refs_7_), channel_id=1, source_target_pairs={{0,16},{1,17},{2,18},{3,19},{4,20},{5,21},{6,22},{7,23},{8,24},{9,... | collective-permute-start | bytes 4718600 | tf_op jit(solution)/shard_map/ppermute | solution.py:189
  267.0 64.9 %collective-permute-start.6 = (bf16[4096,256]{1,0:T(8,128)(2,1)}, bf16[4096,256]{1,0:T(8,128)(2,1)}, u32[]{:S(2)}, u32[]{:S(2)}) collective-permute-start(bf16[4096,256]{1,0:T(8,128)(2,1)} %copy-done.37), channel_id=1, source_target_pairs={{0,1},{1,0},{2,3},{3,2},{4,5},{5,4},{6,7},{7,6},{8,9},{9,8},{10,11... | collective-permute-start | bytes 6291464 | tf_op jit(solution)/shard_map/ppermute | solution.py:189
  267.1 64.8 %collective-permute-start.8 = (bf16[4096,256]{1,0:T(8,128)(2,1)}, bf16[4096,256]{1,0:T(8,128)(2,1)}, u32[]{:S(2)}, u32[]{:S(2)}) collective-permute-start(bf16[4096,256]{1,0:T(8,128)(2,1)} %collective-permute-done.7.refs_12_.refs_16_), channel_id=1, source_target_pairs={{0,1},{1,0},{2,3},{3,2},{4,5},{5,4},{6,7},{7,6},{8,9},{9,8},{10,11... | collective-permute-start | bytes 6291464 | tf_op jit(solution)/shard_map/ppermute | solution.py:189
  (41 other events, 1688.3 us)

commit v2 on v1

v2 whole, which is shorter than its diff:
```python
import functools
import jax
import jax.numpy as jnp
from jax import lax
from jax.experimental import pallas as pl
from jax.experimental.pallas import tpu as pltpu
from jax.sharding import PartitionSpec as P


def stats_kernel(tiles, n_pieces, n_heads, *refs):
    kofs, colbase, side_ref = refs[:3]
    pieces = refs[3 : 3 + n_pieces]
    heads = refs[3 + n_pieces : 3 + n_pieces + n_heads]
    out_ref, x_scr, h_scr, f_scr, t_scr, m_scr, s_scr, w_scr, p_scr, x_sem, h_sem = refs[
        3 + n_pieces + n_heads :
    ]
    step = pl.program_id(0)
    n_tiles, width = len(tiles), h_scr.shape[3]
    firsts = [0]
    for _, columns in tiles:
        firsts.append(firsts[-1] + sum(g[2] for g in columns))
    slot = lax.rem(step, 2)

    def depth_at(j, size):
        return pl.multiple_of(kofs[j], 128) if j >= 0 else (-1 - j) * size

    def row_copies(k):
        return [
            pltpu.make_async_copy(
                pieces[a].at[pl.ds(src, rows)],
                x_scr.at[k % 2, pl.ds(dst, rows), pl.ds(depth_at(j, pieces[a].shape[1]), pieces[a].shape[1])],
                x_sem.at[k % 2],
            )
            for a, j, src, rows, dst in tiles[k][0]
        ]

    def head_copies(parts, block, slot):
        return [
            pltpu.make_async_copy(
                heads[k].at[:, pl.ds(pl.multiple_of(block * width, width), width)],
                h_scr.at[slot, which, pl.ds(n * heads[k].shape[0], heads[k].shape[0])],
                h_sem.at[slot],
            )
            for which in range(2)
            for n, k in enumerate(parts[which])
        ]

    def start_head(at, slot):
        first = 0
        for _, columns in tiles:
            for one, two, blocks in columns:
                @pl.when((at >= first) & (at < first + blocks))
                def _(parts=(one, two), first=first):
                    for copy in head_copies(parts, at - first, slot):
                        copy.start()
                first += blocks

    @pl.when(step == 0)
    def _():
        for copy in row_copies(0):
            copy.start()
        start_head(0, 0)

    for k in range(n_tiles):
        @pl.when(step == firsts[k])
        def _(k=k):
            if k + 1 < n_tiles:
                for copy in row_copies(k + 1):
                    copy.start()
            rows = x_scr.shape[1]
            f_scr[...] = jnp.broadcast_to(side_ref[0:1, :], (128, rows)).T
            lane = lax.broadcasted_iota(jnp.int32, (rows, 128), 1)
            t_scr[...] = jnp.broadcast_to(side_ref[1:2, :], (128, rows)).T.astype(jnp.int32) - lane
            m_scr[...] = jnp.full(m_scr.shape, -jnp.inf, jnp.float32)
            s_scr[...] = jnp.zeros(s_scr.shape, jnp.float32)
            w_scr[...] = jnp.zeros(w_scr.shape, jnp.float32)
            p_scr[...] = jnp.zeros(p_scr.shape, jnp.float32)
            for copy in row_copies(k):
                copy.wait()

    @pl.when(step + 1 < firsts[-1])
    def _():
        start_head(step + 1, lax.rem(step + 1, 2))

    for copy in head_copies(tiles[0][1][0], 0, slot):
        copy.wait()

    held = sum(((step >= f).astype(jnp.int32) for f in firsts[1:-1]), jnp.int32(0))
    rows, sub = x_scr.shape[1], 64

    for which in range(2):
        raw = jnp.dot(x_scr[lax.rem(held, 2)], h_scr[slot, which], preferred_element_type=jnp.float32)
        base = colbase[step * 2 + which]
        for at in range(0, rows, sub):
            here = pl.ds(at, sub)
            scale = f_scr[here, :]
            wanted = t_scr[here, :] - base
            parts = [raw[at : at + sub, c : c + 128] * scale for c in range(0, width, 128)]
            old = m_scr[here, :]
            new = functools.reduce(jnp.maximum, parts, old)
            fade = jnp.exp(old - new)
            total, moment, picked = s_scr[here, :] * fade, w_scr[here, :] * fade, p_scr[here, :]
            for c, part in enumerate(parts):
                weight = jnp.exp(part - new)
                total += weight
                moment += weight * part
                picked = jnp.where(wanted == c * 128, part, picked)
            m_scr[here, :], s_scr[here, :], w_scr[here, :], p_scr[here, :] = new, total, moment, picked

    for last in firsts[1:]:
        @pl.when(step == last - 1)
        def _():
            peak_t = m_scr[...].T
            peak = jnp.max(peak_t, axis=0, keepdims=True)
            fade = jnp.exp(peak_t - peak)
            out_ref[0:1, :] = peak
            out_ref[1:2, :] = jnp.sum(s_scr[...].T * fade, axis=0, keepdims=True)
            out_ref[2:3, :] = jnp.sum(w_scr[...].T * fade, axis=0, keepdims=True)
            out_ref[3:4, :] = jnp.sum(p_scr[...].T, axis=0, keepdims=True)


def stats(tiles, rows, width, kofs, colbase, side, pieces, heads):
    n_tiles = len(tiles)
    counts = [sum(g[2] for g in columns) for _, columns in tiles]
    firsts = [sum(counts[:k]) for k in range(1, n_tiles)]
    n_steps, depth = sum(counts), heads[0].shape[0]

    def block(step):
        return 0, sum(((step >= f).astype(jnp.int32) for f in firsts), jnp.int32(0))

    return pl.pallas_call(
        functools.partial(stats_kernel, tiles, len(pieces), len(heads)),
        grid=(n_steps,),
        in_specs=[pl.BlockSpec(memory_space=pltpu.SMEM)] * 2
        + [pl.BlockSpec((2, rows), block)]
        + [pl.BlockSpec(memory_space=pl.ANY)] * (len(pieces) + len(heads)),
        out_specs=pl.BlockSpec((4, rows), block),
        out_shape=jax.ShapeDtypeStruct((4, n_tiles * rows), jnp.float32),
        scratch_shapes=[
            pltpu.VMEM((min(n_tiles, 2), rows, depth), jnp.bfloat16),
            pltpu.VMEM((2, 2, depth, width), jnp.bfloat16),
        ]
        + [pltpu.VMEM((rows, 128), jnp.float32), pltpu.VMEM((rows, 128), jnp.int32)]
        + [pltpu.VMEM((rows, 128), jnp.float32)] * 4
        + [pltpu.SemaphoreType.DMA((min(n_tiles, 2),)), pltpu.SemaphoreType.DMA((2,))],
        compiler_params=pltpu.CompilerParams(
            dimension_semantics=("arbitrary",), vmem_limit_bytes=48 * 1024 * 1024
        ),
        cost_estimate=pl.CostEstimate(flops=1 << 20, bytes_accessed=1 << 10, transcendentals=0),
    )(kofs, colbase, side, *pieces, *heads)


EPS = 1e-05
SHRINK = 2.0**-9


def merge(stats):
    peak, total, moment, picked = (stats[:, k] for k in range(4))
    best = jnp.max(peak, axis=0)
    fade = jnp.exp(peak - best[None])
    return jnp.stack(
        [best, jnp.sum(total * fade, axis=0), jnp.sum(moment * fade, axis=0), jnp.sum(picked, axis=0)]
    )


def shards(hidden, gain, head, targets, lengths):
    n_req, n_vocab = lax.axis_size("req"), lax.axis_size("vocab")
    q, v = lax.axis_index("req"), lax.axis_index("vocab")
    spots = n_vocab // 2
    s, c = v // 2, v % 2
    rows, feats = hidden.shape
    depth, cols = head.shape
    blk, half = rows // n_vocab, rows // 2
    cut = half - blk
    every = ("req", "vocab")

    def move(x, where):
        pairs = [
            (a * n_vocab + b, where(a, b)) for a in range(n_req) for b in range(n_vocab)
        ]
        return lax.ppermute(x, every, pairs)

    def to_core(x):
        return move(x, lambda a, b: a * n_vocab + (b ^ 1))

    def to_x(x):
        return move(x, lambda a, b: (a ^ 1) * n_vocab + b)

    def to_y(x):
        return move(x, lambda a, b: (a ^ 2) * n_vocab + b)

    def to_z(x, by):
        return move(x, lambda a, b: a * n_vocab + (b + 2 * by) % n_vocab)

    n_far = 4 if cols % 512 == 0 else 1
    far_cols = cols // n_far
    width = min(256, far_cols)

    values = hidden.astype(jnp.float32)
    own_gain = lax.dynamic_slice_in_dim(gain, v * feats, feats) * SHRINK
    scaled = (values * own_gain[None, :]).astype(jnp.bfloat16).reshape(spots, 2, blk, feats)
    square = jnp.sum(values * values, axis=1).reshape(spots, 2, blk)

    def mine(x, core):
        x = lax.dynamic_index_in_dim(x, core, 1, keepdims=False)
        return x.reshape(half, *x.shape[2:])

    token = [None]

    def after(x):
        return x if token[0] is None else lax.optimization_barrier((x, token[0]))[0]

    def step_ends(*results):
        one = results[0][:1, :1].astype(jnp.float32) if token[0] is None else token[0]
        token[0] = lax.optimization_barrier((one, *results))[0]

    def far_part(k):
        return after(head)[:, k * far_cols : (k + 1) * far_cols]

    far = [to_x(far_part(0))]
    other = to_core(mine(scaled, 1 - c))
    other_square = to_core(mine(square, 1 - c).reshape(1, half))
    square_sum = other_square + mine(square, c).reshape(1, half)
    one = mine(scaled, c)
    piece = jnp.where(
        c == 0, jnp.concatenate([one, other], axis=1), jnp.concatenate([other, one], axis=1)
    )
    n_a = half // 2
    a, b = {0: (piece, 0)}, {0: (piece, n_a)}
    ya, yb, far_near = {}, {}, []
    step_ends(other, other_square)
    near = to_core(after(head))

    trip = [0] + [j for k in range(1, spots // 2 + 1) for j in dict.fromkeys((k, spots - k))]
    z_list = [(ring, j) for ring in (a, b) for j in trip[1:]]
    y_list = [(a, ya, 0), (b, yb, 0)] + [(ring, out, j) for ring, out in ((a, ya), (b, yb)) for j in trip[1:]]
    stage = max(1, len(y_list) // 4)
    doubled = 0
    side = y_side = None
    kofs = (s + spots - jnp.arange(spots, dtype=jnp.int32)) % spots * (2 * feats)

    def group(g):
        if g == 0:
            return head, near, (q * n_vocab + v) * cols, (q * n_vocab + (v ^ 1)) * cols
        at = (g - 1) * far_cols
        return (
            far[g - 1],
            far_near[g - 1],
            ((q ^ 1) * n_vocab + v) * cols + at,
            ((q ^ 1) * n_vocab + (v ^ 1)) * cols + at,
        )

    def call(*wanted):
        tiles, arrays, heads, sides, bases, places = [], [], [], [], [], {}
        for name, chosen in wanted:
            ring = {"A": a, "B": b, "E": ya, "F": yb}[name]
            at = n_a if name in "BF" else 0
            sides.append((side if name in "AB" else y_side)[:, at : at + n_a])
            rows = []
            for j in trip:
                key = next((k for k, x in enumerate(arrays) if x is ring[j][0]), len(arrays))
                places[name, j] = key
                if key == len(arrays):
                    arrays.append(ring[j][0])
                rows.append((places[name, j], j, ring[j][1], n_a, 0))
            columns = []
            for g in chosen:
                one, two, base, pair = group(g)
                for key, array in ((("h", g, 0), one), (("h", g, 1), two)):
                    places.setdefault(key, len(heads))
                    if places[key] == len(heads):
                        heads.append(array)
                blocks = one.shape[1] // width
                columns.append(([places["h", g, 0]], [places["h", g, 1]], blocks))
                for k in range(blocks):
                    bases += [base + k * width, pair + k * width]
            tiles.append((rows, columns))
        out = stats(
            tiles,
            n_a,
            width,
            kofs,
            jnp.stack(bases).astype(jnp.int32),
            after(jnp.concatenate(sides, axis=1)),
            arrays,
            heads,
        )
        for k, (name, _) in enumerate(wanted):
            outs[name].append(out[:, k * n_a : (k + 1) * n_a])
        return out

    outs = {name: [] for name in "ABEF"}
    n_steps = 4
    tiny = square_sum
    for step in range(n_steps):
        ends = []
        if 1 <= step and step + 1 < n_far:
            far.append(to_x(far_part(step + 1)))
        if step and step <= n_far:
            far_near.append(to_core(after(far[step - 1])))
        for n in range(len(z_list) if step == n_steps - 2 else min(stage, len(z_list))):
            ring, j = z_list.pop(0)
            by = 1 if j <= spots // 2 else -1
            array, at = ring[(j - by) % spots]
            array = after(array[at : at + n_a])
            if step == 0 and n == 1:
                array = lax.optimization_barrier((array, near))[0]
            ring[j] = (to_z(array, by), 0)
            ends.append(ring[j][0])
            if step == 0 and n == 0 and n_far > 1:
                block = lax.optimization_barrier((head, ends[0]))[0]
                far.append(to_x(block[:, far_cols : 2 * far_cols]))
        batch = [y_list.pop(0) for _ in range(len(y_list) if step == n_steps - 1 else min(stage, len(y_list)))]
        cuts = [[y for y in batch if y[0] is a], [y for y in batch if y[0] is b]] if step == 2 else [batch]
        for part in cuts:
            arrays = [ring[j][0][ring[j][1] : ring[j][1] + n_a] for ring, _, j in part]
            sent = to_y(after(piece if step == 0 and len(part) == 2 else jnp.concatenate(arrays)))
            for n, (_, out, j) in enumerate(part):
                out[j] = (sent, n * n_a)
            ends.append(sent)
        for _ in range(1 if spots == 4 else 5):
            if 2**doubled < spots:
                sent = to_z(after(tiny), 2**doubled)
                tiny = tiny + sent
                doubled += 1
                ends.append(sent)
        if step == 2:
            scale = lax.rsqrt(tiny / depth + EPS) * (1.0 / SHRINK)
            wanted = mine(targets.astype(jnp.float32).reshape(spots, 2, blk), c).reshape(1, half)
            side = jnp.concatenate([scale, wanted])
            y_side = to_y(after(side))
            ends.append(y_side)
        if step == 2:
            many = n_far > 1
            first = call(("A", [0, 1, 2] if many else [0]))
            y_side = lax.optimization_barrier((y_side, first))[0]
            ends.append(call(("E", [0, 1] if many else [0])))
        if step == 3:
            more = [("E", [2, 3]), ("A", [3])] if many else []
            ends.append(call(("B", [0, 1, 2, 3] if many else [0]), *more))
        ends.append(far[min(step, n_far - 1)])
        if step == 0:
            ends.append(near)
        step_ends(*ends)
    if n_far > 3:
        far_near.append(to_core(after(far[3])))
    call(("F", list(range(n_far + 1))), ("A", [n_far]), ("B", [n_far]), ("E", [n_far]))
    own = jnp.concatenate([merge(jnp.stack(outs["A"])), merge(jnp.stack(outs["B"]))], axis=1)
    peer = jnp.concatenate([merge(jnp.stack(outs["E"])), outs["F"][0]], axis=1)

    first = q // 2 == 0
    whole = jnp.stack([jnp.where(first, own, peer), jnp.where(first, peer, own)])
    whole = whole.reshape(2, 4, spots, blk).transpose(0, 2, 1, 3).reshape(2 * spots, 4 * blk)
    kin = [
        [(2 * a + b) * n_vocab + 2 * k + core for a in range(2) for k in range(spots)]
        for b in range(2)
        for core in range(2)
    ]
    whole = lax.all_to_all(
        whole, every, split_axis=0, concat_axis=0, axis_index_groups=kin, tiled=True
    )
    peak, total, moment, picked = merge(whole.reshape(2 * spots, 4, blk))
    log_total = peak + jnp.log(total)
    lp, ent = picked - log_total, log_total - moment / total

    seq_lens = lengths[0, :-1]
    stops = jnp.cumsum(seq_lens)
    starts = stops - seq_lens
    local = v * blk + jnp.arange(blk, dtype=jnp.int32)
    valid = local < stops[-1]
    lp = jnp.where(valid, lp, 0.0)
    ent = jnp.where(valid, ent, 0.0)
    member = (local[None, :] >= starts[:, None]) & (local[None, :] < stops[:, None])
    sums = jnp.sum(jnp.where(member[None], jnp.stack([lp, ent])[:, None, :], 0.0), axis=2)
    sums = jnp.sum(
        lax.all_to_all(
            jnp.broadcast_to(sums.reshape(1, -1), (n_vocab, sums.size)),
            "vocab",
            split_axis=0,
            concat_axis=0,
            tiled=True,
        ),
        axis=0,
    ).reshape(sums.shape)
    means = sums / seq_lens.astype(jnp.float32)[None]
    return (lp, ent, means[0], means[1])


def solution(mesh):
    in_specs = (P("req", "vocab"), P(), P(None, ("req", "vocab")), P("req"), P("req", None))
    out_specs = (P(("req", "vocab")), P(("req", "vocab")), P("req"), P("req"))
    return jax.shard_map(shards, mesh=mesh, in_specs=in_specs, out_specs=out_specs, check_vma=False)
```

time: 439 us -> 290 us (0.66)
  waiting for transfers between devices: 216 us -> 111 us
  blocking collectives: 31 us -> 7.91 us
  local copies, waits for them, and re-layouts: 39.9 us -> 19.5 us
  starting transfers between devices: 26.3 us -> 31.2 us
    ppermute x25, waiting for transfers between devices: 210 us -> 105 us  [move(): return lax.ppermute(x, every, pairs)]
    psum x1 -> x0, blocking collectives: 23.1 us -> none  [shards(): square = lax.psum(jnp.sum(values * values, axis=1), 'vocab')]
    reshape x12 -> x2, local copies, waits for them, and re-layouts: 14.4 us -> 0.02 us  [the longest x1 0.01 us: shards(): targets.astype(jnp.float32).reshape(spots, 2, blk)]
    ppermute x25, starting transfers between devices: 22.7 us -> 27.9 us  [move(): return lax.ppermute(x, every, pairs)]
    unnamed x78 -> x36, local copies, waits for them, and re-layouts: 9.02 us -> 5.69 us
    pallas_call x5 -> x4, Pallas kernels: 109 us -> 107 us  [stats(): pl.pallas_call(functools.partial(stats_kernel, tiles, len(pieces), len(he...]
    slice x12 -> x6, local copies, waits for them, and re-layouts: 12.6 us -> 11.2 us  [the longest x3 9.26 us: far_part(): return after(head)[:, k * far_cols:(k + 1) * far_cols]]
  transfers between devices with their start and end apart: 26 -> 26, of which waited for: 14 -> 14; matrix products, arithmetic and copies ran while one was open for 8% -> 6% of each run, Pallas kernels for 6% -> 24%
where the time goes in v2:
time: 290 us
  waiting for transfers between devices  111 us (38%)
  Pallas kernels  107 us (37%)
  starting transfers between devices  31.2 us (11%)
  local copies, waits for them, and re-layouts  19.5 us (7%)
  other arithmetic  11.4 us (4%)
  blocking collectives  7.91 us (3%)
    pallas_call x4, Pallas kernels, stats(): pl.pallas_call(functools.partial(stats_kernel, tiles, len(pieces), len(he...  107 us
    ppermute x25, waiting for transfers between devices, move(): return lax.ppermute(x, every, pairs)  105 us
    ppermute x25, starting transfers between devices, move(): return lax.ppermute(x, every, pairs)  27.9 us
    slice x3, local copies, waits for them, and re-layouts, far_part(): return after(head)[:, k * far_cols:(k + 1) * far_cols]  9.26 us
    all_to_all x1, blocking collectives, shards(): lax.all_to_all(jnp.broadcast_to(sums.reshape(1, -1), (n_vocab, sums.size)...  7.91 us
    all_to_all x1, waiting for transfers between devices, shards(): lax.all_to_all(whole, every, split_axis=0, concat_axis=0, axis_index_grou...  6.01 us
  transfers between devices with their start and end apart: 26, of which 14 were waited for; matrix products, arithmetic and copies ran while one was open for 6% of the time, Pallas kernels for 24%

profile of v2, /device:TPU:0, one launch (start us, length us, event | category | flops | bytes accessed | tf_op | source)
XLA Modules:
  0.0 289.6 jit_solution(9714653404841067186)
XLA Ops:
  1.4 2.3 fusion.1
  4.5 2.1 collective-permute-done.1
  7.0 3.0 %slice.127 = bf16[4096,256]{1,0:T(8,128)(2,1)} slice(bf16[4096,1024]{1,0:T(8,128)(2,1)} %refs_15_.1), slice={[0:4096], [0:256]} | slice | bytes 4194304 | tf_op jit(solution)/shard_map/slice | solution.py:218
  10.1 2.9 collective-permute-start.7
  13.0 2.3 maximum_select_fusion.refs_3_.refs_6_
  20.2 5.0 %collective-permute-start.5 = (bf16[512,1024]{1,0:T(8,128)(2,1)S(1)}, bf16[512,1024]{1,0:T(8,128)(2,1)S(1)}, u32[]{:S(2)}, u32[]{:S(2)}) collective-permute-start(bf16[512,1024]{1,0:T(8,128)(2,1)S(1)} %get-tuple-element.39), channel_id=1, source_target_pairs={{0,6},{1,7},{2,0},{3,1},{4,2},{5,3},{6,4},{7,5},{8,14},{9,15},{10,... | collective-permute-start | bytes 3145736 | tf_op jit(solution)/shard_map/ppermute | solution.py:181
  25.1 19.8 %collective-permute-done.3.refs_4_.refs_10_.refs_7_ = bf16[512,1024]{1,0:T(8,128)(2,1)S(1)} collective-permute-done((bf16[512,1024]{1,0:T(8,128)(2,1)S(1)}, bf16[512,1024]{1,0:T(8,128)(2,1)S(1)}, u32[]{:S(2)}, u32[]{:S(2)}) %collective-permute-start.3) | collective-permute-done | bytes 1048608 | tf_op jit(solution)/shard_map/ppermute | solution.py:181
  47.3 18.8 %collective-permute-done.5.refs_5_.refs_11_.refs_8_ = bf16[512,1024]{1,0:T(8,128)(2,1)S(1)} collective-permute-done((bf16[512,1024]{1,0:T(8,128)(2,1)S(1)}, bf16[512,1024]{1,0:T(8,128)(2,1)S(1)}, u32[]{:S(2)}, u32[]{:S(2)}) %collective-permute-start.5) | collective-permute-done | bytes 1048608 | tf_op jit(solution)/shard_map/ppermute | solution.py:181
  68.2 3.1 %collective-permute-start.9 = (bf16[512,1024]{1,0:T(8,128)(2,1)S(1)}, bf16[512,1024]{1,0:T(8,128)(2,1)S(1)}, u32[]{:S(2)}, u32[]{:S(2)}) collective-permute-start(bf16[512,1024]{1,0:T(8,128)(2,1)S(1)} %collective-permute-done.3.refs_4_.refs_10_.refs_7_), channel_id=1, source_target_pairs={{0,2},{1,3},{2,4},{3,5},{4,6},{5,7},{6,0},{7,1},{8,10},{9,11},{10,... | collective-permute-start | bytes 3145736 | tf_op jit(solution)/shard_map/ppermute | solution.py:181
  72.4 31.7 %collective-permute-done.12.refs_11_.refs_17_.refs_19_ = bf16[4096,256]{1,0:T(8,128)(2,1)} collective-permute-done((bf16[4096,256]{1,0:T(8,128)(2,1)S(1)}, bf16[4096,256]{1,0:T(8,128)(2,1)}, u32[]{:S(2)}, u32[]{:S(2)}) %collective-permute-start.12) | collective-permute-done | bytes 2097184 | tf_op jit(solution)/shard_map/ppermute | solution.py:181
  104.1 9.1 %collective-permute-done.8 = f32[1,1024]{1,0:T(1,128)S(1)} collective-permute-done((f32[1,1024]{1,0:T(1,128)S(1)}, f32[1,1024]{1,0:T(1,128)S(1)}, u32[]{:S(2)}, u32[]{:S(2)}) %collective-permute-start.8) | collective-permute-done | bytes 4128 | tf_op jit(solution)/shard_map/ppermute | solution.py:181
  113.2 3.8 %collective-permute-done.9.refs_6_.refs_12_.refs_9_ = bf16[512,1024]{1,0:T(8,128)(2,1)S(1)} collective-permute-done((bf16[512,1024]{1,0:T(8,128)(2,1)S(1)}, bf16[512,1024]{1,0:T(8,128)(2,1)S(1)}, u32[]{:S(2)}, u32[]{:S(2)}) %collective-permute-start.9) | collective-permute-done | bytes 1048608 | tf_op jit(solution)/shard_map/ppermute | solution.py:181
  119.3 3.0 %slice.133 = bf16[4096,256]{1,0:T(8,128)(2,1)} slice(bf16[4096,1024]{1,0:T(8,128)(2,1)} %refs_15_.1), slice={[0:4096], [512:768]} | slice | bytes 4194304 | tf_op jit(solution)/shard_map/slice | solution.py:218
  130.6 3.2 %slice.136 = bf16[4096,256]{1,0:T(8,128)(2,1)} slice(bf16[4096,1024]{1,0:T(8,128)(2,1)} %refs_15_.1), slice={[0:4096], [768:1024]} | slice | bytes 4194304 | tf_op jit(solution)/shard_map/slice | solution.py:218
  133.8 19.9 %shard_map.84 = f32[4,512]{1,0:T(4,128)S(1)} custom-call(s32[4]{0:T(128)S(1)} %fusion.29.refs_0_, s32[12]{0:T(128)S(1)} %stack.208.refs_1_, f32[2,512]{1,0:T(2,128)S(1)} %get-tuple-element.48.refs_2_, bf16[1024,1024]{1,0:T(8,128)(2,1)S(1)} %maximum_select_fusion.refs_3_.refs_6_, bf16[512,1024]{1,0:T(8,128)(2,1)S(1)} %collective-permute-done.3.refs_4_.refs_10_.refs_7_, ...), custom_call_target="tpu_custom_call" | custom-call | flops 1048576 | bytes 1024 | tf_op jit(solution)/shard_map/pallas_call | solution.py:131
  155.4 17.4 %shard_map.85 = f32[4,512]{1,0:T(4,128)S(1)} custom-call(s32[4]{0:T(128)S(1)} %fusion.29.refs_0_, s32[10]{0:T(128)S(1)} %stack.213.refs_1_, f32[2,512]{1,0:T(2,128)S(1)} %get-tuple-element.56.refs_2_, bf16[1024,1024]{1,0:T(8,128)(2,1)S(1)} %copy-done.2, bf16[1024,1024]{1,0:T(8,128)(2,1)S(1)} %copy-done.4, ...), custom_call_target="tpu_custom_call" | custom-call | flops 1048576 | bytes 1024 | tf_op jit(solution)/shard_map/pallas_call | solution.py:131
  174.3 3.0 %pad_maximum_fusion.1 = bf16[1024,1024]{1,0:T(8,128)(2,1)} fusion(bf16[512,1024]{1,0:T(8,128)(2,1)} %collective-permute-done.17.refs_6_.refs_12_, bf16[512,1024]{1,0:T(8,128)(2,1)} %collective-permute-done.16.refs_5_.refs_11_), kind=kLoop, calls=%fused_computation.6 | loop fusion | flops 4194304 | bytes 4194304 | tf_op jit(solution)/shard_map/concatenate | solution.py:317
  180.3 33.6 %shard_map.86 = f32[4,1536]{1,0:T(4,128)S(1)} custom-call(s32[4]{0:T(128)S(1)} %fusion.29.refs_0_, s32[20]{0:T(128)S(1)} %stack.212.refs_1_, f32[2,1536]{1,0:T(2,128)S(1)} %pad_maximum_fusion.6.refs_2_, bf16[1024,1024]{1,0:T(8,128)(2,1)} %copy-done, bf16[512,1024]{1,0:T(8,128)(2,1)S(1)} %copy-done.12, ...), custom_call_target="tpu_custom_call" | custom-call | flops 1048576 | bytes 1024 | tf_op jit(solution)/shard_map/pallas_call | solution.py:131
  215.6 10.1 %collective-permute-done.22.refs_5_ = bf16[1024,1024]{1,0:T(8,128)(2,1)} collective-permute-done((bf16[1024,1024]{1,0:T(8,128)(2,1)}, bf16[1024,1024]{1,0:T(8,128)(2,1)}, u32[]{:S(2)}, u32[]{:S(2)}) %collective-permute-start.22) | collective-permute-done | bytes 2097184 | tf_op jit(solution)/shard_map/ppermute | solution.py:181
  226.1 4.2 %collective-permute-done.24.refs_24_ = bf16[4096,256]{1,0:T(8,128)(2,1)} collective-permute-done((bf16[4096,256]{1,0:T(8,128)(2,1)}, bf16[4096,256]{1,0:T(8,128)(2,1)}, u32[]{:S(2)}, u32[]{:S(2)}) %collective-permute-start.24) | collective-permute-done | bytes 2097184 | tf_op jit(solution)/shard_map/ppermute | solution.py:181
  231.5 36.2 %shard_map.87 = f32[4,2048]{1,0:T(4,128)S(1)} custom-call(s32[4]{0:T(128)S(1)} %fusion.29.refs_0_, s32[22]{0:T(128)S(1)} %stack.217.refs_1_, f32[2,2048]{1,0:T(2,128)S(1)} %pad_maximum_fusion.4.refs_2_, bf16[1024,1024]{1,0:T(8,128)(2,1)} %copy-done.1, bf16[512,1024]{1,0:T(8,128)(2,1)} %collective-permute-done.19.refs_4_, ...), custom_call_target="tpu_custom_call" | custom-call | flops 1048576 | bytes 1024 | tf_op jit(solution)/shard_map/pallas_call | solution.py:131
  268.7 3.3 %all-to-all-start = ((f32[8,1,1024]{2,1,0:T(1,128)}), f32[8,1,1024]{2,1,0:T(1,128)S(1)}, u32[]{:S(2)}, u32[]{:S(2)}) async-start(f32[8,1,1024]{2,1,0:T(1,128)} %all_to_all.13), calls=%async_computation | async-start | bytes 65536 | tf_op jit(solution)/shard_map/all_to_all | solution.py:359
  272.7 6.0 %all-to-all-done = f32[8,1,1024]{2,1,0:T(1,128)S(1)} async-done(((f32[8,1,1024]{2,1,0:T(1,128)}), f32[8,1,1024]{2,1,0:T(1,128)S(1)}, u32[]{:S(2)}, u32[]{:S(2)}) %all-to-all-start) | async-done | bytes 32800 | tf_op jit(solution)/shard_map/all_to_all | solution.py:359
  281.1 7.9 %all_to_all.16 = f32[8,1,6]{2,1,0:T(1,128)S(1)} all-to-all(f32[8,1,6]{2,1,0:T(1,128)S(1)} %broadcast_in_dim.60), channel_id=1, replica_groups=mesh['req'=4,'vocab'=8] {'vocab'}, dimensions={0} | all-to-all | bytes 384 | tf_op jit(solution)/shard_map/all_to_all | solution.py:376
  (133 shorter events, 36.9 us)
Async XLA Ops:
  6.7 13.5 %collective-permute-start.4 = (bf16[4096,1024]{1,0:T(8,128)(2,1)}, bf16[4096,1024]{1,0:T(8,128)(2,1)}, u32[]{:S(2)}, u32[]{:S(2)}) collective-permute-start(bf16[4096,1024]{1,0:T(8,128)(2,1)} %refs_15_.1), channel_id=1, source_target_pairs={{0,1},{1,0},{2,3},{3,2},{4,5},{5,4},{6,7},{7,6},{8,9},{9,8},{10,11... | collective-permute-start | bytes 25165832 | tf_op jit(solution)/shard_map/ppermute | solution.py:181
  10.1 57.0 %collective-permute-start.7 = (bf16[4096,256]{1,0:T(8,128)(2,1)}, bf16[4096,256]{1,0:T(8,128)(2,1)}, u32[]{:S(2)}, u32[]{:S(2)}) collective-permute-start(bf16[4096,256]{1,0:T(8,128)(2,1)} %slice.127), channel_id=1, source_target_pairs={{0,8},{1,9},{2,10},{3,11},{4,12},{5,13},{6,14},{7,15},{8,0},{9,1},... | collective-permute-start | bytes 6291464 | tf_op jit(solution)/shard_map/ppermute | solution.py:181
  15.2 51.8 %collective-permute-start.6 = (bf16[1024,1024]{1,0:T(8,128)(2,1)S(1)}, bf16[1024,1024]{1,0:T(8,128)(2,1)S(1)}, u32[]{:S(2)}, u32[]{:S(2)}) collective-permute-start(bf16[1024,1024]{1,0:T(8,128)(2,1)S(1)} %maximum_select_fusion.refs_3_.refs_6_), channel_id=1, source_target_pairs={{0,16},{1,17},{2,18},{3,19},{4,20},{5,21},{6,22},{7,23},{8,24},{9,... | collective-permute-start | bytes 6291464 | tf_op jit(solution)/shard_map/ppermute | solution.py:181
  17.0 28.0 %collective-permute-start.3 = (bf16[512,1024]{1,0:T(8,128)(2,1)S(1)}, bf16[512,1024]{1,0:T(8,128)(2,1)S(1)}, u32[]{:S(2)}, u32[]{:S(2)}) collective-permute-start(bf16[512,1024]{1,0:T(8,128)(2,1)S(1)} %get-tuple-element.39), channel_id=1, source_target_pairs={{0,2},{1,3},{2,4},{3,5},{4,6},{5,7},{6,0},{7,1},{8,10},{9,11},{10,... | collective-permute-start | bytes 3145736 | tf_op jit(solution)/shard_map/ppermute | solution.py:181
  20.2 45.9 %collective-permute-start.5 = (bf16[512,1024]{1,0:T(8,128)(2,1)S(1)}, bf16[512,1024]{1,0:T(8,128)(2,1)S(1)}, u32[]{:S(2)}, u32[]{:S(2)}) collective-permute-start(bf16[512,1024]{1,0:T(8,128)(2,1)S(1)} %get-tuple-element.39), channel_id=1, source_target_pairs={{0,6},{1,7},{2,0},{3,1},{4,2},{5,3},{6,4},{7,5},{8,14},{9,15},{10,... | collective-permute-start | bytes 3145736 | tf_op jit(solution)/shard_map/ppermute | solution.py:181
  25.1 41.9 %collective-permute-start.2 = (f32[1,1024]{1,0:T(1,128)S(1)}, f32[1,1024]{1,0:T(1,128)S(1)}, u32[]{:S(2)}, u32[]{:S(2)}) collective-permute-start(f32[1,1024]{1,0:T(1,128)S(1)} %add.223), channel_id=1, source_target_pairs={{0,2},{1,3},{2,4},{3,5},{4,6},{5,7},{6,0},{7,1},{8,10},{9,11},{10,... | collective-permute-start | bytes 12296 | tf_op jit(solution)/shard_map/ppermute | solution.py:181
  46.7 57.4 %collective-permute-start.12 = (bf16[4096,256]{1,0:T(8,128)(2,1)S(1)}, bf16[4096,256]{1,0:T(8,128)(2,1)}, u32[]{:S(2)}, u32[]{:S(2)}) collective-permute-start(bf16[4096,256]{1,0:T(8,128)(2,1)S(1)} %slice.130), channel_id=1, source_target_pairs={{0,8},{1,9},{2,10},{3,11},{4,12},{5,13},{6,14},{7,15},{8,0},{9,1},... | collective-permute-start | bytes 6291464 | tf_op jit(solution)/shard_map/ppermute | solution.py:181
  67.1 49.9 %collective-permute-start.11 = (bf16[1024,1024]{1,0:T(8,128)(2,1)S(1)}, bf16[1024,1024]{1,0:T(8,128)(2,1)S(1)}, u32[]{:S(2)}, u32[]{:S(2)}) collective-permute-start(bf16[1024,1024]{1,0:T(8,128)(2,1)S(1)} %pad_maximum_fusion), channel_id=1, source_target_pairs={{0,16},{1,17},{2,18},{3,19},{4,20},{5,21},{6,22},{7,23},{8,24},{9,... | collective-permute-start | bytes 6291464 | tf_op jit(solution)/shard_map/ppermute | solution.py:181
  67.7 45.6 %collective-permute-start.10 = (bf16[512,1024]{1,0:T(8,128)(2,1)S(1)}, bf16[512,1024]{1,0:T(8,128)(2,1)S(1)}, u32[]{:S(2)}, u32[]{:S(2)}) collective-permute-start(bf16[512,1024]{1,0:T(8,128)(2,1)S(1)} %get-tuple-element.53), channel_id=1, source_target_pairs={{0,2},{1,3},{2,4},{3,5},{4,6},{5,7},{6,0},{7,1},{8,10},{9,11},{10,... | collective-permute-start | bytes 3145736 | tf_op jit(solution)/shard_map/ppermute | solution.py:181
  68.2 48.8 %collective-permute-start.9 = (bf16[512,1024]{1,0:T(8,128)(2,1)S(1)}, bf16[512,1024]{1,0:T(8,128)(2,1)S(1)}, u32[]{:S(2)}, u32[]{:S(2)}) collective-permute-start(bf16[512,1024]{1,0:T(8,128)(2,1)S(1)} %collective-permute-done.3.refs_4_.refs_10_.refs_7_), channel_id=1, source_target_pairs={{0,2},{1,3},{2,4},{3,5},{4,6},{5,7},{6,0},{7,1},{8,10},{9,11},{10,... | collective-permute-start | bytes 3145736 | tf_op jit(solution)/shard_map/ppermute | solution.py:181
  71.3 41.9 %collective-permute-start.8 = (f32[1,1024]{1,0:T(1,128)S(1)}, f32[1,1024]{1,0:T(1,128)S(1)}, u32[]{:S(2)}, u32[]{:S(2)}) collective-permute-start(f32[1,1024]{1,0:T(1,128)S(1)} %add.225), channel_id=1, source_target_pairs={{0,4},{1,5},{2,6},{3,7},{4,0},{5,1},{6,2},{7,3},{8,12},{9,13},{10,... | collective-permute-start | bytes 12296 | tf_op jit(solution)/shard_map/ppermute | solution.py:181
  104.1 20.9 %collective-permute-start.13 = (bf16[4096,256]{1,0:T(8,128)(2,1)}, bf16[4096,256]{1,0:T(8,128)(2,1)}, u32[]{:S(2)}, u32[]{:S(2)}) collective-permute-start(bf16[4096,256]{1,0:T(8,128)(2,1)} %collective-permute-done.7.refs_9_.refs_8_.refs_15_.refs_17_), channel_id=1, source_target_pairs={{0,1},{1,0},{2,3},{3,2},{4,5},{5,4},{6,7},{7,6},{8,9},{9,8},{10,11... | collective-permute-start | bytes 6291464 | tf_op jit(solution)/shard_map/ppermute | solution.py:181
  119.3 9.0 %collective-permute-start.14 = (bf16[4096,256]{1,0:T(8,128)(2,1)}, bf16[4096,256]{1,0:T(8,128)(2,1)}, u32[]{:S(2)}, u32[]{:S(2)}) collective-permute-start(bf16[4096,256]{1,0:T(8,128)(2,1)} %collective-permute-done.12.refs_11_.refs_17_.refs_19_), channel_id=1, source_target_pairs={{0,1},{1,0},{2,3},{3,2},{4,5},{5,4},{6,7},{7,6},{8,9},{9,8},{10,11... | collective-permute-start | bytes 6291464 | tf_op jit(solution)/shard_map/ppermute | solution.py:181
  122.3 50.5 %collective-permute-start.20 = (bf16[4096,256]{1,0:T(8,128)(2,1)}, bf16[4096,256]{1,0:T(8,128)(2,1)}, u32[]{:S(2)}, u32[]{:S(2)}) collective-permute-start(bf16[4096,256]{1,0:T(8,128)(2,1)} %slice.133), channel_id=1, source_target_pairs={{0,8},{1,9},{2,10},{3,11},{4,12},{5,13},{6,14},{7,15},{8,0},{9,1},... | collective-permute-start | bytes 6291464 | tf_op jit(solution)/shard_map/ppermute | solution.py:181
  122.9 3.7 %collective-permute-start.15 = (f32[2,1024]{1,0:T(2,128)S(1)}, f32[2,1024]{1,0:T(2,128)S(1)}, u32[]{:S(2)}, u32[]{:S(2)}) collective-permute-start(f32[2,1024]{1,0:T(2,128)S(1)} %pad_maximum_fusion.7), channel_id=1, source_target_pairs={{0,16},{1,17},{2,18},{3,19},{4,20},{5,21},{6,22},{7,23},{8,24},{9,... | collective-permute-start | bytes 24584 | tf_op jit(solution)/shard_map/ppermute | solution.py:181
  124.5 29.3 %collective-permute-start.18 = (bf16[512,1024]{1,0:T(8,128)(2,1)}, bf16[512,1024]{1,0:T(8,128)(2,1)}, u32[]{:S(2)}, u32[]{:S(2)}) collective-permute-start(bf16[512,1024]{1,0:T(8,128)(2,1)} %copy-done.8), channel_id=1, source_target_pairs={{0,16},{1,17},{2,18},{3,19},{4,20},{5,21},{6,22},{7,23},{8,24},{9,... | collective-permute-start | bytes 3145736 | tf_op jit(solution)/shard_map/ppermute | solution.py:181
  125.0 47.8 %collective-permute-start.17 = (bf16[512,1024]{1,0:T(8,128)(2,1)}, bf16[512,1024]{1,0:T(8,128)(2,1)}, u32[]{:S(2)}, u32[]{:S(2)}) collective-permute-start(bf16[512,1024]{1,0:T(8,128)(2,1)} %copy-done.11), channel_id=1, source_target_pairs={{0,2},{1,3},{2,4},{3,5},{4,6},{5,7},{6,0},{7,1},{8,10},{9,11},{10,... | collective-permute-start | bytes 3145736 | tf_op jit(solution)/shard_map/ppermute | solution.py:181
  126.6 46.2 %collective-permute-start.19 = (bf16[512,1024]{1,0:T(8,128)(2,1)}, bf16[512,1024]{1,0:T(8,128)(2,1)}, u32[]{:S(2)}, u32[]{:S(2)}) collective-permute-start(bf16[512,1024]{1,0:T(8,128)(2,1)} %copy-done.11), channel_id=1, source_target_pairs={{0,16},{1,17},{2,18},{3,19},{4,20},{5,21},{6,22},{7,23},{8,24},{9,... | collective-permute-start | bytes 3145736 | tf_op jit(solution)/shard_map/ppermute | solution.py:181
  128.2 46.1 %collective-permute-start.16 = (bf16[512,1024]{1,0:T(8,128)(2,1)}, bf16[512,1024]{1,0:T(8,128)(2,1)}, u32[]{:S(2)}, u32[]{:S(2)}) collective-permute-start(bf16[512,1024]{1,0:T(8,128)(2,1)} %copy-done.15), channel_id=1, source_target_pairs={{0,6},{1,7},{2,0},{3,1},{4,2},{5,3},{6,4},{7,5},{8,14},{9,15},{10,... | collective-permute-start | bytes 3145736 | tf_op jit(solution)/shard_map/ppermute | solution.py:181
  153.8 61.8 %collective-permute-start.23 = (bf16[4096,256]{1,0:T(8,128)(2,1)}, bf16[4096,256]{1,0:T(8,128)(2,1)}, u32[]{:S(2)}, u32[]{:S(2)}) collective-permute-start(bf16[4096,256]{1,0:T(8,128)(2,1)} %slice.136), channel_id=1, source_target_pairs={{0,8},{1,9},{2,10},{3,11},{4,12},{5,13},{6,14},{7,15},{8,0},{9,1},... | collective-permute-start | bytes 6291464 | tf_op jit(solution)/shard_map/ppermute | solution.py:181
  174.3 4.5 %collective-permute-start.21 = (bf16[4096,256]{1,0:T(8,128)(2,1)}, bf16[4096,256]{1,0:T(8,128)(2,1)}, u32[]{:S(2)}, u32[]{:S(2)}) collective-permute-start(bf16[4096,256]{1,0:T(8,128)(2,1)} %collective-permute-done.20.refs_19_.refs_21_), channel_id=1, source_target_pairs={{0,1},{1,0},{2,3},{3,2},{4,5},{5,4},{6,7},{7,6},{8,9},{9,8},{10,11... | collective-permute-start | bytes 6291464 | tf_op jit(solution)/shard_map/ppermute | solution.py:181
  177.4 48.4 %collective-permute-start.22 = (bf16[1024,1024]{1,0:T(8,128)(2,1)}, bf16[1024,1024]{1,0:T(8,128)(2,1)}, u32[]{:S(2)}, u32[]{:S(2)}) collective-permute-start(bf16[1024,1024]{1,0:T(8,128)(2,1)} %pad_maximum_fusion.1), channel_id=1, source_target_pairs={{0,16},{1,17},{2,18},{3,19},{4,20},{5,21},{6,22},{7,23},{8,24},{9,... | collective-permute-start | bytes 6291464 | tf_op jit(solution)/shard_map/ppermute | solution.py:181
  225.7 4.5 %collective-permute-start.24 = (bf16[4096,256]{1,0:T(8,128)(2,1)}, bf16[4096,256]{1,0:T(8,128)(2,1)}, u32[]{:S(2)}, u32[]{:S(2)}) collective-permute-start(bf16[4096,256]{1,0:T(8,128)(2,1)} %collective-permute-done.23.refs_23_), channel_id=1, source_target_pairs={{0,1},{1,0},{2,3},{3,2},{4,5},{5,4},{6,7},{7,6},{8,9},{9,8},{10,11... | collective-permute-start | bytes 6291464 | tf_op jit(solution)/shard_map/ppermute | solution.py:181
  268.7 10.0 %all-to-all-start = ((f32[8,1,1024]{2,1,0:T(1,128)}), f32[8,1,1024]{2,1,0:T(1,128)S(1)}, u32[]{:S(2)}, u32[]{:S(2)}) async-start(f32[8,1,1024]{2,1,0:T(1,128)} %all_to_all.13), calls=%async_computation | async-start | bytes 65536 | tf_op jit(solution)/shard_map/all_to_all | solution.py:359
  (20 other events, 495.7 us)

commit v3 on v2

--- a/solution.py
+++ b/solution.py
@@ -19,7 +19,16 @@
     firsts = [0]
     for _, columns in tiles:
         firsts.append(firsts[-1] + sum(g[2] for g in columns))
-    slot = lax.rem(step, 2)
+    blocks = [(g[0][0], k) for _, columns in tiles for g in columns for k in range(g[2])]
+    same = [k for k in range(1, len(blocks)) if blocks[k] == blocks[k - 1]]
+
+    def is_one_of(at, steps):
+        return functools.reduce(jnp.logical_or, [at == k for k in steps], at < 0)
+
+    def slot_of(at):
+        return lax.rem(at - sum(((at >= k).astype(jnp.int32) for k in same), jnp.int32(0)), 2)
+
+    slot = slot_of(step)
 
     def depth_at(j, size):
         return pl.multiple_of(kofs[j], 128) if j >= 0 else (-1 - j) * size
@@ -78,34 +87,37 @@
             for copy in row_copies(k):
                 copy.wait()
 
-    @pl.when(step + 1 < firsts[-1])
+    @pl.when((step + 1 < firsts[-1]) & jnp.logical_not(is_one_of(step + 1, same)))
     def _():
-        start_head(step + 1, lax.rem(step + 1, 2))
-
-    for copy in head_copies(tiles[0][1][0], 0, slot):
-        copy.wait()
+        start_head(step + 1, slot_of(step + 1))
+
+    @pl.when(jnp.logical_not(is_one_of(step, same)))
+    def _():
+        for copy in head_copies(tiles[0][1][0], 0, slot):
+            copy.wait()
 
     held = sum(((step >= f).astype(jnp.int32) for f in firsts[1:-1]), jnp.int32(0))
     rows, sub = x_scr.shape[1], 64
 
-    for which in range(2):
-        raw = jnp.dot(x_scr[lax.rem(held, 2)], h_scr[slot, which], preferred_element_type=jnp.float32)
-        base = colbase[step * 2 + which]
-        for at in range(0, rows, sub):
-            here = pl.ds(at, sub)
-            scale = f_scr[here, :]
-            wanted = t_scr[here, :] - base
-            parts = [raw[at : at + sub, c : c + 128] * scale for c in range(0, width, 128)]
-            old = m_scr[here, :]
-            new = functools.reduce(jnp.maximum, parts, old)
-            fade = jnp.exp(old - new)
-            total, moment, picked = s_scr[here, :] * fade, w_scr[here, :] * fade, p_scr[here, :]
-            for c, part in enumerate(parts):
-                weight = jnp.exp(part - new)
-                total += weight
-                moment += weight * part
-                picked = jnp.where(wanted == c * 128, part, picked)
-            m_scr[here, :], s_scr[here, :], w_scr[here, :], p_scr[here, :] = new, total, moment, picked
+    raws = [
+        jnp.dot(x_scr[lax.rem(held, 2)], h_scr[slot, which], preferred_element_type=jnp.float32)
+        for which in range(2)
+    ]
+    bases = [colbase[step * 2 + which] + c for which in range(2) for c in range(0, width, 128)]
+    for at in range(0, rows, sub):
+        here = pl.ds(at, sub)
+        scale, wanted = f_scr[here, :], t_scr[here, :]
+        parts = [raw[at : at + sub, c : c + 128] * scale for raw in raws for c in range(0, width, 128)]
+        old = m_scr[here, :]
+        new = functools.reduce(jnp.maximum, parts, old)
+        fade = jnp.exp(old - new)
+        total, moment, picked = s_scr[here, :] * fade, w_scr[here, :] * fade, p_scr[here, :]
+        for base, part in zip(bases, parts):
+            weight = jnp.exp(part - new)
+            total += weight
+            moment += weight * part
+            picked = jnp.where(wanted == base, part, picked)
+        m_scr[here, :], s_scr[here, :], w_scr[here, :], p_scr[here, :] = new, total, moment, picked
 
     for last in firsts[1:]:
         @pl.when(step == last - 1)
@@ -214,8 +226,10 @@
         one = results[0][:1, :1].astype(jnp.float32) if token[0] is None else token[0]
         token[0] = lax.optimization_barrier((one, *results))[0]
 
+    blocks = [head[:, :far_cols]]
+
     def far_part(k):
-        return after(head)[:, k * far_cols : (k + 1) * far_cols]
+        return after(blocks[k])
 
     far = [to_x(far_part(0))]
     other = to_core(mine(scaled, 1 - c))
@@ -308,8 +322,16 @@
             ring[j] = (to_z(array, by), 0)
             ends.append(ring[j][0])
             if step == 0 and n == 0 and n_far > 1:
-                block = lax.optimization_barrier((head, ends[0]))[0]
-                far.append(to_x(block[:, far_cols : 2 * far_cols]))
+                rest = lax.optimization_barrier((head, ends[0]))[0]
+                blocks += [rest[:, k * far_cols : (k + 1) * far_cols] for k in range(1, n_far)]
+                far.append(to_x(blocks[1]))
+                ends += blocks[1:]
+        if step == n_steps - 1:
+            for _, out, j in [y for y in y_list if y[2] > spots // 2]:
+                array, at = out[(j + 1) % spots]
+                out[j] = (to_z(after(array[at : at + n_a]), -1), 0)
+                ends.append(out[j][0])
+            y_list = [y for y in y_list if y[2] <= spots // 2]
         batch = [y_list.pop(0) for _ in range(len(y_list) if step == n_steps - 1 else min(stage, len(y_list)))]
         cuts = [[y for y in batch if y[0] is a], [y for y in batch if y[0] is b]] if step == 2 else [batch]
         for part in cuts:
@@ -334,54 +356,53 @@
             many = n_far > 1
             first = call(("A", [0, 1, 2] if many else [0]))
             y_side = lax.optimization_barrier((y_side, first))[0]
-            ends.append(call(("E", [0, 1] if many else [0])))
+            ends.append(call(("E", [0, 1, 2] if many else [0])))
         if step == 3:
-            more = [("E", [2, 3]), ("A", [3])] if many else []
+            more = [("E", [3]), ("A", [3])] if many else []
             ends.append(call(("B", [0, 1, 2, 3] if many else [0]), *more))
-        ends.append(far[min(step, n_far - 1)])
+        if step < n_steps - 1:
+            ends.append(far[min(step, n_far - 1)])
         if step == 0:
             ends.append(near)
         step_ends(*ends)
-    if n_far > 3:
-        far_near.append(to_core(after(far[3])))
-    call(("F", list(range(n_far + 1))), ("A", [n_far]), ("B", [n_far]), ("E", [n_far]))
+    if many:
+        ends = call(("F", [0, 1, 2, 3]))
+        far_near.append(to_core(lax.optimization_barrier((far[3], ends))[0]))
+        y_side = lax.optimization_barrier((y_side, ends))[0]
+        call(("F", [4]), ("A", [4]), ("B", [4]), ("E", [4]))
+    else:
+        call(("F", [0, 1]), ("A", [1]), ("B", [1]), ("E", [1]))
     own = jnp.concatenate([merge(jnp.stack(outs["A"])), merge(jnp.stack(outs["B"]))], axis=1)
-    peer = jnp.concatenate([merge(jnp.stack(outs["E"])), outs["F"][0]], axis=1)
+    peer = jnp.concatenate([merge(jnp.stack(outs["E"])), merge(jnp.stack(outs["F"]))], axis=1)
 
     first = q // 2 == 0
     whole = jnp.stack([jnp.where(first, own, peer), jnp.where(first, peer, own)])
-    whole = whole.reshape(2, 4, spots, blk).transpose(0, 2, 1, 3).reshape(2 * spots, 4 * blk)
+    whole = jnp.broadcast_to(whole.reshape(2, 1, 4 * half), (2, spots, 4 * half))
     kin = [
         [(2 * a + b) * n_vocab + 2 * k + core for a in range(2) for k in range(spots)]
         for b in range(2)
         for core in range(2)
     ]
     whole = lax.all_to_all(
-        whole, every, split_axis=0, concat_axis=0, axis_index_groups=kin, tiled=True
+        whole.reshape(2 * spots, 4 * half), every, split_axis=0, concat_axis=0, axis_index_groups=kin, tiled=True
     )
-    peak, total, moment, picked = merge(whole.reshape(2 * spots, 4, blk))
+    peak, total, moment, picked = merge(whole.reshape(2 * spots, 4, half))
     log_total = peak + jnp.log(total)
     lp, ent = picked - log_total, log_total - moment / total
 
     seq_lens = lengths[0, :-1]
     stops = jnp.cumsum(seq_lens)
     starts = stops - seq_lens
-    local = v * blk + jnp.arange(blk, dtype=jnp.int32)
+    local = jnp.arange(half, dtype=jnp.int32)
+    local = (local // blk * 2 + c) * blk + local % blk
     valid = local < stops[-1]
     lp = jnp.where(valid, lp, 0.0)
     ent = jnp.where(valid, ent, 0.0)
     member = (local[None, :] >= starts[:, None]) & (local[None, :] < stops[:, None])
     sums = jnp.sum(jnp.where(member[None], jnp.stack([lp, ent])[:, None, :], 0.0), axis=2)
-    sums = jnp.sum(
-        lax.all_to_all(
-            jnp.broadcast_to(sums.reshape(1, -1), (n_vocab, sums.size)),
-            "vocab",
-            split_axis=0,
-            concat_axis=0,
-            tiled=True,
-        ),
-        axis=0,
-    ).reshape(sums.shape)
+    sums = sums + to_core(sums)
+    lp = lax.dynamic_slice_in_dim(lp, s * blk, blk)
+    ent = lax.dynamic_slice_in_dim(ent, s * blk, blk)
     means = sums / seq_lens.astype(jnp.float32)[None]
     return (lp, ent, means[0], means[1])
 

time: 290 us -> 268 us (0.924)
  waiting for transfers between devices: 111 us -> 98.9 us
  blocking collectives: 7.91 us -> 0 us
  other arithmetic: 11.4 us -> 8.38 us
    ppermute x25 -> x27, waiting for transfers between devices: 105 us -> 91.9 us  [move(): return lax.ppermute(x, every, pairs)]
    all_to_all x1 -> x0, blocking collectives: 7.91 us -> none  [shards(): lax.all_to_all(jnp.broadcast_to(sums.reshape(1, -1), (n_vocab, sums.size)...]
    slice x4, local copies, waits for them, and re-layouts: 11 us -> 4.36 us  [the longest x1 2.32 us: shards(): rest[:, k * far_cols:(k + 1) * far_cols]]
    concatenate x2 -> x1, other arithmetic: 3.29 us -> 0.17 us  [shards(): jnp.concatenate(arrays)]
    ppermute x25 -> x27, starting transfers between devices: 27.9 us -> 29.9 us  [move(): return lax.ppermute(x, every, pairs)]
    unnamed x36 -> x34, local copies, waits for them, and re-layouts: 5.69 us -> 7.49 us
    pallas_call x4 -> x5, Pallas kernels: 107 us -> 109 us  [stats(): pl.pallas_call(functools.partial(stats_kernel, tiles, len(pieces), len(he...]
  transfers between devices with their start and end apart: 26 -> 28, of which waited for: 14 -> 10; matrix products, arithmetic and copies ran while one was open for 6% -> 3% of each run, Pallas kernels for 24% -> 35%
where the time goes in v3:
time: 268 us; the launch traced here: 267 us
  Pallas kernels  109 us (41%)
  waiting for transfers between devices  98.9 us (37%)
  starting transfers between devices  33.3 us (12%)
  local copies, waits for them, and re-layouts  16.6 us (6%)
  other arithmetic  8.38 us (3%)
    pallas_call x5, Pallas kernels, stats(): pl.pallas_call(functools.partial(stats_kernel, tiles, len(pieces), len(he...  109 us
    ppermute x27, waiting for transfers between devices, move(): return lax.ppermute(x, every, pairs)  91.9 us
    ppermute x27, starting transfers between devices, move(): return lax.ppermute(x, every, pairs)  29.9 us
    unnamed x34, local copies, waits for them, and re-layouts  7.49 us
    all_to_all x1, waiting for transfers between devices, shards(): lax.all_to_all(whole.reshape(2 * spots, 4 * half), every, split_axis=0, c...  7 us
  transfers between devices with their start and end apart: 28, of which 10 were waited for; matrix products, arithmetic and copies ran while one was open for 3% of the time, Pallas kernels for 35%

profile of v3, /device:TPU:0, one launch (start us, length us, event | category | flops | bytes accessed | tf_op | source)
XLA Modules:
  0.0 267.3 jit_solution(6940198495940824252)
XLA Ops:
  1.4 2.3 fusion.1
  5.6 2.1 collective-permute-done.1
  8.1 2.5 maximum_select_fusion.refs_3_.refs_7_
  10.8 2.8 %collective-permute-start.3 = (bf16[512,1024]{1,0:T(8,128)(2,1)S(1)}, bf16[512,1024]{1,0:T(8,128)(2,1)S(1)}, u32[]{:S(2)}, u32[]{:S(2)}) collective-permute-start(bf16[512,1024]{1,0:T(8,128)(2,1)S(1)} %get-tuple-element.43), channel_id=1, source_target_pairs={{0,2},{1,3},{2,4},{3,5},{4,6},{5,7},{6,0},{7,1},{8,10},{9,11},{10,... | collective-permute-start | bytes 3145736 | tf_op jit(solution)/shard_map/ppermute | solution.py:193
  13.8 2.4 collective-permute-start.7
  19.3 20.0 %collective-permute-done.3.refs_4_.refs_10_.refs_8_ = bf16[512,1024]{1,0:T(8,128)(2,1)S(1)} collective-permute-done((bf16[512,1024]{1,0:T(8,128)(2,1)S(1)}, bf16[512,1024]{1,0:T(8,128)(2,1)S(1)}, u32[]{:S(2)}, u32[]{:S(2)}) %collective-permute-start.3) | collective-permute-done | bytes 1048608 | tf_op jit(solution)/shard_map/ppermute | solution.py:193
  39.3 1.7 collective-permute-start.5
  41.0 2.3 fusion.62
  44.9 19.3 %collective-permute-done.5.refs_5_.refs_11_.refs_9_ = bf16[512,1024]{1,0:T(8,128)(2,1)S(1)} collective-permute-done((bf16[512,1024]{1,0:T(8,128)(2,1)S(1)}, bf16[512,1024]{1,0:T(8,128)(2,1)S(1)}, u32[]{:S(2)}, u32[]{:S(2)}) %collective-permute-start.5) | collective-permute-done | bytes 1048608 | tf_op jit(solution)/shard_map/ppermute | solution.py:193
  69.8 2.4 collective-permute-start.8
  72.2 35.2 %collective-permute-done.12.refs_11_.refs_10_.refs_17_ = bf16[4096,256]{1,0:T(8,128)(2,1)} collective-permute-done((bf16[4096,256]{1,0:T(8,128)(2,1)S(1)}, bf16[4096,256]{1,0:T(8,128)(2,1)}, u32[]{:S(2)}, u32[]{:S(2)}) %collective-permute-start.12) | collective-permute-done | bytes 2097184 | tf_op jit(solution)/shard_map/ppermute | solution.py:193
  107.4 5.0 %collective-permute-done.8 = f32[1,1024]{1,0:T(1,128)S(1)} collective-permute-done((f32[1,1024]{1,0:T(1,128)S(1)}, f32[1,1024]{1,0:T(1,128)S(1)}, u32[]{:S(2)}, u32[]{:S(2)}) %collective-permute-start.8) | collective-permute-done | bytes 4128 | tf_op jit(solution)/shard_map/ppermute | solution.py:193
  112.4 3.3 %collective-permute-done.10.refs_4_.refs_11_ = bf16[512,1024]{1,0:T(8,128)(2,1)S(1)} collective-permute-done((bf16[512,1024]{1,0:T(8,128)(2,1)S(1)}, bf16[512,1024]{1,0:T(8,128)(2,1)S(1)}, u32[]{:S(2)}, u32[]{:S(2)}) %collective-permute-start.10) | collective-permute-done | bytes 1048608 | tf_op jit(solution)/shard_map/ppermute | solution.py:193
  121.1 1.6 collective-permute-start.16
  127.1 19.7 %shard_map.84 = f32[4,512]{1,0:T(4,128)S(1)} custom-call(s32[4]{0:T(128)S(1)} %fusion.55.refs_0_, s32[12]{0:T(128)S(1)} %stack.233.refs_1_, f32[2,512]{1,0:T(2,128)S(1)} %get-tuple-element.51.refs_2_, bf16[1024,1024]{1,0:T(8,128)(2,1)S(1)} %maximum_select_fusion.refs_3_.refs_7_, bf16[512,1024]{1,0:T(8,128)(2,1)S(1)} %collective-permute-done.3.refs_4_.refs_10_.refs_8_, ...), custom_call_target="tpu_custom_call" | custom-call | flops 1048576 | bytes 1024 | tf_op jit(solution)/shard_map/pallas_call | solution.py:143
  146.8 19.8 %shard_map.85 = f32[4,512]{1,0:T(4,128)S(1)} custom-call(s32[4]{0:T(128)S(1)} %fusion.55.refs_0_, s32[12]{0:T(128)S(1)} %stack.233.refs_1_, f32[2,512]{1,0:T(2,128)S(1)} %get-tuple-element.59.refs_2_, bf16[1024,1024]{1,0:T(8,128)(2,1)S(1)} %copy-done.2, bf16[1024,1024]{1,0:T(8,128)(2,1)S(1)} %copy-done.5, ...), custom_call_target="tpu_custom_call" | custom-call | flops 1048576 | bytes 1024 | tf_op jit(solution)/shard_map/pallas_call | solution.py:143
  166.7 1.6 collective-permute-done.17.refs_6_.refs_13_
  170.6 3.0 %collective-permute-start.22 = (bf16[512,1024]{1,0:T(8,128)(2,1)}, bf16[512,1024]{1,0:T(8,128)(2,1)S(1)}, u32[]{:S(2)}, u32[]{:S(2)}) collective-permute-start(bf16[512,1024]{1,0:T(8,128)(2,1)} %slice.196), channel_id=1, source_target_pairs={{0,6},{1,7},{2,0},{3,1},{4,2},{5,3},{6,4},{7,5},{8,14},{9,15},{10,... | collective-permute-start | bytes 3145736 | tf_op jit(solution)/shard_map/ppermute | solution.py:193
  174.3 30.4 %shard_map.86 = f32[4,1536]{1,0:T(4,128)S(1)} custom-call(s32[4]{0:T(128)S(1)} %fusion.55.refs_0_, s32[18]{0:T(128)S(1)} %stack.237.refs_1_, f32[2,1536]{1,0:T(2,128)S(1)} %pad_maximum_fusion.6.refs_2_, bf16[1024,1024]{1,0:T(8,128)(2,1)} %copy-done, bf16[512,1024]{1,0:T(8,128)(2,1)S(1)} %copy-done.12, ...), custom_call_target="tpu_custom_call" | custom-call | flops 1048576 | bytes 1024 | tf_op jit(solution)/shard_map/pallas_call | solution.py:143
  204.8 22.5 %shard_map.87 = f32[4,512]{1,0:T(4,128)S(1)} custom-call(s32[4]{0:T(128)S(1)} %fusion.55.refs_0_, s32[14]{0:T(128)S(1)} %stack.242.refs_1_, f32[2,512]{1,0:T(2,128)S(1)} %get-tuple-element.67.refs_2_, bf16[1024,1024]{1,0:T(8,128)(2,1)S(1)} %copy-done.3, bf16[512,1024]{1,0:T(8,128)(2,1)} %collective-permute-done.19.refs_4_, ...), custom_call_target="tpu_custom_call" | custom-call | flops 1048576 | bytes 1024 | tf_op jit(solution)/shard_map/pallas_call | solution.py:143
  227.8 4.1 %collective-permute-done.25.refs_17_ = bf16[4096,256]{1,0:T(8,128)(2,1)} collective-permute-done((bf16[4096,256]{1,0:T(8,128)(2,1)}, bf16[4096,256]{1,0:T(8,128)(2,1)}, u32[]{:S(2)}, u32[]{:S(2)}) %collective-permute-start.25) | collective-permute-done | bytes 2097184 | tf_op jit(solution)/shard_map/ppermute | solution.py:193
  233.1 16.4 %shard_map.88 = f32[4,2048]{1,0:T(4,128)S(1)} custom-call(s32[4]{0:T(128)S(1)} %fusion.55.refs_0_, s32[8]{0:T(128)S(1)} %stack.241.refs_1_, f32[2,2048]{1,0:T(2,128)S(1)} %pad_maximum_fusion.3.refs_2_, bf16[1024,1024]{1,0:T(8,128)(2,1)} %copy-done.1, bf16[512,1024]{1,0:T(8,128)(2,1)} %collective-permute-done.19.refs_4_, ...), custom_call_target="tpu_custom_call" | custom-call | flops 1048576 | bytes 1024 | tf_op jit(solution)/shard_map/pallas_call | solution.py:143
  251.0 3.4 %all-to-all-start = ((f32[8,1,4096]{2,1,0:T(1,128)}), f32[8,1,4096]{2,1,0:T(1,128)S(1)}, u32[]{:S(2)}, u32[]{:S(2)}) async-start(f32[8,1,4096]{2,1,0:T(1,128)} %all_to_all.6), calls=%async_computation | async-start | bytes 262144 | tf_op jit(solution)/shard_map/all_to_all | solution.py:386
  255.0 7.0 %all-to-all-done = f32[8,1,4096]{2,1,0:T(1,128)S(1)} async-done(((f32[8,1,4096]{2,1,0:T(1,128)}), f32[8,1,4096]{2,1,0:T(1,128)S(1)}, u32[]{:S(2)}, u32[]{:S(2)}) %all-to-all-start) | async-done | bytes 131104 | tf_op jit(solution)/shard_map/all_to_all | solution.py:386
  (139 shorter events, 35.1 us)
Async XLA Ops:
  7.7 31.6 %collective-permute-start.4 = (bf16[4096,1024]{1,0:T(8,128)(2,1)}, bf16[4096,1024]{1,0:T(8,128)(2,1)}, u32[]{:S(2)}, u32[]{:S(2)}) collective-permute-start(bf16[4096,1024]{1,0:T(8,128)(2,1)} %refs_7_.3), channel_id=1, source_target_pairs={{0,1},{1,0},{2,3},{3,2},{4,5},{5,4},{6,7},{7,6},{8,9},{9,8},{10,11... | collective-permute-start | bytes 25165832 | tf_op jit(solution)/shard_map/ppermute | solution.py:193
  10.8 28.5 %collective-permute-start.3 = (bf16[512,1024]{1,0:T(8,128)(2,1)S(1)}, bf16[512,1024]{1,0:T(8,128)(2,1)S(1)}, u32[]{:S(2)}, u32[]{:S(2)}) collective-permute-start(bf16[512,1024]{1,0:T(8,128)(2,1)S(1)} %get-tuple-element.43), channel_id=1, source_target_pairs={{0,2},{1,3},{2,4},{3,5},{4,6},{5,7},{6,0},{7,1},{8,10},{9,11},{10,... | collective-permute-start | bytes 3145736 | tf_op jit(solution)/shard_map/ppermute | solution.py:193
  13.8 51.3 %collective-permute-start.7 = (bf16[4096,256]{1,0:T(8,128)(2,1)S(1)}, bf16[4096,256]{1,0:T(8,128)(2,1)}, u32[]{:S(2)}, u32[]{:S(2)}) collective-permute-start(bf16[4096,256]{1,0:T(8,128)(2,1)S(1)} %slice.150), channel_id=1, source_target_pairs={{0,8},{1,9},{2,10},{3,11},{4,12},{5,13},{6,14},{7,15},{8,0},{9,1},... | collective-permute-start | bytes 6291464 | tf_op jit(solution)/shard_map/ppermute | solution.py:193
  16.2 48.9 %collective-permute-start.6 = (bf16[1024,1024]{1,0:T(8,128)(2,1)S(1)}, bf16[1024,1024]{1,0:T(8,128)(2,1)S(1)}, u32[]{:S(2)}, u32[]{:S(2)}) collective-permute-start(bf16[1024,1024]{1,0:T(8,128)(2,1)S(1)} %maximum_select_fusion.refs_3_.refs_7_), channel_id=1, source_target_pairs={{0,16},{1,17},{2,18},{3,19},{4,20},{5,21},{6,22},{7,23},{8,24},{9,... | collective-permute-start | bytes 6291464 | tf_op jit(solution)/shard_map/ppermute | solution.py:193
  17.8 47.4 %collective-permute-start.2 = (f32[1,1024]{1,0:T(1,128)S(1)}, f32[1,1024]{1,0:T(1,128)S(1)}, u32[]{:S(2)}, u32[]{:S(2)}) collective-permute-start(f32[1,1024]{1,0:T(1,128)S(1)} %add.288), channel_id=1, source_target_pairs={{0,2},{1,3},{2,4},{3,5},{4,6},{5,7},{6,0},{7,1},{8,10},{9,11},{10,... | collective-permute-start | bytes 12296 | tf_op jit(solution)/shard_map/ppermute | solution.py:193
  39.3 24.8 %collective-permute-start.5 = (bf16[512,1024]{1,0:T(8,128)(2,1)S(1)}, bf16[512,1024]{1,0:T(8,128)(2,1)S(1)}, u32[]{:S(2)}, u32[]{:S(2)}) collective-permute-start(bf16[512,1024]{1,0:T(8,128)(2,1)S(1)} %get-tuple-element.43), channel_id=1, source_target_pairs={{0,6},{1,7},{2,0},{3,1},{4,2},{5,3},{6,4},{7,5},{8,14},{9,15},{10,... | collective-permute-start | bytes 3145736 | tf_op jit(solution)/shard_map/ppermute | solution.py:193
  43.4 64.1 %collective-permute-start.12 = (bf16[4096,256]{1,0:T(8,128)(2,1)S(1)}, bf16[4096,256]{1,0:T(8,128)(2,1)}, u32[]{:S(2)}, u32[]{:S(2)}) collective-permute-start(bf16[4096,256]{1,0:T(8,128)(2,1)S(1)} %get-tuple-element.100), channel_id=1, source_target_pairs={{0,8},{1,9},{2,10},{3,11},{4,12},{5,13},{6,14},{7,15},{8,0},{9,1},... | collective-permute-start | bytes 6291464 | tf_op jit(solution)/shard_map/ppermute | solution.py:193
  66.4 49.3 %collective-permute-start.11 = (bf16[1024,1024]{1,0:T(8,128)(2,1)S(1)}, bf16[1024,1024]{1,0:T(8,128)(2,1)S(1)}, u32[]{:S(2)}, u32[]{:S(2)}) collective-permute-start(bf16[1024,1024]{1,0:T(8,128)(2,1)S(1)} %pad_maximum_fusion), channel_id=1, source_target_pairs={{0,16},{1,17},{2,18},{3,19},{4,20},{5,21},{6,22},{7,23},{8,24},{9,... | collective-permute-start | bytes 6291464 | tf_op jit(solution)/shard_map/ppermute | solution.py:193
  67.8 44.7 %collective-permute-start.9 = (bf16[512,1024]{1,0:T(8,128)(2,1)S(1)}, bf16[512,1024]{1,0:T(8,128)(2,1)S(1)}, u32[]{:S(2)}, u32[]{:S(2)}) collective-permute-start(bf16[512,1024]{1,0:T(8,128)(2,1)S(1)} %collective-permute-done.3.refs_4_.refs_10_.refs_8_), channel_id=1, source_target_pairs={{0,2},{1,3},{2,4},{3,5},{4,6},{5,7},{6,0},{7,1},{8,10},{9,11},{10,... | collective-permute-start | bytes 3145736 | tf_op jit(solution)/shard_map/ppermute | solution.py:193
  68.3 47.5 %collective-permute-start.10 = (bf16[512,1024]{1,0:T(8,128)(2,1)S(1)}, bf16[512,1024]{1,0:T(8,128)(2,1)S(1)}, u32[]{:S(2)}, u32[]{:S(2)}) collective-permute-start(bf16[512,1024]{1,0:T(8,128)(2,1)S(1)} %get-tuple-element.56), channel_id=1, source_target_pairs={{0,2},{1,3},{2,4},{3,5},{4,6},{5,7},{6,0},{7,1},{8,10},{9,11},{10,... | collective-permute-start | bytes 3145736 | tf_op jit(solution)/shard_map/ppermute | solution.py:193
  69.8 42.6 %collective-permute-start.8 = (f32[1,1024]{1,0:T(1,128)S(1)}, f32[1,1024]{1,0:T(1,128)S(1)}, u32[]{:S(2)}, u32[]{:S(2)}) collective-permute-start(f32[1,1024]{1,0:T(1,128)S(1)} %add.290), channel_id=1, source_target_pairs={{0,4},{1,5},{2,6},{3,7},{4,0},{5,1},{6,2},{7,3},{8,12},{9,13},{10,... | collective-permute-start | bytes 12296 | tf_op jit(solution)/shard_map/ppermute | solution.py:193
  107.4 13.7 %collective-permute-start.13 = (bf16[4096,256]{1,0:T(8,128)(2,1)}, bf16[4096,256]{1,0:T(8,128)(2,1)}, u32[]{:S(2)}, u32[]{:S(2)}) collective-permute-start(bf16[4096,256]{1,0:T(8,128)(2,1)} %collective-permute-done.7.refs_9_.refs_8_.refs_15_), channel_id=1, source_target_pairs={{0,1},{1,0},{2,3},{3,2},{4,5},{5,4},{6,7},{7,6},{8,9},{9,8},{10,11... | collective-permute-start | bytes 6291464 | tf_op jit(solution)/shard_map/ppermute | solution.py:193
  117.2 6.9 %collective-permute-start.14 = (bf16[4096,256]{1,0:T(8,128)(2,1)}, bf16[4096,256]{1,0:T(8,128)(2,1)}, u32[]{:S(2)}, u32[]{:S(2)}) collective-permute-start(bf16[4096,256]{1,0:T(8,128)(2,1)} %collective-permute-done.12.refs_11_.refs_10_.refs_17_), channel_id=1, source_target_pairs={{0,1},{1,0},{2,3},{3,2},{4,5},{5,4},{6,7},{7,6},{8,9},{9,8},{10,11... | collective-permute-start | bytes 6291464 | tf_op jit(solution)/shard_map/ppermute | solution.py:193
  117.5 49.2 %collective-permute-start.20 = (bf16[4096,256]{1,0:T(8,128)(2,1)}, bf16[4096,256]{1,0:T(8,128)(2,1)}, u32[]{:S(2)}, u32[]{:S(2)}) collective-permute-start(bf16[4096,256]{1,0:T(8,128)(2,1)} %get-tuple-element.60), channel_id=1, source_target_pairs={{0,8},{1,9},{2,10},{3,11},{4,12},{5,13},{6,14},{7,15},{8,0},{9,1},... | collective-permute-start | bytes 6291464 | tf_op jit(solution)/shard_map/ppermute | solution.py:193
  119.6 27.2 %collective-permute-start.18 = (bf16[512,1024]{1,0:T(8,128)(2,1)}, bf16[512,1024]{1,0:T(8,128)(2,1)}, u32[]{:S(2)}, u32[]{:S(2)}) collective-permute-start(bf16[512,1024]{1,0:T(8,128)(2,1)} %copy-done.9), channel_id=1, source_target_pairs={{0,16},{1,17},{2,18},{3,19},{4,20},{5,21},{6,22},{7,23},{8,24},{9,... | collective-permute-start | bytes 3145736 | tf_op jit(solution)/shard_map/ppermute | solution.py:193
  121.1 45.6 %collective-permute-start.16 = (bf16[512,1024]{1,0:T(8,128)(2,1)}, bf16[512,1024]{1,0:T(8,128)(2,1)}, u32[]{:S(2)}, u32[]{:S(2)}) collective-permute-start(bf16[512,1024]{1,0:T(8,128)(2,1)} %copy-done.14), channel_id=1, source_target_pairs={{0,6},{1,7},{2,0},{3,1},{4,2},{5,3},{6,4},{7,5},{8,14},{9,15},{10,... | collective-permute-start | bytes 3145736 | tf_op jit(solution)/shard_map/ppermute | solution.py:193
  122.8 45.6 %collective-permute-start.17 = (bf16[512,1024]{1,0:T(8,128)(2,1)}, bf16[512,1024]{1,0:T(8,128)(2,1)}, u32[]{:S(2)}, u32[]{:S(2)}) collective-permute-start(bf16[512,1024]{1,0:T(8,128)(2,1)} %copy-done.11), channel_id=1, source_target_pairs={{0,2},{1,3},{2,4},{3,5},{4,6},{5,7},{6,0},{7,1},{8,10},{9,11},{10,... | collective-permute-start | bytes 3145736 | tf_op jit(solution)/shard_map/ppermute | solution.py:193
  124.1 44.3 %collective-permute-start.19 = (bf16[512,1024]{1,0:T(8,128)(2,1)}, bf16[512,1024]{1,0:T(8,128)(2,1)}, u32[]{:S(2)}, u32[]{:S(2)}) collective-permute-start(bf16[512,1024]{1,0:T(8,128)(2,1)} %copy-done.11), channel_id=1, source_target_pairs={{0,16},{1,17},{2,18},{3,19},{4,20},{5,21},{6,22},{7,23},{8,24},{9,... | collective-permute-start | bytes 3145736 | tf_op jit(solution)/shard_map/ppermute | solution.py:193
  168.4 6.0 %collective-permute-start.21 = (bf16[4096,256]{1,0:T(8,128)(2,1)}, bf16[4096,256]{1,0:T(8,128)(2,1)}, u32[]{:S(2)}, u32[]{:S(2)}) collective-permute-start(bf16[4096,256]{1,0:T(8,128)(2,1)} %collective-permute-done.20.refs_19_.refs_13_), channel_id=1, source_target_pairs={{0,1},{1,0},{2,3},{3,2},{4,5},{5,4},{6,7},{7,6},{8,9},{9,8},{10,11... | collective-permute-start | bytes 6291464 | tf_op jit(solution)/shard_map/ppermute | solution.py:193
  168.4 59.0 %collective-permute-start.24 = (bf16[4096,256]{1,0:T(8,128)(2,1)}, bf16[4096,256]{1,0:T(8,128)(2,1)}, u32[]{:S(2)}, u32[]{:S(2)}) collective-permute-start(bf16[4096,256]{1,0:T(8,128)(2,1)} %get-tuple-element.70), channel_id=1, source_target_pairs={{0,8},{1,9},{2,10},{3,11},{4,12},{5,13},{6,14},{7,15},{8,0},{9,1},... | collective-permute-start | bytes 6291464 | tf_op jit(solution)/shard_map/ppermute | solution.py:193
  170.6 34.1 %collective-permute-start.22 = (bf16[512,1024]{1,0:T(8,128)(2,1)}, bf16[512,1024]{1,0:T(8,128)(2,1)S(1)}, u32[]{:S(2)}, u32[]{:S(2)}) collective-permute-start(bf16[512,1024]{1,0:T(8,128)(2,1)} %slice.196), channel_id=1, source_target_pairs={{0,6},{1,7},{2,0},{3,1},{4,2},{5,3},{6,4},{7,5},{8,14},{9,15},{10,... | collective-permute-start | bytes 3145736 | tf_op jit(solution)/shard_map/ppermute | solution.py:193
  173.6 31.2 %collective-permute-start.23 = (bf16[512,1024]{1,0:T(8,128)(2,1)}, bf16[512,1024]{1,0:T(8,128)(2,1)}, u32[]{:S(2)}, u32[]{:S(2)}) collective-permute-start(bf16[512,1024]{1,0:T(8,128)(2,1)} %collective-permute-done.17.refs_6_.refs_13_), channel_id=1, source_target_pairs={{0,16},{1,17},{2,18},{3,19},{4,20},{5,21},{6,22},{7,23},{8,24},{9,... | collective-permute-start | bytes 3145736 | tf_op jit(solution)/shard_map/ppermute | solution.py:193
  227.3 4.6 %collective-permute-start.25 = (bf16[4096,256]{1,0:T(8,128)(2,1)}, bf16[4096,256]{1,0:T(8,128)(2,1)}, u32[]{:S(2)}, u32[]{:S(2)}) collective-permute-start(bf16[4096,256]{1,0:T(8,128)(2,1)} %collective-permute-done.24.refs_16_), channel_id=1, source_target_pairs={{0,1},{1,0},{2,3},{3,2},{4,5},{5,4},{6,7},{7,6},{8,9},{9,8},{10,11... | collective-permute-start | bytes 6291464 | tf_op jit(solution)/shard_map/ppermute | solution.py:193
  251.0 11.1 %all-to-all-start = ((f32[8,1,4096]{2,1,0:T(1,128)}), f32[8,1,4096]{2,1,0:T(1,128)S(1)}, u32[]{:S(2)}, u32[]{:S(2)}) async-start(f32[8,1,4096]{2,1,0:T(1,128)} %all_to_all.6), calls=%async_computation | async-start | bytes 262144 | tf_op jit(solution)/shard_map/all_to_all | solution.py:386
  (21 other events, 375.1 us)

commit v4 on v3

--- a/solution.py
+++ b/solution.py
@@ -208,11 +208,6 @@
     far_cols = cols // n_far
     width = min(256, far_cols)
 
-    values = hidden.astype(jnp.float32)
-    own_gain = lax.dynamic_slice_in_dim(gain, v * feats, feats) * SHRINK
-    scaled = (values * own_gain[None, :]).astype(jnp.bfloat16).reshape(spots, 2, blk, feats)
-    square = jnp.sum(values * values, axis=1).reshape(spots, 2, blk)
-
     def mine(x, core):
         x = lax.dynamic_index_in_dim(x, core, 1, keepdims=False)
         return x.reshape(half, *x.shape[2:])
@@ -232,17 +227,19 @@
         return after(blocks[k])
 
     far = [to_x(far_part(0))]
-    other = to_core(mine(scaled, 1 - c))
-    other_square = to_core(mine(square, 1 - c).reshape(1, half))
-    square_sum = other_square + mine(square, c).reshape(1, half)
-    one = mine(scaled, c)
-    piece = jnp.where(
+    raw = hidden.reshape(spots, 2, blk, feats)
+    other = to_core(mine(raw, 1 - c))
+    one = mine(raw, c)
+    values = jnp.where(
         c == 0, jnp.concatenate([one, other], axis=1), jnp.concatenate([other, one], axis=1)
-    )
+    ).astype(jnp.float32)
+    pair_gain = lax.dynamic_slice_in_dim(gain, 2 * s * feats, 2 * feats) * SHRINK
+    piece = (values * pair_gain[None, :]).astype(jnp.bfloat16)
+    square_sum = jnp.sum(values * values, axis=1).reshape(1, half)
     n_a = half // 2
     a, b = {0: (piece, 0)}, {0: (piece, n_a)}
     ya, yb, far_near = {}, {}, []
-    step_ends(other, other_square)
+    step_ends(other)
     near = to_core(after(head))
 
     trip = [0] + [j for k in range(1, spots // 2 + 1) for j in dict.fromkeys((k, spots - k))]
@@ -317,8 +314,6 @@
             by = 1 if j <= spots // 2 else -1
             array, at = ring[(j - by) % spots]
             array = after(array[at : at + n_a])
-            if step == 0 and n == 1:
-                array = lax.optimization_barrier((array, near))[0]
             ring[j] = (to_z(array, by), 0)
             ends.append(ring[j][0])
             if step == 0 and n == 0 and n_far > 1:
@@ -342,7 +337,7 @@
             ends.append(sent)
         for _ in range(1 if spots == 4 else 5):
             if 2**doubled < spots:
-                sent = to_z(after(tiny), 2**doubled)
+                sent = to_z(lax.optimization_barrier((after(tiny), ends[0]))[0] if step == 0 else after(tiny), 2**doubled)
                 tiny = tiny + sent
                 doubled += 1
                 ends.append(sent)
@@ -358,8 +353,7 @@
             y_side = lax.optimization_barrier((y_side, first))[0]
             ends.append(call(("E", [0, 1, 2] if many else [0])))
         if step == 3:
-            more = [("E", [3]), ("A", [3])] if many else []
-            ends.append(call(("B", [0, 1, 2, 3] if many else [0]), *more))
+            ends.append(call(("B", [0, 1, 2, 3] if many else [0])))
         if step < n_steps - 1:
             ends.append(far[min(step, n_far - 1)])
         if step == 0:
@@ -368,6 +362,8 @@
     if many:
         ends = call(("F", [0, 1, 2, 3]))
         far_near.append(to_core(lax.optimization_barrier((far[3], ends))[0]))
+        y_side = lax.optimization_barrier((y_side, ends))[0]
+        ends = call(("E", [3]), ("A", [3]))
         y_side = lax.optimization_barrier((y_side, ends))[0]
         call(("F", [4]), ("A", [4]), ("B", [4]), ("E", [4]))
     else:

time: 268 us -> 266 us (level)
  Pallas kernels: 109 us -> 112 us
    pallas_call x5 -> x6, Pallas kernels: 109 us -> 112 us  [stats(): pl.pallas_call(functools.partial(stats_kernel, tiles, len(pieces), len(he...]
    ppermute x27 -> x26, waiting for transfers between devices: 91.9 us -> 89.1 us  [move(): return lax.ppermute(x, every, pairs)]
    unnamed x34 -> x36, local copies, waits for them, and re-layouts: 7.49 us -> 6.82 us
    ppermute x27 -> x26, starting transfers between devices: 29.9 us -> 29.9 us  [move(): return lax.ppermute(x, every, pairs)]
  transfers between devices with their start and end apart: 28 -> 27, of which waited for: 10 -> 11; matrix products, arithmetic and copies ran while one was open for 3% -> 3% of each run, Pallas kernels for 35% -> 36%
where the time goes in v4:
time: 266 us
  Pallas kernels  112 us (42%)
  waiting for transfers between devices  96.5 us (36%)
  starting transfers between devices  33.2 us (12%)
  local copies, waits for them, and re-layouts  16.5 us (6%)
  other arithmetic  6.21 us (2%)
    pallas_call x6, Pallas kernels, stats(): pl.pallas_call(functools.partial(stats_kernel, tiles, len(pieces), len(he...  112 us
    ppermute x26, waiting for transfers between devices, move(): return lax.ppermute(x, every, pairs)  89.1 us
    ppermute x26, starting transfers between devices, move(): return lax.ppermute(x, every, pairs)  29.9 us
    all_to_all x1, waiting for transfers between devices, shards(): lax.all_to_all(whole.reshape(2 * spots, 4 * half), every, split_axis=0, c...  7.35 us
    unnamed x36, local copies, waits for them, and re-layouts  6.82 us
  transfers between devices with their start and end apart: 27, of which 11 were waited for; matrix products, arithmetic and copies ran while one was open for 3% of the time, Pallas kernels for 36%

profile of v4, /device:TPU:0, one launch (start us, length us, event | category | flops | bytes accessed | tf_op | source)
XLA Modules:
  0.0 265.5 jit_solution(5740264388420105236)
XLA Ops:
  0.7 1.8 constant_dynamic-slice_fusion.1
  3.0 2.4 collective-permute-done
  6.4 2.6 fusion.1
  9.2 2.8 %collective-permute-start.1 = (bf16[512,1024]{1,0:T(8,128)(2,1)S(1)}, bf16[512,1024]{1,0:T(8,128)(2,1)S(1)}, u32[]{:S(2)}, u32[]{:S(2)}) collective-permute-start(bf16[512,1024]{1,0:T(8,128)(2,1)S(1)} %get-tuple-element.42), channel_id=1, source_target_pairs={{0,2},{1,3},{2,4},{3,5},{4,6},{5,7},{6,0},{7,1},{8,10},{9,11},{10,... | collective-permute-start | bytes 3145736 | tf_op jit(solution)/shard_map/ppermute | solution.py:193
  12.3 2.2 collective-permute-start.5
  16.0 3.6 %collective-permute-start.3 = (bf16[512,1024]{1,0:T(8,128)(2,1)S(1)}, bf16[512,1024]{1,0:T(8,128)(2,1)S(1)}, u32[]{:S(2)}, u32[]{:S(2)}) collective-permute-start(bf16[512,1024]{1,0:T(8,128)(2,1)S(1)} %get-tuple-element.42), channel_id=1, source_target_pairs={{0,6},{1,7},{2,0},{3,1},{4,2},{5,3},{6,4},{7,5},{8,14},{9,15},{10,... | collective-permute-start | bytes 3145736 | tf_op jit(solution)/shard_map/ppermute | solution.py:193
  19.6 18.4 %collective-permute-done.1.refs_4_.refs_7_.refs_8_ = bf16[512,1024]{1,0:T(8,128)(2,1)S(1)} collective-permute-done((bf16[512,1024]{1,0:T(8,128)(2,1)S(1)}, bf16[512,1024]{1,0:T(8,128)(2,1)S(1)}, u32[]{:S(2)}, u32[]{:S(2)}) %collective-permute-start.1) | collective-permute-done | bytes 1048608 | tf_op jit(solution)/shard_map/ppermute | solution.py:193
  38.1 2.5 fusion.62
  40.6 19.6 %collective-permute-done.3.refs_5_.refs_8_.refs_9_ = bf16[512,1024]{1,0:T(8,128)(2,1)S(1)} collective-permute-done((bf16[512,1024]{1,0:T(8,128)(2,1)S(1)}, bf16[512,1024]{1,0:T(8,128)(2,1)S(1)}, u32[]{:S(2)}, u32[]{:S(2)}) %collective-permute-start.3) | collective-permute-done | bytes 1048608 | tf_op jit(solution)/shard_map/ppermute | solution.py:193
  66.3 1.8 collective-permute-start.8
  68.1 2.1 collective-permute-start.9
  70.7 37.3 %collective-permute-done.11.refs_11_.refs_10_ = bf16[4096,256]{1,0:T(8,128)(2,1)} collective-permute-done((bf16[4096,256]{1,0:T(8,128)(2,1)S(1)}, bf16[4096,256]{1,0:T(8,128)(2,1)}, u32[]{:S(2)}, u32[]{:S(2)}) %collective-permute-start.11) | collective-permute-done | bytes 2097184 | tf_op jit(solution)/shard_map/ppermute | solution.py:193
  108.0 2.6 collective-permute-done.7
  110.6 3.2 %collective-permute-done.9.refs_4_.refs_11_ = bf16[512,1024]{1,0:T(8,128)(2,1)S(1)} collective-permute-done((bf16[512,1024]{1,0:T(8,128)(2,1)S(1)}, bf16[512,1024]{1,0:T(8,128)(2,1)S(1)}, u32[]{:S(2)}, u32[]{:S(2)}) %collective-permute-start.9) | collective-permute-done | bytes 1048608 | tf_op jit(solution)/shard_map/ppermute | solution.py:193
  124.7 19.7 %shard_map.84 = f32[4,512]{1,0:T(4,128)S(1)} custom-call(s32[4]{0:T(128)S(1)} %fusion.55.refs_0_, s32[12]{0:T(128)S(1)} %stack.234.refs_1_, f32[2,512]{1,0:T(2,128)S(1)} %get-tuple-element.53.refs_2_, bf16[1024,1024]{1,0:T(8,128)(2,1)S(1)} %get-tuple-element.45.refs_3_.refs_6_.refs_7_, bf16[512,1024]{1,0:T(8,128)(2,1)S(1)} %collective-permute-done.1.refs_4_.refs_7_.refs_8_, ...), custom_call_target="tpu_custom_call" | custom-call | flops 1048576 | bytes 1024 | tf_op jit(solution)/shard_map/pallas_call | solution.py:143
  144.4 19.8 %shard_map.85 = f32[4,512]{1,0:T(4,128)S(1)} custom-call(s32[4]{0:T(128)S(1)} %fusion.55.refs_0_, s32[12]{0:T(128)S(1)} %stack.234.refs_1_, f32[2,512]{1,0:T(2,128)S(1)} %get-tuple-element.61.refs_2_, bf16[1024,1024]{1,0:T(8,128)(2,1)S(1)} %copy-done.2, bf16[1024,1024]{1,0:T(8,128)(2,1)S(1)} %copy-done.5, ...), custom_call_target="tpu_custom_call" | custom-call | flops 1048576 | bytes 1024 | tf_op jit(solution)/shard_map/pallas_call | solution.py:143
  164.3 2.1 collective-permute-done.16.refs_6_.refs_13_
  168.8 3.0 %collective-permute-start.20 = (bf16[512,1024]{1,0:T(8,128)(2,1)}, bf16[512,1024]{1,0:T(8,128)(2,1)}, u32[]{:S(2)}, u32[]{:S(2)}) collective-permute-start(bf16[512,1024]{1,0:T(8,128)(2,1)} %slice.192), channel_id=1, source_target_pairs={{0,6},{1,7},{2,0},{3,1},{4,2},{5,3},{6,4},{7,5},{8,14},{9,15},{10,... | collective-permute-start | bytes 3145736 | tf_op jit(solution)/shard_map/ppermute | solution.py:193
  173.8 22.6 %shard_map.86 = f32[4,512]{1,0:T(4,128)S(1)} custom-call(s32[4]{0:T(128)S(1)} %fusion.55.refs_0_, s32[14]{0:T(128)S(1)} %stack.239.refs_1_, f32[2,512]{1,0:T(2,128)S(1)} %get-tuple-element.66.refs_2_, bf16[1024,1024]{1,0:T(8,128)(2,1)S(1)} %get-tuple-element.45.refs_3_.refs_6_.refs_7_, bf16[512,1024]{1,0:T(8,128)(2,1)S(1)} %copy-done.13, ...), custom_call_target="tpu_custom_call" | custom-call | flops 1048576 | bytes 1024 | tf_op jit(solution)/shard_map/pallas_call | solution.py:143
  197.1 22.8 %shard_map.87 = f32[4,512]{1,0:T(4,128)S(1)} custom-call(s32[4]{0:T(128)S(1)} %fusion.55.refs_0_, s32[14]{0:T(128)S(1)} %stack.239.refs_1_, f32[2,512]{1,0:T(2,128)S(1)} %get-tuple-element.69.refs_2_, bf16[1024,1024]{1,0:T(8,128)(2,1)S(1)} %copy-done.3, bf16[512,1024]{1,0:T(8,128)(2,1)} %collective-permute-done.18.refs_4_, ...), custom_call_target="tpu_custom_call" | custom-call | flops 1048576 | bytes 1024 | tf_op jit(solution)/shard_map/pallas_call | solution.py:143
  220.4 10.2 %shard_map.88 = f32[4,1024]{1,0:T(4,128)S(1)} custom-call(s32[4]{0:T(128)S(1)} %fusion.55.refs_0_, s32[4]{0:T(128)S(1)} %pad_add_fusion.refs_1_, f32[2,1024]{1,0:T(2,128)S(1)} %pad_maximum_fusion.7.refs_2_, bf16[1024,1024]{1,0:T(8,128)(2,1)} %copy-done.1, bf16[1024,1024]{1,0:T(8,128)(2,1)} %copy-done.4, ...), custom_call_target="tpu_custom_call" | custom-call | flops 1048576 | bytes 1024 | tf_op jit(solution)/shard_map/pallas_call | solution.py:143
  230.8 16.7 %shard_map.89 = f32[4,2048]{1,0:T(4,128)S(1)} custom-call(s32[4]{0:T(128)S(1)} %fusion.55.refs_0_, s32[8]{0:T(128)S(1)} %stack.243.refs_1_, f32[2,2048]{1,0:T(2,128)S(1)} %pad_maximum_fusion.3.refs_2_, bf16[1024,1024]{1,0:T(8,128)(2,1)} %copy-done.1, bf16[512,1024]{1,0:T(8,128)(2,1)} %collective-permute-done.18.refs_4_, ...), custom_call_target="tpu_custom_call" | custom-call | flops 1048576 | bytes 1024 | tf_op jit(solution)/shard_map/pallas_call | solution.py:143
  248.9 3.4 %all-to-all-start = ((f32[8,1,4096]{2,1,0:T(1,128)}), f32[8,1,4096]{2,1,0:T(1,128)S(1)}, u32[]{:S(2)}, u32[]{:S(2)}) async-start(f32[8,1,4096]{2,1,0:T(1,128)} %all_to_all.6), calls=%async_computation | async-start | bytes 262144 | tf_op jit(solution)/shard_map/all_to_all | solution.py:382
  252.9 7.4 %all-to-all-done = f32[8,1,4096]{2,1,0:T(1,128)S(1)} async-done(((f32[8,1,4096]{2,1,0:T(1,128)}), f32[8,1,4096]{2,1,0:T(1,128)S(1)}, u32[]{:S(2)}, u32[]{:S(2)}) %all-to-all-start) | async-done | bytes 131104 | tf_op jit(solution)/shard_map/all_to_all | solution.py:382
  (137 shorter events, 33.7 us)
Async XLA Ops:
  5.4 59.4 %collective-permute-start.6 = (bf16[4096,1024]{1,0:T(8,128)(2,1)}, bf16[4096,1024]{1,0:T(8,128)(2,1)}, u32[]{:S(2)}, u32[]{:S(2)}) collective-permute-start(bf16[4096,1024]{1,0:T(8,128)(2,1)} %refs_7_.5), channel_id=1, source_target_pairs={{0,1},{1,0},{2,3},{3,2},{4,5},{5,4},{6,7},{7,6},{8,9},{9,8},{10,11... | collective-permute-start | bytes 25165832 | tf_op jit(solution)/shard_map/ppermute | solution.py:193
  9.2 28.8 %collective-permute-start.1 = (bf16[512,1024]{1,0:T(8,128)(2,1)S(1)}, bf16[512,1024]{1,0:T(8,128)(2,1)S(1)}, u32[]{:S(2)}, u32[]{:S(2)}) collective-permute-start(bf16[512,1024]{1,0:T(8,128)(2,1)S(1)} %get-tuple-element.42), channel_id=1, source_target_pairs={{0,2},{1,3},{2,4},{3,5},{4,6},{5,7},{6,0},{7,1},{8,10},{9,11},{10,... | collective-permute-start | bytes 3145736 | tf_op jit(solution)/shard_map/ppermute | solution.py:193
  12.3 49.6 %collective-permute-start.5 = (bf16[4096,256]{1,0:T(8,128)(2,1)S(1)}, bf16[4096,256]{1,0:T(8,128)(2,1)}, u32[]{:S(2)}, u32[]{:S(2)}) collective-permute-start(bf16[4096,256]{1,0:T(8,128)(2,1)S(1)} %slice.149), channel_id=1, source_target_pairs={{0,8},{1,9},{2,10},{3,11},{4,12},{5,13},{6,14},{7,15},{8,0},{9,1},... | collective-permute-start | bytes 6291464 | tf_op jit(solution)/shard_map/ppermute | solution.py:193
  14.5 49.0 %collective-permute-start.4 = (bf16[1024,1024]{1,0:T(8,128)(2,1)S(1)}, bf16[1024,1024]{1,0:T(8,128)(2,1)S(1)}, u32[]{:S(2)}, u32[]{:S(2)}) collective-permute-start(bf16[1024,1024]{1,0:T(8,128)(2,1)S(1)} %get-tuple-element.45.refs_3_.refs_6_.refs_7_), channel_id=1, source_target_pairs={{0,16},{1,17},{2,18},{3,19},{4,20},{5,21},{6,22},{7,23},{8,24},{9,... | collective-permute-start | bytes 6291464 | tf_op jit(solution)/shard_map/ppermute | solution.py:193
  16.0 44.2 %collective-permute-start.3 = (bf16[512,1024]{1,0:T(8,128)(2,1)S(1)}, bf16[512,1024]{1,0:T(8,128)(2,1)S(1)}, u32[]{:S(2)}, u32[]{:S(2)}) collective-permute-start(bf16[512,1024]{1,0:T(8,128)(2,1)S(1)} %get-tuple-element.42), channel_id=1, source_target_pairs={{0,6},{1,7},{2,0},{3,1},{4,2},{5,3},{6,4},{7,5},{8,14},{9,15},{10,... | collective-permute-start | bytes 3145736 | tf_op jit(solution)/shard_map/ppermute | solution.py:193
  38.1 25.4 %collective-permute-start.2 = (f32[1,1024]{1,0:T(1,128)S(1)}, f32[1,1024]{1,0:T(1,128)S(1)}, u32[]{:S(2)}, u32[]{:S(2)}) collective-permute-start(f32[1,1024]{1,0:T(1,128)S(1)} %bitcast.195), channel_id=1, source_target_pairs={{0,2},{1,3},{2,4},{3,5},{4,6},{5,7},{6,0},{7,1},{8,10},{9,11},{10,... | collective-permute-start | bytes 12296 | tf_op jit(solution)/shard_map/ppermute | solution.py:193
  60.2 47.8 %collective-permute-start.11 = (bf16[4096,256]{1,0:T(8,128)(2,1)S(1)}, bf16[4096,256]{1,0:T(8,128)(2,1)}, u32[]{:S(2)}, u32[]{:S(2)}) collective-permute-start(bf16[4096,256]{1,0:T(8,128)(2,1)S(1)} %get-tuple-element.104), channel_id=1, source_target_pairs={{0,8},{1,9},{2,10},{3,11},{4,12},{5,13},{6,14},{7,15},{8,0},{9,1},... | collective-permute-start | bytes 6291464 | tf_op jit(solution)/shard_map/ppermute | solution.py:193
  64.8 49.0 %collective-permute-start.10 = (bf16[1024,1024]{1,0:T(8,128)(2,1)S(1)}, bf16[1024,1024]{1,0:T(8,128)(2,1)S(1)}, u32[]{:S(2)}, u32[]{:S(2)}) collective-permute-start(bf16[1024,1024]{1,0:T(8,128)(2,1)S(1)} %pad_maximum_fusion), channel_id=1, source_target_pairs={{0,16},{1,17},{2,18},{3,19},{4,20},{5,21},{6,22},{7,23},{8,24},{9,... | collective-permute-start | bytes 6291464 | tf_op jit(solution)/shard_map/ppermute | solution.py:193
  66.3 44.3 %collective-permute-start.8 = (bf16[512,1024]{1,0:T(8,128)(2,1)S(1)}, bf16[512,1024]{1,0:T(8,128)(2,1)S(1)}, u32[]{:S(2)}, u32[]{:S(2)}) collective-permute-start(bf16[512,1024]{1,0:T(8,128)(2,1)S(1)} %collective-permute-done.1.refs_4_.refs_7_.refs_8_), channel_id=1, source_target_pairs={{0,2},{1,3},{2,4},{3,5},{4,6},{5,7},{6,0},{7,1},{8,10},{9,11},{10,... | collective-permute-start | bytes 3145736 | tf_op jit(solution)/shard_map/ppermute | solution.py:193
  68.1 45.7 %collective-permute-start.9 = (bf16[512,1024]{1,0:T(8,128)(2,1)S(1)}, bf16[512,1024]{1,0:T(8,128)(2,1)S(1)}, u32[]{:S(2)}, u32[]{:S(2)}) collective-permute-start(bf16[512,1024]{1,0:T(8,128)(2,1)S(1)} %get-tuple-element.58), channel_id=1, source_target_pairs={{0,2},{1,3},{2,4},{3,5},{4,6},{5,7},{6,0},{7,1},{8,10},{9,11},{10,... | collective-permute-start | bytes 3145736 | tf_op jit(solution)/shard_map/ppermute | solution.py:193
  70.2 40.4 %collective-permute-start.7 = (f32[1,1024]{1,0:T(1,128)S(1)}, f32[1,1024]{1,0:T(1,128)S(1)}, u32[]{:S(2)}, u32[]{:S(2)}) collective-permute-start(f32[1,1024]{1,0:T(1,128)S(1)} %add.284), channel_id=1, source_target_pairs={{0,4},{1,5},{2,6},{3,7},{4,0},{5,1},{6,2},{7,3},{8,12},{9,13},{10,... | collective-permute-start | bytes 12296 | tf_op jit(solution)/shard_map/ppermute | solution.py:193
  108.0 10.7 %collective-permute-start.12 = (bf16[4096,256]{1,0:T(8,128)(2,1)}, bf16[4096,256]{1,0:T(8,128)(2,1)}, u32[]{:S(2)}, u32[]{:S(2)}) collective-permute-start(bf16[4096,256]{1,0:T(8,128)(2,1)} %collective-permute-done.5.refs_9_.refs_8_), channel_id=1, source_target_pairs={{0,1},{1,0},{2,3},{3,2},{4,5},{5,4},{6,7},{7,6},{8,9},{9,8},{10,11... | collective-permute-start | bytes 6291464 | tf_op jit(solution)/shard_map/ppermute | solution.py:193
  115.2 6.5 %collective-permute-start.13 = (bf16[4096,256]{1,0:T(8,128)(2,1)}, bf16[4096,256]{1,0:T(8,128)(2,1)}, u32[]{:S(2)}, u32[]{:S(2)}) collective-permute-start(bf16[4096,256]{1,0:T(8,128)(2,1)} %collective-permute-done.11.refs_11_.refs_10_), channel_id=1, source_target_pairs={{0,1},{1,0},{2,3},{3,2},{4,5},{5,4},{6,7},{7,6},{8,9},{9,8},{10,11... | collective-permute-start | bytes 6291464 | tf_op jit(solution)/shard_map/ppermute | solution.py:193
  115.5 48.8 %collective-permute-start.19 = (bf16[4096,256]{1,0:T(8,128)(2,1)}, bf16[4096,256]{1,0:T(8,128)(2,1)}, u32[]{:S(2)}, u32[]{:S(2)}) collective-permute-start(bf16[4096,256]{1,0:T(8,128)(2,1)} %get-tuple-element.62), channel_id=1, source_target_pairs={{0,8},{1,9},{2,10},{3,11},{4,12},{5,13},{6,14},{7,15},{8,0},{9,1},... | collective-permute-start | bytes 6291464 | tf_op jit(solution)/shard_map/ppermute | solution.py:193
  117.2 27.2 %collective-permute-start.17 = (bf16[512,1024]{1,0:T(8,128)(2,1)}, bf16[512,1024]{1,0:T(8,128)(2,1)}, u32[]{:S(2)}, u32[]{:S(2)}) collective-permute-start(bf16[512,1024]{1,0:T(8,128)(2,1)} %copy-done.9), channel_id=1, source_target_pairs={{0,16},{1,17},{2,18},{3,19},{4,20},{5,21},{6,22},{7,23},{8,24},{9,... | collective-permute-start | bytes 3145736 | tf_op jit(solution)/shard_map/ppermute | solution.py:193
  118.7 45.6 %collective-permute-start.15 = (bf16[512,1024]{1,0:T(8,128)(2,1)}, bf16[512,1024]{1,0:T(8,128)(2,1)}, u32[]{:S(2)}, u32[]{:S(2)}) collective-permute-start(bf16[512,1024]{1,0:T(8,128)(2,1)} %copy-done.15), channel_id=1, source_target_pairs={{0,6},{1,7},{2,0},{3,1},{4,2},{5,3},{6,4},{7,5},{8,14},{9,15},{10,... | collective-permute-start | bytes 3145736 | tf_op jit(solution)/shard_map/ppermute | solution.py:193
  120.4 46.0 %collective-permute-start.16 = (bf16[512,1024]{1,0:T(8,128)(2,1)}, bf16[512,1024]{1,0:T(8,128)(2,1)}, u32[]{:S(2)}, u32[]{:S(2)}) collective-permute-start(bf16[512,1024]{1,0:T(8,128)(2,1)} %copy-done.12), channel_id=1, source_target_pairs={{0,2},{1,3},{2,4},{3,5},{4,6},{5,7},{6,0},{7,1},{8,10},{9,11},{10,... | collective-permute-start | bytes 3145736 | tf_op jit(solution)/shard_map/ppermute | solution.py:193
  121.7 44.7 %collective-permute-start.18 = (bf16[512,1024]{1,0:T(8,128)(2,1)}, bf16[512,1024]{1,0:T(8,128)(2,1)}, u32[]{:S(2)}, u32[]{:S(2)}) collective-permute-start(bf16[512,1024]{1,0:T(8,128)(2,1)} %copy-done.12), channel_id=1, source_target_pairs={{0,16},{1,17},{2,18},{3,19},{4,20},{5,21},{6,22},{7,23},{8,24},{9,... | collective-permute-start | bytes 3145736 | tf_op jit(solution)/shard_map/ppermute | solution.py:193
  166.4 6.0 %collective-permute-start.22 = (bf16[4096,256]{1,0:T(8,128)(2,1)}, bf16[4096,256]{1,0:T(8,128)(2,1)}, u32[]{:S(2)}, u32[]{:S(2)}) collective-permute-start(bf16[4096,256]{1,0:T(8,128)(2,1)} %collective-permute-done.19.refs_13_.refs_10_), channel_id=1, source_target_pairs={{0,1},{1,0},{2,3},{3,2},{4,5},{5,4},{6,7},{7,6},{8,9},{9,8},{10,11... | collective-permute-start | bytes 6291464 | tf_op jit(solution)/shard_map/ppermute | solution.py:193
  166.4 53.5 %collective-permute-start.23 = (bf16[4096,256]{1,0:T(8,128)(2,1)}, bf16[4096,256]{1,0:T(8,128)(2,1)}, u32[]{:S(2)}, u32[]{:S(2)}) collective-permute-start(bf16[4096,256]{1,0:T(8,128)(2,1)} %get-tuple-element.74), channel_id=1, source_target_pairs={{0,8},{1,9},{2,10},{3,11},{4,12},{5,13},{6,14},{7,15},{8,0},{9,1},... | collective-permute-start | bytes 6291464 | tf_op jit(solution)/shard_map/ppermute | solution.py:193
  168.8 27.6 %collective-permute-start.20 = (bf16[512,1024]{1,0:T(8,128)(2,1)}, bf16[512,1024]{1,0:T(8,128)(2,1)}, u32[]{:S(2)}, u32[]{:S(2)}) collective-permute-start(bf16[512,1024]{1,0:T(8,128)(2,1)} %slice.192), channel_id=1, source_target_pairs={{0,6},{1,7},{2,0},{3,1},{4,2},{5,3},{6,4},{7,5},{8,14},{9,15},{10,... | collective-permute-start | bytes 3145736 | tf_op jit(solution)/shard_map/ppermute | solution.py:193
  171.8 25.3 %collective-permute-start.21 = (bf16[512,1024]{1,0:T(8,128)(2,1)}, bf16[512,1024]{1,0:T(8,128)(2,1)}, u32[]{:S(2)}, u32[]{:S(2)}) collective-permute-start(bf16[512,1024]{1,0:T(8,128)(2,1)} %collective-permute-done.16.refs_6_.refs_13_), channel_id=1, source_target_pairs={{0,16},{1,17},{2,18},{3,19},{4,20},{5,21},{6,22},{7,23},{8,24},{9,... | collective-permute-start | bytes 3145736 | tf_op jit(solution)/shard_map/ppermute | solution.py:193
  219.9 10.8 %collective-permute-start.24 = (bf16[4096,256]{1,0:T(8,128)(2,1)}, bf16[4096,256]{1,0:T(8,128)(2,1)}, u32[]{:S(2)}, u32[]{:S(2)}) collective-permute-start(bf16[4096,256]{1,0:T(8,128)(2,1)} %collective-permute-done.23.refs_16_), channel_id=1, source_target_pairs={{0,1},{1,0},{2,3},{3,2},{4,5},{5,4},{6,7},{7,6},{8,9},{9,8},{10,11... | collective-permute-start | bytes 6291464 | tf_op jit(solution)/shard_map/ppermute | solution.py:193
  248.9 11.4 %all-to-all-start = ((f32[8,1,4096]{2,1,0:T(1,128)}), f32[8,1,4096]{2,1,0:T(1,128)S(1)}, u32[]{:S(2)}, u32[]{:S(2)}) async-start(f32[8,1,4096]{2,1,0:T(1,128)} %all_to_all.6), calls=%async_computation | async-start | bytes 262144 | tf_op jit(solution)/shard_map/all_to_all | solution.py:382
  (21 other events, 438.8 us)

commit v5 on v4

--- a/solution.py
+++ b/solution.py
@@ -241,6 +241,11 @@
     ya, yb, far_near = {}, {}, []
     step_ends(other)
     near = to_core(after(head))
+
+    seq_lens = lengths[0, :-1]
+    stops = jnp.cumsum(seq_lens)
+    starts = stops - seq_lens
+    live_rows = jnp.sum(seq_lens)
 
     trip = [0] + [j for k in range(1, spots // 2 + 1) for j in dict.fromkeys((k, spots - k))]
     z_list = [(ring, j) for ring in (a, b) for j in trip[1:]]
@@ -324,7 +329,8 @@
         if step == n_steps - 1:
             for _, out, j in [y for y in y_list if y[2] > spots // 2]:
                 array, at = out[(j + 1) % spots]
-                out[j] = (to_z(after(array[at : at + n_a]), -1), 0)
+                block = first_yb if (j + 1) % spots == 0 else array[at : at + n_a]
+                out[j] = (to_z(after(block), -1), 0)
                 ends.append(out[j][0])
             y_list = [y for y in y_list if y[2] <= spots // 2]
         batch = [y_list.pop(0) for _ in range(len(y_list) if step == n_steps - 1 else min(stage, len(y_list)))]
@@ -354,6 +360,11 @@
             ends.append(call(("E", [0, 1, 2] if many else [0])))
         if step == 3:
             ends.append(call(("B", [0, 1, 2, 3] if many else [0])))
+        if step == 0:
+            ends += [stops, starts, live_rows]
+        if step == n_steps - 2:
+            first_yb = after(yb[0][0][yb[0][1] : yb[0][1] + n_a])
+            ends.append(first_yb)
         if step < n_steps - 1:
             ends.append(far[min(step, n_far - 1)])
         if step == 0:
@@ -386,19 +397,15 @@
     log_total = peak + jnp.log(total)
     lp, ent = picked - log_total, log_total - moment / total
 
-    seq_lens = lengths[0, :-1]
-    stops = jnp.cumsum(seq_lens)
-    starts = stops - seq_lens
     local = jnp.arange(half, dtype=jnp.int32)
     local = (local // blk * 2 + c) * blk + local % blk
-    valid = local < stops[-1]
-    lp = jnp.where(valid, lp, 0.0)
-    ent = jnp.where(valid, ent, 0.0)
     member = (local[None, :] >= starts[:, None]) & (local[None, :] < stops[:, None])
-    sums = jnp.sum(jnp.where(member[None], jnp.stack([lp, ent])[:, None, :], 0.0), axis=2)
+    both = jnp.stack([lp, ent])
+    sums = jnp.sum(jnp.where(member[None], both[:, None, :], 0.0), axis=2)
+    both = lax.optimization_barrier((both, sums))[0]
+    valid = v * blk + jnp.arange(blk, dtype=jnp.int32) < live_rows
+    lp, ent = jnp.where(valid[None], lax.dynamic_slice_in_dim(both, s * blk, blk, axis=1), 0.0)
     sums = sums + to_core(sums)
-    lp = lax.dynamic_slice_in_dim(lp, s * blk, blk)
-    ent = lax.dynamic_slice_in_dim(ent, s * blk, blk)
     means = sums / seq_lens.astype(jnp.float32)[None]
     return (lp, ent, means[0], means[1])
 

time: 266 us -> 262 us (0.985)
  transfers between devices with their start and end apart: 27 -> 27, of which waited for: 11 -> 11; matrix products, arithmetic and copies ran while one was open for 3% -> 4% of each run, Pallas kernels for 36% -> 36%
where the time goes in v5:
time: 262 us
  Pallas kernels  112 us (43%)
  waiting for transfers between devices  95.5 us (36%)
  starting transfers between devices  33.2 us (13%)
  local copies, waits for them, and re-layouts  13.9 us (5%)
  other arithmetic  6.04 us (2%)
    pallas_call x6, Pallas kernels, stats(): pl.pallas_call(functools.partial(stats_kernel, tiles, len(pieces), len(he...  112 us
    ppermute x26, waiting for transfers between devices, move(): return lax.ppermute(x, every, pairs)  88.1 us
    ppermute x26, starting transfers between devices, move(): return lax.ppermute(x, every, pairs)  29.9 us
    all_to_all x1, waiting for transfers between devices, shards(): lax.all_to_all(whole.reshape(2 * spots, 4 * half), every, split_axis=0, c...  7.39 us
  transfers between devices with their start and end apart: 27, of which 11 were waited for; matrix products, arithmetic and copies ran while one was open for 4% of the time, Pallas kernels for 36%

profile of v5, /device:TPU:0, one launch (start us, length us, event | category | flops | bytes accessed | tf_op | source)
XLA Modules:
  0.0 261.9 jit_solution(3842600801446609677)
XLA Ops:
  0.7 1.8 constant_dynamic-slice_fusion.1
  3.0 2.4 collective-permute-done
  6.4 2.6 fusion.1
  9.2 2.8 %collective-permute-start.1 = (bf16[512,1024]{1,0:T(8,128)(2,1)S(1)}, bf16[512,1024]{1,0:T(8,128)(2,1)S(1)}, u32[]{:S(2)}, u32[]{:S(2)}) collective-permute-start(bf16[512,1024]{1,0:T(8,128)(2,1)S(1)} %get-tuple-element.44), channel_id=1, source_target_pairs={{0,2},{1,3},{2,4},{3,5},{4,6},{5,7},{6,0},{7,1},{8,10},{9,11},{10,... | collective-permute-start | bytes 3145736 | tf_op jit(solution)/shard_map/ppermute | solution.py:193
  12.3 2.2 collective-permute-start.5
  16.6 3.6 %collective-permute-start.3 = (bf16[512,1024]{1,0:T(8,128)(2,1)S(1)}, bf16[512,1024]{1,0:T(8,128)(2,1)S(1)}, u32[]{:S(2)}, u32[]{:S(2)}) collective-permute-start(bf16[512,1024]{1,0:T(8,128)(2,1)S(1)} %get-tuple-element.44), channel_id=1, source_target_pairs={{0,6},{1,7},{2,0},{3,1},{4,2},{5,3},{6,4},{7,5},{8,14},{9,15},{10,... | collective-permute-start | bytes 3145736 | tf_op jit(solution)/shard_map/ppermute | solution.py:193
  20.2 17.8 %collective-permute-done.1.refs_4_.refs_7_.refs_8_ = bf16[512,1024]{1,0:T(8,128)(2,1)S(1)} collective-permute-done((bf16[512,1024]{1,0:T(8,128)(2,1)S(1)}, bf16[512,1024]{1,0:T(8,128)(2,1)S(1)}, u32[]{:S(2)}, u32[]{:S(2)}) %collective-permute-start.1) | collective-permute-done | bytes 1048608 | tf_op jit(solution)/shard_map/ppermute | solution.py:193
  38.1 2.3 fusion.57
  40.4 19.8 %collective-permute-done.3.refs_5_.refs_8_.refs_9_ = bf16[512,1024]{1,0:T(8,128)(2,1)S(1)} collective-permute-done((bf16[512,1024]{1,0:T(8,128)(2,1)S(1)}, bf16[512,1024]{1,0:T(8,128)(2,1)S(1)}, u32[]{:S(2)}, u32[]{:S(2)}) %collective-permute-start.3) | collective-permute-done | bytes 1048608 | tf_op jit(solution)/shard_map/ppermute | solution.py:193
  67.9 2.1 collective-permute-start.9
  70.7 37.3 %collective-permute-done.11.refs_11_.refs_10_ = bf16[4096,256]{1,0:T(8,128)(2,1)} collective-permute-done((bf16[4096,256]{1,0:T(8,128)(2,1)S(1)}, bf16[4096,256]{1,0:T(8,128)(2,1)}, u32[]{:S(2)}, u32[]{:S(2)}) %collective-permute-start.11) | collective-permute-done | bytes 2097184 | tf_op jit(solution)/shard_map/ppermute | solution.py:193
  108.0 2.6 collective-permute-done.7
  110.6 3.2 %collective-permute-done.9.refs_4_.refs_11_ = bf16[512,1024]{1,0:T(8,128)(2,1)S(1)} collective-permute-done((bf16[512,1024]{1,0:T(8,128)(2,1)S(1)}, bf16[512,1024]{1,0:T(8,128)(2,1)S(1)}, u32[]{:S(2)}, u32[]{:S(2)}) %collective-permute-start.9) | collective-permute-done | bytes 1048608 | tf_op jit(solution)/shard_map/ppermute | solution.py:193
  122.2 2.4 slice.187
  124.7 19.7 %shard_map.84 = f32[4,512]{1,0:T(4,128)S(1)} custom-call(s32[4]{0:T(128)S(1)} %fusion.51.refs_0_, s32[12]{0:T(128)S(1)} %stack.234.refs_1_, f32[2,512]{1,0:T(2,128)S(1)} %get-tuple-element.55.refs_2_, bf16[1024,1024]{1,0:T(8,128)(2,1)S(1)} %get-tuple-element.47.refs_3_.refs_6_.refs_7_, bf16[512,1024]{1,0:T(8,128)(2,1)S(1)} %collective-permute-done.1.refs_4_.refs_7_.refs_8_, ...), custom_call_target="tpu_custom_call" | custom-call | flops 1048576 | bytes 1024 | tf_op jit(solution)/shard_map/pallas_call | solution.py:143
  144.5 19.8 %shard_map.85 = f32[4,512]{1,0:T(4,128)S(1)} custom-call(s32[4]{0:T(128)S(1)} %fusion.51.refs_0_, s32[12]{0:T(128)S(1)} %stack.234.refs_1_, f32[2,512]{1,0:T(2,128)S(1)} %get-tuple-element.63.refs_2_, bf16[1024,1024]{1,0:T(8,128)(2,1)S(1)} %copy-done.2, bf16[1024,1024]{1,0:T(8,128)(2,1)S(1)} %copy-done.5, ...), custom_call_target="tpu_custom_call" | custom-call | flops 1048576 | bytes 1024 | tf_op jit(solution)/shard_map/pallas_call | solution.py:143
  164.3 2.1 collective-permute-done.16.refs_6_.refs_13_
  167.7 3.0 %collective-permute-start.20 = (bf16[512,1024]{1,0:T(8,128)(2,1)}, bf16[512,1024]{1,0:T(8,128)(2,1)}, u32[]{:S(2)}, u32[]{:S(2)}) collective-permute-start(bf16[512,1024]{1,0:T(8,128)(2,1)} %slice.187), channel_id=1, source_target_pairs={{0,6},{1,7},{2,0},{3,1},{4,2},{5,3},{6,4},{7,5},{8,14},{9,15},{10,... | collective-permute-start | bytes 3145736 | tf_op jit(solution)/shard_map/ppermute | solution.py:193
  172.7 22.6 %shard_map.86 = f32[4,512]{1,0:T(4,128)S(1)} custom-call(s32[4]{0:T(128)S(1)} %fusion.51.refs_0_, s32[14]{0:T(128)S(1)} %stack.239.refs_1_, f32[2,512]{1,0:T(2,128)S(1)} %get-tuple-element.69.refs_2_, bf16[1024,1024]{1,0:T(8,128)(2,1)S(1)} %get-tuple-element.47.refs_3_.refs_6_.refs_7_, bf16[512,1024]{1,0:T(8,128)(2,1)S(1)} %copy-done.13, ...), custom_call_target="tpu_custom_call" | custom-call | flops 1048576 | bytes 1024 | tf_op jit(solution)/shard_map/pallas_call | solution.py:143
  196.1 22.8 %shard_map.87 = f32[4,512]{1,0:T(4,128)S(1)} custom-call(s32[4]{0:T(128)S(1)} %fusion.51.refs_0_, s32[14]{0:T(128)S(1)} %stack.239.refs_1_, f32[2,512]{1,0:T(2,128)S(1)} %get-tuple-element.72.refs_2_, bf16[1024,1024]{1,0:T(8,128)(2,1)S(1)} %copy-done.3, bf16[512,1024]{1,0:T(8,128)(2,1)} %collective-permute-done.18.refs_4_, ...), custom_call_target="tpu_custom_call" | custom-call | flops 1048576 | bytes 1024 | tf_op jit(solution)/shard_map/pallas_call | solution.py:143
  219.4 10.2 %shard_map.88 = f32[4,1024]{1,0:T(4,128)S(1)} custom-call(s32[4]{0:T(128)S(1)} %fusion.51.refs_0_, s32[4]{0:T(128)S(1)} %pad_add_fusion.refs_1_, f32[2,1024]{1,0:T(2,128)S(1)} %pad_maximum_fusion.7.refs_2_, bf16[1024,1024]{1,0:T(8,128)(2,1)} %copy-done.1, bf16[1024,1024]{1,0:T(8,128)(2,1)} %copy-done.4, ...), custom_call_target="tpu_custom_call" | custom-call | flops 1048576 | bytes 1024 | tf_op jit(solution)/shard_map/pallas_call | solution.py:143
  229.7 16.7 %shard_map.89 = f32[4,2048]{1,0:T(4,128)S(1)} custom-call(s32[4]{0:T(128)S(1)} %fusion.51.refs_0_, s32[8]{0:T(128)S(1)} %stack.243.refs_1_, f32[2,2048]{1,0:T(2,128)S(1)} %pad_maximum_fusion.3.refs_2_, bf16[1024,1024]{1,0:T(8,128)(2,1)} %copy-done.1, bf16[512,1024]{1,0:T(8,128)(2,1)} %collective-permute-done.18.refs_4_, ...), custom_call_target="tpu_custom_call" | custom-call | flops 1048576 | bytes 1024 | tf_op jit(solution)/shard_map/pallas_call | solution.py:143
  247.8 3.4 %all-to-all-start = ((f32[8,1,4096]{2,1,0:T(1,128)}), f32[8,1,4096]{2,1,0:T(1,128)S(1)}, u32[]{:S(2)}, u32[]{:S(2)}) async-start(f32[8,1,4096]{2,1,0:T(1,128)} %all_to_all.6), calls=%async_computation | async-start | bytes 262144 | tf_op jit(solution)/shard_map/all_to_all | solution.py:393
  251.8 7.4 %all-to-all-done = f32[8,1,4096]{2,1,0:T(1,128)S(1)} async-done(((f32[8,1,4096]{2,1,0:T(1,128)}), f32[8,1,4096]{2,1,0:T(1,128)S(1)}, u32[]{:S(2)}, u32[]{:S(2)}) %all-to-all-start) | async-done | bytes 131104 | tf_op jit(solution)/shard_map/all_to_all | solution.py:393
  (134 shorter events, 29.9 us)
Async XLA Ops:
  5.4 59.4 %collective-permute-start.6 = (bf16[4096,1024]{1,0:T(8,128)(2,1)}, bf16[4096,1024]{1,0:T(8,128)(2,1)}, u32[]{:S(2)}, u32[]{:S(2)}) collective-permute-start(bf16[4096,1024]{1,0:T(8,128)(2,1)} %refs_7_.5), channel_id=1, source_target_pairs={{0,1},{1,0},{2,3},{3,2},{4,5},{5,4},{6,7},{7,6},{8,9},{9,8},{10,11... | collective-permute-start | bytes 25165832 | tf_op jit(solution)/shard_map/ppermute | solution.py:193
  9.2 28.8 %collective-permute-start.1 = (bf16[512,1024]{1,0:T(8,128)(2,1)S(1)}, bf16[512,1024]{1,0:T(8,128)(2,1)S(1)}, u32[]{:S(2)}, u32[]{:S(2)}) collective-permute-start(bf16[512,1024]{1,0:T(8,128)(2,1)S(1)} %get-tuple-element.44), channel_id=1, source_target_pairs={{0,2},{1,3},{2,4},{3,5},{4,6},{5,7},{6,0},{7,1},{8,10},{9,11},{10,... | collective-permute-start | bytes 3145736 | tf_op jit(solution)/shard_map/ppermute | solution.py:193
  12.3 49.6 %collective-permute-start.5 = (bf16[4096,256]{1,0:T(8,128)(2,1)S(1)}, bf16[4096,256]{1,0:T(8,128)(2,1)}, u32[]{:S(2)}, u32[]{:S(2)}) collective-permute-start(bf16[4096,256]{1,0:T(8,128)(2,1)S(1)} %slice.144), channel_id=1, source_target_pairs={{0,8},{1,9},{2,10},{3,11},{4,12},{5,13},{6,14},{7,15},{8,0},{9,1},... | collective-permute-start | bytes 6291464 | tf_op jit(solution)/shard_map/ppermute | solution.py:193
  14.5 49.0 %collective-permute-start.4 = (bf16[1024,1024]{1,0:T(8,128)(2,1)S(1)}, bf16[1024,1024]{1,0:T(8,128)(2,1)S(1)}, u32[]{:S(2)}, u32[]{:S(2)}) collective-permute-start(bf16[1024,1024]{1,0:T(8,128)(2,1)S(1)} %get-tuple-element.47.refs_3_.refs_6_.refs_7_), channel_id=1, source_target_pairs={{0,16},{1,17},{2,18},{3,19},{4,20},{5,21},{6,22},{7,23},{8,24},{9,... | collective-permute-start | bytes 6291464 | tf_op jit(solution)/shard_map/ppermute | solution.py:193
  16.6 43.6 %collective-permute-start.3 = (bf16[512,1024]{1,0:T(8,128)(2,1)S(1)}, bf16[512,1024]{1,0:T(8,128)(2,1)S(1)}, u32[]{:S(2)}, u32[]{:S(2)}) collective-permute-start(bf16[512,1024]{1,0:T(8,128)(2,1)S(1)} %get-tuple-element.44), channel_id=1, source_target_pairs={{0,6},{1,7},{2,0},{3,1},{4,2},{5,3},{6,4},{7,5},{8,14},{9,15},{10,... | collective-permute-start | bytes 3145736 | tf_op jit(solution)/shard_map/ppermute | solution.py:193
  38.1 25.4 %collective-permute-start.2 = (f32[1,1024]{1,0:T(1,128)S(1)}, f32[1,1024]{1,0:T(1,128)S(1)}, u32[]{:S(2)}, u32[]{:S(2)}) collective-permute-start(f32[1,1024]{1,0:T(1,128)S(1)} %bitcast.196), channel_id=1, source_target_pairs={{0,2},{1,3},{2,4},{3,5},{4,6},{5,7},{6,0},{7,1},{8,10},{9,11},{10,... | collective-permute-start | bytes 12296 | tf_op jit(solution)/shard_map/ppermute | solution.py:193
  60.2 47.8 %collective-permute-start.11 = (bf16[4096,256]{1,0:T(8,128)(2,1)S(1)}, bf16[4096,256]{1,0:T(8,128)(2,1)}, u32[]{:S(2)}, u32[]{:S(2)}) collective-permute-start(bf16[4096,256]{1,0:T(8,128)(2,1)S(1)} %get-tuple-element.104), channel_id=1, source_target_pairs={{0,8},{1,9},{2,10},{3,11},{4,12},{5,13},{6,14},{7,15},{8,0},{9,1},... | collective-permute-start | bytes 6291464 | tf_op jit(solution)/shard_map/ppermute | solution.py:193
  64.8 49.0 %collective-permute-start.10 = (bf16[1024,1024]{1,0:T(8,128)(2,1)S(1)}, bf16[1024,1024]{1,0:T(8,128)(2,1)S(1)}, u32[]{:S(2)}, u32[]{:S(2)}) collective-permute-start(bf16[1024,1024]{1,0:T(8,128)(2,1)S(1)} %pad_maximum_fusion), channel_id=1, source_target_pairs={{0,16},{1,17},{2,18},{3,19},{4,20},{5,21},{6,22},{7,23},{8,24},{9,... | collective-permute-start | bytes 6291464 | tf_op jit(solution)/shard_map/ppermute | solution.py:193
  66.3 44.3 %collective-permute-start.8 = (bf16[512,1024]{1,0:T(8,128)(2,1)S(1)}, bf16[512,1024]{1,0:T(8,128)(2,1)S(1)}, u32[]{:S(2)}, u32[]{:S(2)}) collective-permute-start(bf16[512,1024]{1,0:T(8,128)(2,1)S(1)} %collective-permute-done.1.refs_4_.refs_7_.refs_8_), channel_id=1, source_target_pairs={{0,2},{1,3},{2,4},{3,5},{4,6},{5,7},{6,0},{7,1},{8,10},{9,11},{10,... | collective-permute-start | bytes 3145736 | tf_op jit(solution)/shard_map/ppermute | solution.py:193
  67.9 45.9 %collective-permute-start.9 = (bf16[512,1024]{1,0:T(8,128)(2,1)S(1)}, bf16[512,1024]{1,0:T(8,128)(2,1)S(1)}, u32[]{:S(2)}, u32[]{:S(2)}) collective-permute-start(bf16[512,1024]{1,0:T(8,128)(2,1)S(1)} %get-tuple-element.60), channel_id=1, source_target_pairs={{0,2},{1,3},{2,4},{3,5},{4,6},{5,7},{6,0},{7,1},{8,10},{9,11},{10,... | collective-permute-start | bytes 3145736 | tf_op jit(solution)/shard_map/ppermute | solution.py:193
  70.0 40.6 %collective-permute-start.7 = (f32[1,1024]{1,0:T(1,128)S(1)}, f32[1,1024]{1,0:T(1,128)S(1)}, u32[]{:S(2)}, u32[]{:S(2)}) collective-permute-start(f32[1,1024]{1,0:T(1,128)S(1)} %add.243), channel_id=1, source_target_pairs={{0,4},{1,5},{2,6},{3,7},{4,0},{5,1},{6,2},{7,3},{8,12},{9,13},{10,... | collective-permute-start | bytes 12296 | tf_op jit(solution)/shard_map/ppermute | solution.py:193
  108.0 10.7 %collective-permute-start.12 = (bf16[4096,256]{1,0:T(8,128)(2,1)}, bf16[4096,256]{1,0:T(8,128)(2,1)}, u32[]{:S(2)}, u32[]{:S(2)}) collective-permute-start(bf16[4096,256]{1,0:T(8,128)(2,1)} %collective-permute-done.5.refs_9_.refs_8_), channel_id=1, source_target_pairs={{0,1},{1,0},{2,3},{3,2},{4,5},{5,4},{6,7},{7,6},{8,9},{9,8},{10,11... | collective-permute-start | bytes 6291464 | tf_op jit(solution)/shard_map/ppermute | solution.py:193
  115.2 6.5 %collective-permute-start.13 = (bf16[4096,256]{1,0:T(8,128)(2,1)}, bf16[4096,256]{1,0:T(8,128)(2,1)}, u32[]{:S(2)}, u32[]{:S(2)}) collective-permute-start(bf16[4096,256]{1,0:T(8,128)(2,1)} %collective-permute-done.11.refs_11_.refs_10_), channel_id=1, source_target_pairs={{0,1},{1,0},{2,3},{3,2},{4,5},{5,4},{6,7},{7,6},{8,9},{9,8},{10,11... | collective-permute-start | bytes 6291464 | tf_op jit(solution)/shard_map/ppermute | solution.py:193
  115.5 48.8 %collective-permute-start.19 = (bf16[4096,256]{1,0:T(8,128)(2,1)}, bf16[4096,256]{1,0:T(8,128)(2,1)}, u32[]{:S(2)}, u32[]{:S(2)}) collective-permute-start(bf16[4096,256]{1,0:T(8,128)(2,1)} %get-tuple-element.65), channel_id=1, source_target_pairs={{0,8},{1,9},{2,10},{3,11},{4,12},{5,13},{6,14},{7,15},{8,0},{9,1},... | collective-permute-start | bytes 6291464 | tf_op jit(solution)/shard_map/ppermute | solution.py:193
  117.2 27.3 %collective-permute-start.17 = (bf16[512,1024]{1,0:T(8,128)(2,1)}, bf16[512,1024]{1,0:T(8,128)(2,1)}, u32[]{:S(2)}, u32[]{:S(2)}) collective-permute-start(bf16[512,1024]{1,0:T(8,128)(2,1)} %copy-done.9), channel_id=1, source_target_pairs={{0,16},{1,17},{2,18},{3,19},{4,20},{5,21},{6,22},{7,23},{8,24},{9,... | collective-permute-start | bytes 3145736 | tf_op jit(solution)/shard_map/ppermute | solution.py:193
  118.7 45.6 %collective-permute-start.15 = (bf16[512,1024]{1,0:T(8,128)(2,1)}, bf16[512,1024]{1,0:T(8,128)(2,1)}, u32[]{:S(2)}, u32[]{:S(2)}) collective-permute-start(bf16[512,1024]{1,0:T(8,128)(2,1)} %copy-done.15), channel_id=1, source_target_pairs={{0,6},{1,7},{2,0},{3,1},{4,2},{5,3},{6,4},{7,5},{8,14},{9,15},{10,... | collective-permute-start | bytes 3145736 | tf_op jit(solution)/shard_map/ppermute | solution.py:193
  120.4 46.0 %collective-permute-start.16 = (bf16[512,1024]{1,0:T(8,128)(2,1)}, bf16[512,1024]{1,0:T(8,128)(2,1)}, u32[]{:S(2)}, u32[]{:S(2)}) collective-permute-start(bf16[512,1024]{1,0:T(8,128)(2,1)} %copy-done.12), channel_id=1, source_target_pairs={{0,2},{1,3},{2,4},{3,5},{4,6},{5,7},{6,0},{7,1},{8,10},{9,11},{10,... | collective-permute-start | bytes 3145736 | tf_op jit(solution)/shard_map/ppermute | solution.py:193
  121.7 44.7 %collective-permute-start.18 = (bf16[512,1024]{1,0:T(8,128)(2,1)}, bf16[512,1024]{1,0:T(8,128)(2,1)}, u32[]{:S(2)}, u32[]{:S(2)}) collective-permute-start(bf16[512,1024]{1,0:T(8,128)(2,1)} %copy-done.12), channel_id=1, source_target_pairs={{0,16},{1,17},{2,18},{3,19},{4,20},{5,21},{6,22},{7,23},{8,24},{9,... | collective-permute-start | bytes 3145736 | tf_op jit(solution)/shard_map/ppermute | solution.py:193
  166.4 4.9 %collective-permute-start.22 = (bf16[4096,256]{1,0:T(8,128)(2,1)}, bf16[4096,256]{1,0:T(8,128)(2,1)}, u32[]{:S(2)}, u32[]{:S(2)}) collective-permute-start(bf16[4096,256]{1,0:T(8,128)(2,1)} %collective-permute-done.19.refs_13_.refs_10_), channel_id=1, source_target_pairs={{0,1},{1,0},{2,3},{3,2},{4,5},{5,4},{6,7},{7,6},{8,9},{9,8},{10,11... | collective-permute-start | bytes 6291464 | tf_op jit(solution)/shard_map/ppermute | solution.py:193
  166.4 52.5 %collective-permute-start.23 = (bf16[4096,256]{1,0:T(8,128)(2,1)}, bf16[4096,256]{1,0:T(8,128)(2,1)}, u32[]{:S(2)}, u32[]{:S(2)}) collective-permute-start(bf16[4096,256]{1,0:T(8,128)(2,1)} %get-tuple-element.77), channel_id=1, source_target_pairs={{0,8},{1,9},{2,10},{3,11},{4,12},{5,13},{6,14},{7,15},{8,0},{9,1},... | collective-permute-start | bytes 6291464 | tf_op jit(solution)/shard_map/ppermute | solution.py:193
  167.7 27.6 %collective-permute-start.20 = (bf16[512,1024]{1,0:T(8,128)(2,1)}, bf16[512,1024]{1,0:T(8,128)(2,1)}, u32[]{:S(2)}, u32[]{:S(2)}) collective-permute-start(bf16[512,1024]{1,0:T(8,128)(2,1)} %slice.187), channel_id=1, source_target_pairs={{0,6},{1,7},{2,0},{3,1},{4,2},{5,3},{6,4},{7,5},{8,14},{9,15},{10,... | collective-permute-start | bytes 3145736 | tf_op jit(solution)/shard_map/ppermute | solution.py:193
  170.7 25.3 %collective-permute-start.21 = (bf16[512,1024]{1,0:T(8,128)(2,1)}, bf16[512,1024]{1,0:T(8,128)(2,1)}, u32[]{:S(2)}, u32[]{:S(2)}) collective-permute-start(bf16[512,1024]{1,0:T(8,128)(2,1)} %collective-permute-done.16.refs_6_.refs_13_), channel_id=1, source_target_pairs={{0,16},{1,17},{2,18},{3,19},{4,20},{5,21},{6,22},{7,23},{8,24},{9,... | collective-permute-start | bytes 3145736 | tf_op jit(solution)/shard_map/ppermute | solution.py:193
  218.9 10.8 %collective-permute-start.24 = (bf16[4096,256]{1,0:T(8,128)(2,1)}, bf16[4096,256]{1,0:T(8,128)(2,1)}, u32[]{:S(2)}, u32[]{:S(2)}) collective-permute-start(bf16[4096,256]{1,0:T(8,128)(2,1)} %collective-permute-done.23.refs_16_), channel_id=1, source_target_pairs={{0,1},{1,0},{2,3},{3,2},{4,5},{5,4},{6,7},{7,6},{8,9},{9,8},{10,11... | collective-permute-start | bytes 6291464 | tf_op jit(solution)/shard_map/ppermute | solution.py:193
  247.8 11.4 %all-to-all-start = ((f32[8,1,4096]{2,1,0:T(1,128)}), f32[8,1,4096]{2,1,0:T(1,128)S(1)}, u32[]{:S(2)}, u32[]{:S(2)}) async-start(f32[8,1,4096]{2,1,0:T(1,128)} %all_to_all.6), calls=%async_computation | async-start | bytes 262144 | tf_op jit(solution)/shard_map/all_to_all | solution.py:393
  (21 other events, 423.9 us)
